TPU v7x, 512 devices: a whole 4x8x8 slice. The times are simulated.
512 devices in a mesh: row: 32 (over x, z), col: 16 (over y, core).
Axes of the slice: x: 4, y: 8, z: 8, core: 2. Of those that a mesh axis runs over, the one named last changes fastest.
Arguments:
- charges: bfloat16 [64, 64, 64, 512], P('row', 'col'), may hold values from -6 to 6
- offsets: bfloat16 [64, 64, 3, 512], P('row', 'col'), may hold values from 0 to 1
- leaf_basis: bfloat16 [64, 64, 64, 512], P('row', 'col'), may hold values from -0.25 to 0.25
- near_mask: int32 [64, 64, 8], P('row', 'col'), may hold values 0 or 1
- leaf_coupling: bfloat16 [64, 64, 64, 1600], P('row', 'col'), may hold values from -0.15625 to 0.15625
- leaf_distant_flags: int32 [64, 64, 25], P('row', 'col'), may hold values 0 or 1
- leaf_transfer: bfloat16 [64, 64, 64, 64], P('row', 'col'), may hold values from -0.25 to 0.25
- box_coupling: bfloat16 [32, 16, 3, 64, 1600], P('row', 'col'), may hold values from -0.15625 to 0.15625
- box_far: int32 [32, 16, 3, 25], P('row', 'col'), may hold values 0 or 1
- parent_child_transfer: bfloat16 [32, 16, 2, 64, 64], P('row', 'col'), may hold values from -0.375 to 0.375
Outputs:
- potential: bfloat16 [64, 64, 64, 512], P('row', 'col')
All inputs are finite; a program needn't handle non-finite values. No bound on the sum of `near_mask` or of `leaf_distant_flags` or of `box_far` on one device may be relied on, other than what follows from the above.
Results may differ from a plain program's by a relative error of at most 0.0049.
Values may be sent and summed in bfloat16 or wider, within the bound.
No kernel may reach another device: no remote copies, remote signals or barrier semaphores. Data moves between devices by JAX's collectives and lax.ppermute only.
A program may use at most 128 MiB of HBM per device.

v0:
```python
import math

import jax
import jax.numpy as jnp
from jax import lax
from jax.sharding import PartitionSpec as P

PANELS = 512
RANK = 64
LOADS = 64


EPSILON = 0.001


def from_behind(value, axis, steps):
    count = lax.axis_size(axis)
    initial, last = (max(0, -steps), min(count, count - steps))
    return lax.ppermute(value, axis, [(source, source + steps) for source in range(initial, last)])


def padded(array, sides, width):
    for axis, dim in sides:
        peers, length = (lax.axis_size(axis), array.shape[dim])
        up = [(i, (i + 1) % peers) for i in range(peers - 1)]
        down = [(j, i) for i, j in up]
        last = lax.slice_in_dim(array, length - width, length, axis=dim)
        initial = lax.slice_in_dim(array, 0, width, axis=dim)
        before = lax.ppermute(last, axis, up)
        after = lax.ppermute(initial, axis, down)
        array = jnp.concatenate([before, array, after], axis=dim)
    return array


def swapped(array, axis, bit):
    return lax.ppermute(array, axis, [(i, i ^ 1 << bit) for i in range(lax.axis_size(axis))])


def near_tile(source_off, target_off, row_off, col_off, factor):
    source = source_off.astype(jnp.float32)
    target = target_off.astype(jnp.float32)
    delta_x = (col_off + source[0])[:, None] - target[0][None, :]
    delta_y = (row_off + source[1])[:, None] - target[1][None, :]
    delta_z = source[2][:, None] - target[2][None, :]
    squared = delta_x * delta_x + delta_y * delta_y + delta_z * delta_z + EPSILON
    return (lax.rsqrt(squared) * factor).astype(jnp.bfloat16)


def near_weights(near_mask):
    flags = near_mask.astype(jnp.float32)
    center = jnp.ones(flags.shape[:-1] + (1,), jnp.float32)
    return jnp.concatenate([flags[..., :4], center, flags[..., 4:]], axis=-1)


def adjacent_box_list(flattened, stride):
    by_rows = []
    for row_off in (-2, -1, 0, 1, 2):
        moved = stride * row_off
        if moved == 0:
            by_rows.append(flattened)
        else:
            by_rows.append(from_behind(flattened, "row", -moved))
    stacked_blocks = jnp.stack(by_rows, axis=2)
    by_cols = []
    for col_off in (-2, -1, 0, 1, 2):
        moved = stride * col_off
        if moved == 0:
            by_cols.append(stacked_blocks)
        else:
            by_cols.append(from_behind(stacked_blocks, "col", -moved))
    return jnp.stack(by_cols, axis=3)[0, 0].reshape(25, RANK * LOADS)


def apply_level(coupling, flags, neighbours):
    masked = neighbours * flags[:, None].astype(jnp.bfloat16)
    return jnp.dot(coupling, masked.reshape(25 * RANK, LOADS), preferred_element_type=jnp.float32)


def body(
    charges,
    offsets,
    leaf_basis,
    near_mask,
    leaf_coupling,
    leaf_distant_flags,
    leaf_transfer,
    box_coupling,
    box_far,
    parent_child_transfer,
):
    rows_here = charges.shape[0]
    cols_here = charges.shape[1]
    leaf_count = rows_here * cols_here
    factor = 1.0 / math.sqrt(PANELS)
    outer_charges, outer_offsets = (
        padded(charges, (("row", 0), ("col", 1)), 1),
        padded(offsets, (("row", 0), ("col", 1)), 1),
    )
    source_charges = []
    source_offsets = []
    for slot in range(9):
        row_off = slot // 3 - 1
        col_off = slot % 3 - 1
        source_charges.append(
            outer_charges[
                1 + row_off : 1 + row_off + rows_here, 1 + col_off : 1 + col_off + cols_here
            ]
        )
        source_offsets.append(
            outer_offsets[
                1 + row_off : 1 + row_off + rows_here, 1 + col_off : 1 + col_off + cols_here
            ]
        )
    source_charges = jnp.stack(source_charges, axis=2).reshape(leaf_count, 9, LOADS, PANELS)
    source_offsets = jnp.stack(source_offsets, axis=2).reshape(leaf_count, 9, 3, PANELS)
    target_offsets = offsets.reshape(leaf_count, 3, PANELS)
    weights = near_weights(near_mask).reshape(leaf_count, 9)

    def near_leaf(leaf_items):
        leaf_charges, leaf_offsets, target, leaf_weights = leaf_items
        tiles = jnp.stack(
            [
                near_tile(leaf_offsets[slot], target, slot // 3 - 1, slot % 3 - 1, factor)
                for slot in range(9)
            ],
            axis=0,
        )
        weighted = leaf_charges * leaf_weights[:, None, None].astype(jnp.bfloat16)
        return jnp.einsum("slp,spq->lq", weighted, tiles, preferred_element_type=jnp.float32)

    near_field = lax.map(near_leaf, (source_charges, source_offsets, target_offsets, weights))
    near_field = near_field.reshape(rows_here, cols_here, LOADS, PANELS)
    multipoles = jnp.einsum(
        "abkp,abrp->abkr", leaf_basis, charges, preferred_element_type=jnp.float32
    ).astype(jnp.bfloat16)
    flat_poles = multipoles.reshape(rows_here, cols_here, RANK * LOADS)
    outer_poles = padded(flat_poles, (("row", 0), ("col", 1)), 2)
    windows = []
    for place in range(25):
        row_off = place // 5 - 2
        col_off = place % 5 - 2
        windows.append(
            outer_poles[
                2 + row_off : 2 + row_off + rows_here, 2 + col_off : 2 + col_off + cols_here
            ]
        )
    windows = jnp.stack(windows, axis=2) * leaf_distant_flags[:, :, :, None].astype(jnp.bfloat16)
    windows = windows.reshape(rows_here, cols_here, 25 * RANK, LOADS)
    leaf_local = jnp.einsum(
        "abkm,abmr->abkr", leaf_coupling, windows, preferred_element_type=jnp.float32
    )
    coarse_box_one = jnp.einsum(
        "abkj,abkr->jr", leaf_transfer, multipoles, preferred_element_type=jnp.float32
    ).astype(jnp.bfloat16)
    level_terms = jnp.einsum(
        "fyn,yb->fnb",
        parent_child_transfer[0, 0],
        coarse_box_one,
        preferred_element_type=jnp.float32,
    ).astype(jnp.bfloat16)
    second_term = level_terms[0].reshape(1, 1, RANK * LOADS)
    third_term = level_terms[1].reshape(1, 1, RANK * LOADS)
    first_near = adjacent_box_list(coarse_box_one.reshape(1, 1, RANK * LOADS), 1)
    box_local = apply_level(box_coupling[0, 0, 0], box_far[0, 0, 0], first_near)
    second_peer, third_peer = swapped((second_term, third_term), "row", 0)
    second_sum = second_term.astype(jnp.float32) + second_peer.astype(jnp.float32)
    third_sum = third_term.astype(jnp.float32) + third_peer.astype(jnp.float32)
    second_peer, third_peer = (
        swapped(second_sum.astype(jnp.bfloat16), "col", 0).astype(second_sum.dtype),
        swapped(third_sum.astype(jnp.bfloat16), "col", 0).astype(third_sum.dtype),
    )
    box2 = (second_sum + second_peer).astype(jnp.bfloat16)
    third_sum = third_sum + third_peer
    third_peer = swapped(third_sum, "row", 1)
    third_sum = third_sum + third_peer
    third_peer = swapped(third_sum, "col", 1)
    box3 = (third_sum + third_peer).astype(jnp.bfloat16)
    second_near = adjacent_box_list(box2, 2)
    third_near = adjacent_box_list(box3, 4)
    box_local = box_local + apply_level(box_coupling[0, 0, 1], box_far[0, 0, 1], second_near)
    box_local = box_local + apply_level(box_coupling[0, 0, 2], box_far[0, 0, 2], third_near)
    box_local = box_local.astype(jnp.bfloat16)
    local = leaf_local + jnp.einsum(
        "abkj,jr->abkr", leaf_transfer, box_local, preferred_element_type=jnp.float32
    )
    local = local.astype(jnp.bfloat16)
    far_part = jnp.einsum("abkr,abkp->abrp", local, leaf_basis, preferred_element_type=jnp.float32)
    return (near_field + far_part).astype(jnp.bfloat16)


def solution(mesh):
    return jax.shard_map(
        body,
        mesh=mesh,
        in_specs=(
            P("row", "col", None, None),
            P("row", "col", None, None),
            P("row", "col", None, None),
            P("row", "col", None),
            P("row", "col", None, None),
            P("row", "col", None),
            P("row", "col", None, None),
            P("row", "col", None, None, None),
            P("row", "col", None, None),
            P("row", "col", None, None, None),
        ),
        out_specs=P("row", "col", None, None),
        check_vma=False,
    )
```

profile of v0, /device:TPU:29, one launch (start us, length us, event | category | flops | bytes accessed | tf_op | source)
XLA Modules:
  0.0 273.2 jit_solution(10919819661634155686)
XLA Ops:
  3.0 5.8 %collective-permute-start.12 = (bf16[1,1,4096]{2,1,0:T(2,128)(2,1)S(1)}, bf16[1,1,4096]{2,1,0:T(2,128)(2,1)S(1)}, u32[]{:S(2)}, u32[]{:S(2)}) collective-permute-start(bf16[1,1,4096]{2,1,0:T(2,128)(2,1)S(1)} %reshape.2172), channel_id=1, source_target_pairs={{0,32},{16,48},{32,64},{48,80},{64,96},{80,112},{96,128},{112,144}... | collective-permute-start | bytes 24584 | tf_op jit(solution)/shard_map/ppermute | solution.py:19
  8.8 4.0 %collective-permute-start.13 = (bf16[1,1,4096]{2,1,0:T(2,128)(2,1)S(1)}, bf16[1,1,4096]{2,1,0:T(2,128)(2,1)S(1)}, u32[]{:S(2)}, u32[]{:S(2)}) collective-permute-start(bf16[1,1,4096]{2,1,0:T(2,128)(2,1)S(1)} %reshape.2172), channel_id=1, source_target_pairs={{0,16},{16,32},{32,48},{48,64},{64,80},{80,96},{96,112},{112,128},... | collective-permute-start | bytes 24584 | tf_op jit(solution)/shard_map/ppermute | solution.py:19
  12.8 4.7 %collective-permute-start.14 = (bf16[1,1,4096]{2,1,0:T(2,128)(2,1)S(1)}, bf16[1,1,4096]{2,1,0:T(2,128)(2,1)S(1)}, u32[]{:S(2)}, u32[]{:S(2)}) collective-permute-start(bf16[1,1,4096]{2,1,0:T(2,128)(2,1)S(1)} %reshape.2172), channel_id=1, source_target_pairs={{16,0},{32,16},{48,32},{64,48},{80,64},{96,80},{112,96},{128,112},... | collective-permute-start | bytes 24584 | tf_op jit(solution)/shard_map/ppermute | solution.py:19
  17.5 4.3 %collective-permute-start.15 = (bf16[1,1,4096]{2,1,0:T(2,128)(2,1)S(1)}, bf16[1,1,4096]{2,1,0:T(2,128)(2,1)S(1)}, u32[]{:S(2)}, u32[]{:S(2)}) collective-permute-start(bf16[1,1,4096]{2,1,0:T(2,128)(2,1)S(1)} %reshape.2172), channel_id=1, source_target_pairs={{32,0},{48,16},{64,32},{80,48},{96,64},{112,80},{128,96},{144,112}... | collective-permute-start | bytes 24584 | tf_op jit(solution)/shard_map/ppermute | solution.py:19
  22.8 2.2 collective-permute-start.20
  30.6 3.1 %collective-permute-start.30 = (bf16[1,1,4096]{2,1,0:T(2,128)(2,1)S(1)}, bf16[1,1,4096]{2,1,0:T(2,128)(2,1)S(1)}, u32[]{:S(2)}, u32[]{:S(2)}) collective-permute-start(bf16[1,1,4096]{2,1,0:T(2,128)(2,1)S(1)} %reshape_squeeze.10), channel_id=1, source_target_pairs={{0,16},{16,0},{32,48},{48,32},{64,80},{80,64},{96,112},{112,96},{1... | collective-permute-start | bytes 24584 | tf_op jit(solution)/shard_map/ppermute | solution.py:36
  35.0 3.1 %collective-permute-start.4 = (bf16[1,4,3,512]{3,1,2,0:T(4,128)(2,1)S(1)}, bf16[1,4,3,512]{3,1,2,0:T(4,128)(2,1)S(1)}, u32[]{:S(2)}, u32[]{:S(2)}) collective-permute-start(bf16[1,4,3,512]{3,1,2,0:T(4,128)(2,1)S(1)} %get-tuple-element.139), channel_id=1, source_target_pairs={{0,16},{16,32},{32,48},{48,64},{64,80},{80,96},{96,112},{112,128},... | collective-permute-start | bytes 36872 | tf_op jit(solution)/shard_map/ppermute | solution.py:29
  38.2 4.3 %collective-permute-start.5 = (bf16[1,4,3,512]{3,1,2,0:T(4,128)(2,1)S(1)}, bf16[1,4,3,512]{3,1,2,0:T(4,128)(2,1)S(1)}, u32[]{:S(2)}, u32[]{:S(2)}) collective-permute-start(bf16[1,4,3,512]{3,1,2,0:T(4,128)(2,1)S(1)} %get-tuple-element.138), channel_id=1, source_target_pairs={{16,0},{32,16},{48,32},{64,48},{80,64},{96,80},{112,96},{128,112},... | collective-permute-start | bytes 36872 | tf_op jit(solution)/shard_map/ppermute | solution.py:30
  42.5 5.4 %collective-permute-start.21 = (bf16[1,1,4096]{2,1,0:T(2,128)(2,1)S(1)}, bf16[1,1,4096]{2,1,0:T(2,128)(2,1)S(1)}, u32[]{:S(2)}, u32[]{:S(2)}) collective-permute-start(bf16[1,1,4096]{2,1,0:T(2,128)(2,1)S(1)} %fusion.63), channel_id=1, source_target_pairs={{0,1},{1,0},{2,3},{3,2},{4,5},{5,4},{6,7},{7,6},{8,9},{9,8},{10,11... | collective-permute-start | bytes 24584 | tf_op jit(solution)/shard_map/ppermute | solution.py:36
  50.1 4.9 %collective-permute-start.22 = (bf16[1,1,4096]{2,1,0:T(2,128)(2,1)S(1)}, bf16[1,1,4096]{2,1,0:T(2,128)(2,1)S(1)}, u32[]{:S(2)}, u32[]{:S(2)}) collective-permute-start(bf16[1,1,4096]{2,1,0:T(2,128)(2,1)S(1)} %add_convert_fusion.1), channel_id=1, source_target_pairs={{0,64},{16,80},{32,96},{48,112},{64,128},{80,144},{96,160},{112,17... | collective-permute-start | bytes 24584 | tf_op jit(solution)/shard_map/ppermute | solution.py:19
  55.1 2.7 collective-permute-start.7
  57.8 4.3 %collective-permute-start.6 = (bf16[4,1,3,512]{3,1,2,0:T(2,128)(2,1)S(1)}, bf16[4,1,3,512]{3,1,2,0:T(2,128)(2,1)S(1)}, u32[]{:S(2)}, u32[]{:S(2)}) collective-permute-start(bf16[4,1,3,512]{3,1,2,0:T(2,128)(2,1)S(1)} %get-tuple-element.132), channel_id=1, source_target_pairs={{0,1},{1,2},{2,3},{3,4},{4,5},{5,6},{6,7},{7,8},{8,9},{9,10},{10,1... | collective-permute-start | bytes 36872 | tf_op jit(solution)/shard_map/ppermute | solution.py:29
  64.0 6.4 %collective-permute-start.24 = (bf16[1,1,4096]{2,1,0:T(2,128)(2,1)S(1)}, bf16[1,1,4096]{2,1,0:T(2,128)(2,1)S(1)}, u32[]{:S(2)}, u32[]{:S(2)}) collective-permute-start(bf16[1,1,4096]{2,1,0:T(2,128)(2,1)S(1)} %add_convert_fusion.1), channel_id=1, source_target_pairs={{32,0},{48,16},{64,32},{80,48},{96,64},{112,80},{128,96},{144,112}... | collective-permute-start | bytes 24584 | tf_op jit(solution)/shard_map/ppermute | solution.py:19
  70.4 4.3 %collective-permute-start.25 = (bf16[1,1,4096]{2,1,0:T(2,128)(2,1)S(1)}, bf16[1,1,4096]{2,1,0:T(2,128)(2,1)S(1)}, u32[]{:S(2)}, u32[]{:S(2)}) collective-permute-start(bf16[1,1,4096]{2,1,0:T(2,128)(2,1)S(1)} %add_convert_fusion.1), channel_id=1, source_target_pairs={{64,0},{80,16},{96,32},{112,48},{128,64},{144,80},{160,96},{176,11... | collective-permute-start | bytes 24584 | tf_op jit(solution)/shard_map/ppermute | solution.py:19
  76.8 3.0 %collective-permute-start.16 = (bf16[1,1,5,4096]{3,2,1,0:T(8,128)(2,1)S(1)}, bf16[1,1,5,4096]{3,2,1,0:T(8,128)(2,1)S(1)}, u32[]{:S(2)}, u32[]{:S(2)}) collective-permute-start(bf16[1,1,5,4096]{3,2,1,0:T(8,128)(2,1)S(1)} %stack.304), channel_id=1, source_target_pairs={{0,2},{1,3},{2,4},{3,5},{4,6},{5,7},{6,8},{7,9},{8,10},{9,11},{10,... | collective-permute-start | bytes 122888 | tf_op jit(solution)/shard_map/ppermute | solution.py:19
  79.8 3.2 %collective-permute-start.17 = (bf16[1,1,5,4096]{3,2,1,0:T(8,128)(2,1)S(1)}, bf16[1,1,5,4096]{3,2,1,0:T(8,128)(2,1)S(1)}, u32[]{:S(2)}, u32[]{:S(2)}) collective-permute-start(bf16[1,1,5,4096]{3,2,1,0:T(8,128)(2,1)S(1)} %stack.304), channel_id=1, source_target_pairs={{0,1},{1,2},{2,3},{3,4},{4,5},{5,6},{6,7},{7,8},{8,9},{9,10},{10,1... | collective-permute-start | bytes 122888 | tf_op jit(solution)/shard_map/ppermute | solution.py:19
  87.5 3.0 %collective-permute-done.32 = f32[1,1,4096]{2,1,0:T(1,128)S(1)} collective-permute-done((f32[1,1,4096]{2,1,0:T(1,128)S(1)}, f32[1,1,4096]{2,1,0:T(1,128)S(1)}, u32[]{:S(2)}, u32[]{:S(2)}) %collective-permute-start.32) | collective-permute-done | bytes 16416 | tf_op jit(solution)/shard_map/ppermute | solution.py:36
  90.4 2.7 %collective-permute-start.33 = (f32[1,1,4096]{2,1,0:T(1,128)S(1)}, f32[1,1,4096]{2,1,0:T(1,128)S(1)}, u32[]{:S(2)}, u32[]{:S(2)}) collective-permute-start(f32[1,1,4096]{2,1,0:T(1,128)S(1)} %add.442), channel_id=1, source_target_pairs={{0,2},{1,3},{2,0},{3,1},{4,6},{5,7},{6,4},{7,5},{8,10},{9,11},{10,... | collective-permute-start | bytes 49160 | tf_op jit(solution)/shard_map/ppermute | solution.py:36
  94.9 2.7 %collective-permute-start.19 = (bf16[1,1,5,4096]{3,2,1,0:T(8,128)(2,1)S(1)}, bf16[1,1,5,4096]{3,2,1,0:T(8,128)(2,1)S(1)}, u32[]{:S(2)}, u32[]{:S(2)}) collective-permute-start(bf16[1,1,5,4096]{3,2,1,0:T(8,128)(2,1)S(1)} %stack.304), channel_id=1, source_target_pairs={{2,0},{3,1},{4,2},{5,3},{6,4},{7,5},{8,6},{9,7},{10,8},{11,9},{12,... | collective-permute-start | bytes 122888 | tf_op jit(solution)/shard_map/ppermute | solution.py:19
  97.7 3.1 %collective-permute-start.34 = (bf16[1,1,4096]{2,1,0:T(2,128)(2,1)S(1)}, bf16[1,1,4096]{2,1,0:T(2,128)(2,1)S(1)}, u32[]{:S(2)}, u32[]{:S(2)}) collective-permute-start(bf16[1,1,4096]{2,1,0:T(2,128)(2,1)S(1)} %add_convert_fusion), channel_id=1, source_target_pairs={{0,128},{16,144},{32,160},{48,176},{64,192},{80,208},{96,224},{112... | collective-permute-start | bytes 24584 | tf_op jit(solution)/shard_map/ppermute | solution.py:19
  100.9 4.6 %collective-permute-start.35 = (bf16[1,1,4096]{2,1,0:T(2,128)(2,1)S(1)}, bf16[1,1,4096]{2,1,0:T(2,128)(2,1)S(1)}, u32[]{:S(2)}, u32[]{:S(2)}) collective-permute-start(bf16[1,1,4096]{2,1,0:T(2,128)(2,1)S(1)} %add_convert_fusion), channel_id=1, source_target_pairs={{0,64},{16,80},{32,96},{48,112},{64,128},{80,144},{96,160},{112,17... | collective-permute-start | bytes 24584 | tf_op jit(solution)/shard_map/ppermute | solution.py:19
  105.5 5.5 %collective-permute-start.36 = (bf16[1,1,4096]{2,1,0:T(2,128)(2,1)S(1)}, bf16[1,1,4096]{2,1,0:T(2,128)(2,1)S(1)}, u32[]{:S(2)}, u32[]{:S(2)}) collective-permute-start(bf16[1,1,4096]{2,1,0:T(2,128)(2,1)S(1)} %add_convert_fusion), channel_id=1, source_target_pairs={{64,0},{80,16},{96,32},{112,48},{128,64},{144,80},{160,96},{176,11... | collective-permute-start | bytes 24584 | tf_op jit(solution)/shard_map/ppermute | solution.py:19
  111.0 2.2 collective-permute-start.37
  115.1 4.8 %collective-permute-start.9 = (bf16[2,4,4096]{2,1,0:T(4,128)(2,1)S(1)}, bf16[2,4,4096]{2,1,0:T(4,128)(2,1)S(1)}, u32[]{:S(2)}, u32[]{:S(2)}) collective-permute-start(bf16[2,4,4096]{2,1,0:T(4,128)(2,1)S(1)} %reshape.2171), channel_id=1, source_target_pairs={{16,0},{32,16},{48,32},{64,48},{80,64},{96,80},{112,96},{128,112},... | collective-permute-start | bytes 196616 | tf_op jit(solution)/shard_map/ppermute | solution.py:30
  122.0 3.4 %collective-permute-start = (bf16[1,4,64,512]{3,2,1,0:T(8,128)(2,1)}, bf16[1,4,64,512]{3,2,1,0:T(8,128)(2,1)}, u32[]{:S(2)}, u32[]{:S(2)}) collective-permute-start(bf16[1,4,64,512]{3,2,1,0:T(8,128)(2,1)} %get-tuple-element.119), channel_id=1, source_target_pairs={{0,16},{16,32},{32,48},{48,64},{64,80},{80,96},{96,112},{112,128},... | collective-permute-start | bytes 786440 | tf_op jit(solution)/shard_map/ppermute | solution.py:29
  125.3 2.5 collective-permute-start.26
  128.0 3.0 %collective-permute-start.27 = (bf16[1,1,5,4096]{3,2,1,0:T(8,128)(2,1)S(1)}, bf16[1,1,5,4096]{3,2,1,0:T(8,128)(2,1)S(1)}, u32[]{:S(2)}, u32[]{:S(2)}) collective-permute-start(bf16[1,1,5,4096]{3,2,1,0:T(8,128)(2,1)S(1)} %stack.316), channel_id=1, source_target_pairs={{0,2},{1,3},{2,4},{3,5},{4,6},{5,7},{6,8},{7,9},{8,10},{9,11},{10,... | collective-permute-start | bytes 122888 | tf_op jit(solution)/shard_map/ppermute | solution.py:19
  131.1 3.1 %collective-permute-start.28 = (bf16[1,1,5,4096]{3,2,1,0:T(8,128)(2,1)S(1)}, bf16[1,1,5,4096]{3,2,1,0:T(8,128)(2,1)S(1)}, u32[]{:S(2)}, u32[]{:S(2)}) collective-permute-start(bf16[1,1,5,4096]{3,2,1,0:T(8,128)(2,1)S(1)} %stack.316), channel_id=1, source_target_pairs={{2,0},{3,1},{4,2},{5,3},{6,4},{7,5},{8,6},{9,7},{10,8},{11,9},{12,... | collective-permute-start | bytes 122888 | tf_op jit(solution)/shard_map/ppermute | solution.py:19
  135.1 3.1 %collective-permute-start.29 = (bf16[1,1,5,4096]{3,2,1,0:T(8,128)(2,1)S(1)}, bf16[1,1,5,4096]{3,2,1,0:T(8,128)(2,1)S(1)}, u32[]{:S(2)}, u32[]{:S(2)}) collective-permute-start(bf16[1,1,5,4096]{3,2,1,0:T(8,128)(2,1)S(1)} %stack.316), channel_id=1, source_target_pairs={{4,0},{5,1},{6,2},{7,3},{8,4},{9,5},{10,6},{11,7},{12,8},{13,9},{1... | collective-permute-start | bytes 122888 | tf_op jit(solution)/shard_map/ppermute | solution.py:19
  138.2 2.8 %collective-permute-start.38 = (bf16[1,1,5,4096]{3,2,1,0:T(8,128)(2,1)S(1)}, bf16[1,1,5,4096]{3,2,1,0:T(8,128)(2,1)S(1)}, u32[]{:S(2)}, u32[]{:S(2)}) collective-permute-start(bf16[1,1,5,4096]{3,2,1,0:T(8,128)(2,1)S(1)} %stack.328), channel_id=1, source_target_pairs={{0,8},{1,9},{2,10},{3,11},{4,12},{5,13},{6,14},{7,15},{16,24},{17,... | collective-permute-start | bytes 122888 | tf_op jit(solution)/shard_map/ppermute | solution.py:19
  141.1 2.8 %collective-permute-start.39 = (bf16[1,1,5,4096]{3,2,1,0:T(8,128)(2,1)S(1)}, bf16[1,1,5,4096]{3,2,1,0:T(8,128)(2,1)}, u32[]{:S(2)}, u32[]{:S(2)}) collective-permute-start(bf16[1,1,5,4096]{3,2,1,0:T(8,128)(2,1)S(1)} %stack.328), channel_id=1, source_target_pairs={{0,4},{1,5},{2,6},{3,7},{4,8},{5,9},{6,10},{7,11},{8,12},{9,13},{1... | collective-permute-start | bytes 122888 | tf_op jit(solution)/shard_map/ppermute | solution.py:19
  143.9 4.6 %collective-permute-start.40 = (bf16[1,1,5,4096]{3,2,1,0:T(8,128)(2,1)S(1)}, bf16[1,1,5,4096]{3,2,1,0:T(8,128)(2,1)}, u32[]{:S(2)}, u32[]{:S(2)}) collective-permute-start(bf16[1,1,5,4096]{3,2,1,0:T(8,128)(2,1)S(1)} %stack.328), channel_id=1, source_target_pairs={{4,0},{5,1},{6,2},{7,3},{8,4},{9,5},{10,6},{11,7},{12,8},{13,9},{1... | collective-permute-start | bytes 122888 | tf_op jit(solution)/shard_map/ppermute | solution.py:19
  152.3 13.7 %collective-permute-start.10 = (bf16[6,2,4096]{2,1,0:T(2,128)(2,1)}, bf16[6,2,4096]{2,1,0:T(2,128)(2,1)S(1)}, u32[]{:S(2)}, u32[]{:S(2)}) collective-permute-start(bf16[6,2,4096]{2,1,0:T(2,128)(2,1)} %get-tuple-element.121), channel_id=1, source_target_pairs={{0,1},{1,2},{2,3},{3,4},{4,5},{5,6},{6,7},{7,8},{8,9},{9,10},{10,1... | collective-permute-start | bytes 294920 | tf_op jit(solution)/shard_map/ppermute | solution.py:29
  176.4 2.3 copy.84
  178.7 5.8 %stack.299 = bf16[2,4,1600,64]{3,2,1,0:T(8,128)(2,1)} reshape(bf16[2,4,25,4096]{3,2,1,0:T(8,128)(2,1)} %copy.84) | data formatting | bytes 3276800 | tf_op jit(solution)/shard_map/stack | solution.py:147
  189.7 5.0 %collective-permute-start.2 = (bf16[4,1,64,512]{3,2,1,0:T(8,128)(2,1)S(1)}, bf16[4,1,64,512]{3,2,1,0:T(8,128)(2,1)S(1)}, u32[]{:S(2)}, u32[]{:S(2)}) collective-permute-start(bf16[4,1,64,512]{3,2,1,0:T(8,128)(2,1)S(1)} %get-tuple-element.114), channel_id=1, source_target_pairs={{0,1},{1,2},{2,3},{3,4},{4,5},{5,6},{6,7},{7,8},{8,9},{9,10},{10,1... | collective-permute-start | bytes 786440 | tf_op jit(solution)/shard_map/ppermute | solution.py:29
  194.8 4.1 %fusion.20 = f32[2,4,64,64]{2,3,1,0:T(8,128)} fusion(bf16[2,4,64,1600]{3,2,1,0:T(8,128)(2,1)S(1)} %copy-done, bf16[2,4,1600,64]{3,2,1,0:T(8,128)(2,1)S(1)} %copy-done.2, bf16[2,4,1600]{2,1,0:T(4,128)(2,1)S(1)} %copy-done.12), kind=kOutput, calls=%fused_computation.82 | convolution fusion | flops 105676800 | bytes 3433472 | tf_op jit(solution)/shard_map/abkm,abmr->abkr/dot_general | solution.py:149
  199.7 2.2 copy-done.3
  201.9 69.1 %while.10 = (s32[]{:T(128)}, f32[8,64,512]{2,1,0:T(8,128)S(1)}, bf16[8,9,64,512]{3,2,1,0:T(8,128)(2,1)}, bf16[8,9]{1,0:T(8,128)(2,1)}, bf16[8,9,3,512]{3,2,1,0:T...) while((s32[]{:T(128)}, f32[8,64,512]{2,1,0:T(8,128)S(1)}, ...), condition=%wide.region_1.2_spmd, body=%wide.region_0.1_spmd.sunk | while | flops 328258560 | bytes 10485581 | solution.py:131
  208.5 2.0 fusion.117
  217.1 2.0 fusion.117
  225.8 2.0 fusion.117
  234.4 2.0 fusion.117
  243.0 2.0 fusion.117
  251.6 2.0 fusion.117
  260.3 2.0 fusion.117
  268.9 2.0 fusion.117
  271.0 2.2 fusion.18
  (362 shorter events, 99.8 us)
Async XLA Ops:
  0.0 194.8 %copy-start = (bf16[2,4,64,1600]{3,2,1,0:T(8,128)(2,1)S(1)}, bf16[2,4,64,1600]{3,2,1,0:T(8,128)(2,1)}, u32[]{:S(2)}) copy-start(bf16[2,4,64,1600]{3,2,1,0:T(8,128)(2,1)} %param.16) | copy-start | bytes 4915204
  3.0 35.2 %collective-permute-start.12 = (bf16[1,1,4096]{2,1,0:T(2,128)(2,1)S(1)}, bf16[1,1,4096]{2,1,0:T(2,128)(2,1)S(1)}, u32[]{:S(2)}, u32[]{:S(2)}) collective-permute-start(bf16[1,1,4096]{2,1,0:T(2,128)(2,1)S(1)} %reshape.2172), channel_id=1, source_target_pairs={{0,32},{16,48},{32,64},{48,80},{64,96},{80,112},{96,128},{112,144}... | collective-permute-start | bytes 24584 | tf_op jit(solution)/shard_map/ppermute | solution.py:19
  8.8 33.7 %collective-permute-start.13 = (bf16[1,1,4096]{2,1,0:T(2,128)(2,1)S(1)}, bf16[1,1,4096]{2,1,0:T(2,128)(2,1)S(1)}, u32[]{:S(2)}, u32[]{:S(2)}) collective-permute-start(bf16[1,1,4096]{2,1,0:T(2,128)(2,1)S(1)} %reshape.2172), channel_id=1, source_target_pairs={{0,16},{16,32},{32,48},{48,64},{64,80},{80,96},{96,112},{112,128},... | collective-permute-start | bytes 24584 | tf_op jit(solution)/shard_map/ppermute | solution.py:19
  12.8 35.1 %collective-permute-start.14 = (bf16[1,1,4096]{2,1,0:T(2,128)(2,1)S(1)}, bf16[1,1,4096]{2,1,0:T(2,128)(2,1)S(1)}, u32[]{:S(2)}, u32[]{:S(2)}) collective-permute-start(bf16[1,1,4096]{2,1,0:T(2,128)(2,1)S(1)} %reshape.2172), channel_id=1, source_target_pairs={{16,0},{32,16},{48,32},{64,48},{80,64},{96,80},{112,96},{128,112},... | collective-permute-start | bytes 24584 | tf_op jit(solution)/shard_map/ppermute | solution.py:19
  17.5 32.4 %collective-permute-start.15 = (bf16[1,1,4096]{2,1,0:T(2,128)(2,1)S(1)}, bf16[1,1,4096]{2,1,0:T(2,128)(2,1)S(1)}, u32[]{:S(2)}, u32[]{:S(2)}) collective-permute-start(bf16[1,1,4096]{2,1,0:T(2,128)(2,1)S(1)} %reshape.2172), channel_id=1, source_target_pairs={{32,0},{48,16},{64,32},{80,48},{96,64},{112,80},{128,96},{144,112}... | collective-permute-start | bytes 24584 | tf_op jit(solution)/shard_map/ppermute | solution.py:19
  22.8 7.7 %collective-permute-start.20 = (bf16[1,1,4096]{2,1,0:T(2,128)(2,1)S(1)}, bf16[1,1,4096]{2,1,0:T(2,128)(2,1)S(1)}, u32[]{:S(2)}, u32[]{:S(2)}) collective-permute-start(bf16[1,1,4096]{2,1,0:T(2,128)(2,1)S(1)} %reshape_squeeze.4), channel_id=1, source_target_pairs={{0,16},{16,0},{32,48},{48,32},{64,80},{80,64},{96,112},{112,96},{1... | collective-permute-start | bytes 24584 | tf_op jit(solution)/shard_map/ppermute | solution.py:36
  26.8 78.7 %copy-start.8 = (bf16[2,4,3,512]{3,2,1,0:T(4,128)(2,1)}, bf16[2,4,3,512]{3,2,1,0:T(4,128)(2,1)S(1)}, u32[]{:S(2)}) copy-start(bf16[2,4,3,512]{3,2,1,0:T(4,128)(2,1)S(1)} %copy.78) | copy-start | bytes 73732
  30.6 4.5 %collective-permute-start.30 = (bf16[1,1,4096]{2,1,0:T(2,128)(2,1)S(1)}, bf16[1,1,4096]{2,1,0:T(2,128)(2,1)S(1)}, u32[]{:S(2)}, u32[]{:S(2)}) collective-permute-start(bf16[1,1,4096]{2,1,0:T(2,128)(2,1)S(1)} %reshape_squeeze.10), channel_id=1, source_target_pairs={{0,16},{16,0},{32,48},{48,32},{64,80},{80,64},{96,112},{112,96},{1... | collective-permute-start | bytes 24584 | tf_op jit(solution)/shard_map/ppermute | solution.py:36
  35.0 15.0 %collective-permute-start.4 = (bf16[1,4,3,512]{3,1,2,0:T(4,128)(2,1)S(1)}, bf16[1,4,3,512]{3,1,2,0:T(4,128)(2,1)S(1)}, u32[]{:S(2)}, u32[]{:S(2)}) collective-permute-start(bf16[1,4,3,512]{3,1,2,0:T(4,128)(2,1)S(1)} %get-tuple-element.139), channel_id=1, source_target_pairs={{0,16},{16,32},{32,48},{48,64},{64,80},{80,96},{96,112},{112,128},... | collective-permute-start | bytes 36872 | tf_op jit(solution)/shard_map/ppermute | solution.py:29
  38.2 11.9 %collective-permute-start.5 = (bf16[1,4,3,512]{3,1,2,0:T(4,128)(2,1)S(1)}, bf16[1,4,3,512]{3,1,2,0:T(4,128)(2,1)S(1)}, u32[]{:S(2)}, u32[]{:S(2)}) collective-permute-start(bf16[1,4,3,512]{3,1,2,0:T(4,128)(2,1)S(1)} %get-tuple-element.138), channel_id=1, source_target_pairs={{16,0},{32,16},{48,32},{64,48},{80,64},{96,80},{112,96},{128,112},... | collective-permute-start | bytes 36872 | tf_op jit(solution)/shard_map/ppermute | solution.py:30
  42.5 7.6 %collective-permute-start.21 = (bf16[1,1,4096]{2,1,0:T(2,128)(2,1)S(1)}, bf16[1,1,4096]{2,1,0:T(2,128)(2,1)S(1)}, u32[]{:S(2)}, u32[]{:S(2)}) collective-permute-start(bf16[1,1,4096]{2,1,0:T(2,128)(2,1)S(1)} %fusion.63), channel_id=1, source_target_pairs={{0,1},{1,0},{2,3},{3,2},{4,5},{5,4},{6,7},{7,6},{8,9},{9,8},{10,11... | collective-permute-start | bytes 24584 | tf_op jit(solution)/shard_map/ppermute | solution.py:36
  47.9 16.1 %collective-permute-start.31 = (bf16[1,1,4096]{2,1,0:T(2,128)(2,1)S(1)}, bf16[1,1,4096]{2,1,0:T(2,128)(2,1)S(1)}, u32[]{:S(2)}, u32[]{:S(2)}) collective-permute-start(bf16[1,1,4096]{2,1,0:T(2,128)(2,1)S(1)} %fusion.64), channel_id=1, source_target_pairs={{0,1},{1,0},{2,3},{3,2},{4,5},{5,4},{6,7},{7,6},{8,9},{9,8},{10,11... | collective-permute-start | bytes 24584 | tf_op jit(solution)/shard_map/ppermute | solution.py:36
  50.1 20.3 %collective-permute-start.22 = (bf16[1,1,4096]{2,1,0:T(2,128)(2,1)S(1)}, bf16[1,1,4096]{2,1,0:T(2,128)(2,1)S(1)}, u32[]{:S(2)}, u32[]{:S(2)}) collective-permute-start(bf16[1,1,4096]{2,1,0:T(2,128)(2,1)S(1)} %add_convert_fusion.1), channel_id=1, source_target_pairs={{0,64},{16,80},{32,96},{48,112},{64,128},{80,144},{96,160},{112,17... | collective-permute-start | bytes 24584 | tf_op jit(solution)/shard_map/ppermute | solution.py:19
  55.1 28.0 %collective-permute-start.7 = (bf16[4,1,3,512]{3,1,2,0:T(2,128)(2,1)S(1)}, bf16[4,1,3,512]{3,1,2,0:T(2,128)(2,1)S(1)}, u32[]{:S(2)}, u32[]{:S(2)}) collective-permute-start(bf16[4,1,3,512]{3,1,2,0:T(2,128)(2,1)S(1)} %get-tuple-element.131), channel_id=1, source_target_pairs={{1,0},{2,1},{3,2},{4,3},{5,4},{6,5},{7,6},{8,7},{9,8},{10,9},{11,1... | collective-permute-start | bytes 36872 | tf_op jit(solution)/shard_map/ppermute | solution.py:30
  57.8 27.3 %collective-permute-start.6 = (bf16[4,1,3,512]{3,1,2,0:T(2,128)(2,1)S(1)}, bf16[4,1,3,512]{3,1,2,0:T(2,128)(2,1)S(1)}, u32[]{:S(2)}, u32[]{:S(2)}) collective-permute-start(bf16[4,1,3,512]{3,1,2,0:T(2,128)(2,1)S(1)} %get-tuple-element.132), channel_id=1, source_target_pairs={{0,1},{1,2},{2,3},{3,4},{4,5},{5,6},{6,7},{7,8},{8,9},{9,10},{10,1... | collective-permute-start | bytes 36872 | tf_op jit(solution)/shard_map/ppermute | solution.py:29
  62.1 12.7 %collective-permute-start.23 = (bf16[1,1,4096]{2,1,0:T(2,128)(2,1)S(1)}, bf16[1,1,4096]{2,1,0:T(2,128)(2,1)S(1)}, u32[]{:S(2)}, u32[]{:S(2)}) collective-permute-start(bf16[1,1,4096]{2,1,0:T(2,128)(2,1)S(1)} %add_convert_fusion.1), channel_id=1, source_target_pairs={{0,32},{16,48},{32,64},{48,80},{64,96},{80,112},{96,128},{112,144}... | collective-permute-start | bytes 24584 | tf_op jit(solution)/shard_map/ppermute | solution.py:19
  64.0 12.7 %collective-permute-start.24 = (bf16[1,1,4096]{2,1,0:T(2,128)(2,1)S(1)}, bf16[1,1,4096]{2,1,0:T(2,128)(2,1)S(1)}, u32[]{:S(2)}, u32[]{:S(2)}) collective-permute-start(bf16[1,1,4096]{2,1,0:T(2,128)(2,1)S(1)} %add_convert_fusion.1), channel_id=1, source_target_pairs={{32,0},{48,16},{64,32},{80,48},{96,64},{112,80},{128,96},{144,112}... | collective-permute-start | bytes 24584 | tf_op jit(solution)/shard_map/ppermute | solution.py:19
  70.4 9.3 %collective-permute-start.25 = (bf16[1,1,4096]{2,1,0:T(2,128)(2,1)S(1)}, bf16[1,1,4096]{2,1,0:T(2,128)(2,1)S(1)}, u32[]{:S(2)}, u32[]{:S(2)}) collective-permute-start(bf16[1,1,4096]{2,1,0:T(2,128)(2,1)S(1)} %add_convert_fusion.1), channel_id=1, source_target_pairs={{64,0},{80,16},{96,32},{112,48},{128,64},{144,80},{160,96},{176,11... | collective-permute-start | bytes 24584 | tf_op jit(solution)/shard_map/ppermute | solution.py:19
  74.8 53.1 %collective-permute-start.8 = (bf16[2,4,4096]{2,1,0:T(4,128)(2,1)S(1)}, bf16[2,4,4096]{2,1,0:T(4,128)(2,1)S(1)}, u32[]{:S(2)}, u32[]{:S(2)}) collective-permute-start(bf16[2,4,4096]{2,1,0:T(4,128)(2,1)S(1)} %reshape.2171), channel_id=1, source_target_pairs={{0,16},{16,32},{32,48},{48,64},{64,80},{80,96},{96,112},{112,128},... | collective-permute-start | bytes 196616 | tf_op jit(solution)/shard_map/ppermute | solution.py:29
  76.8 20.9 %collective-permute-start.16 = (bf16[1,1,5,4096]{3,2,1,0:T(8,128)(2,1)S(1)}, bf16[1,1,5,4096]{3,2,1,0:T(8,128)(2,1)S(1)}, u32[]{:S(2)}, u32[]{:S(2)}) collective-permute-start(bf16[1,1,5,4096]{3,2,1,0:T(8,128)(2,1)S(1)} %stack.304), channel_id=1, source_target_pairs={{0,2},{1,3},{2,4},{3,5},{4,6},{5,7},{6,8},{7,9},{8,10},{9,11},{10,... | collective-permute-start | bytes 122888 | tf_op jit(solution)/shard_map/ppermute | solution.py:19
  79.8 21.1 %collective-permute-start.17 = (bf16[1,1,5,4096]{3,2,1,0:T(8,128)(2,1)S(1)}, bf16[1,1,5,4096]{3,2,1,0:T(8,128)(2,1)S(1)}, u32[]{:S(2)}, u32[]{:S(2)}) collective-permute-start(bf16[1,1,5,4096]{3,2,1,0:T(8,128)(2,1)S(1)} %stack.304), channel_id=1, source_target_pairs={{0,1},{1,2},{2,3},{3,4},{4,5},{5,6},{6,7},{7,8},{8,9},{9,10},{10,1... | collective-permute-start | bytes 122888 | tf_op jit(solution)/shard_map/ppermute | solution.py:19
  83.1 22.4 %collective-permute-start.18 = (bf16[1,1,5,4096]{3,2,1,0:T(8,128)(2,1)S(1)}, bf16[1,1,5,4096]{3,2,1,0:T(8,128)(2,1)S(1)}, u32[]{:S(2)}, u32[]{:S(2)}) collective-permute-start(bf16[1,1,5,4096]{3,2,1,0:T(8,128)(2,1)S(1)} %stack.304), channel_id=1, source_target_pairs={{1,0},{2,1},{3,2},{4,3},{5,4},{6,5},{7,6},{8,7},{9,8},{10,9},{11,1... | collective-permute-start | bytes 122888 | tf_op jit(solution)/shard_map/ppermute | solution.py:19
  85.0 5.4 %collective-permute-start.32 = (f32[1,1,4096]{2,1,0:T(1,128)S(1)}, f32[1,1,4096]{2,1,0:T(1,128)S(1)}, u32[]{:S(2)}, u32[]{:S(2)}) collective-permute-start(f32[1,1,4096]{2,1,0:T(1,128)S(1)} %convert_add_fusion), channel_id=1, source_target_pairs={{0,32},{16,48},{32,0},{48,16},{64,96},{80,112},{96,64},{112,80},{1... | collective-permute-start | bytes 49160 | tf_op jit(solution)/shard_map/ppermute | solution.py:36
  90.4 4.5 %collective-permute-start.33 = (f32[1,1,4096]{2,1,0:T(1,128)S(1)}, f32[1,1,4096]{2,1,0:T(1,128)S(1)}, u32[]{:S(2)}, u32[]{:S(2)}) collective-permute-start(f32[1,1,4096]{2,1,0:T(1,128)S(1)} %add.442), channel_id=1, source_target_pairs={{0,2},{1,3},{2,0},{3,1},{4,6},{5,7},{6,4},{7,5},{8,10},{9,11},{10,... | collective-permute-start | bytes 49160 | tf_op jit(solution)/shard_map/ppermute | solution.py:36
  94.9 16.1 %collective-permute-start.19 = (bf16[1,1,5,4096]{3,2,1,0:T(8,128)(2,1)S(1)}, bf16[1,1,5,4096]{3,2,1,0:T(8,128)(2,1)S(1)}, u32[]{:S(2)}, u32[]{:S(2)}) collective-permute-start(bf16[1,1,5,4096]{3,2,1,0:T(8,128)(2,1)S(1)} %stack.304), channel_id=1, source_target_pairs={{2,0},{3,1},{4,2},{5,3},{6,4},{7,5},{8,6},{9,7},{10,8},{11,9},{12,... | collective-permute-start | bytes 122888 | tf_op jit(solution)/shard_map/ppermute | solution.py:19
  97.7 17.4 %collective-permute-start.34 = (bf16[1,1,4096]{2,1,0:T(2,128)(2,1)S(1)}, bf16[1,1,4096]{2,1,0:T(2,128)(2,1)S(1)}, u32[]{:S(2)}, u32[]{:S(2)}) collective-permute-start(bf16[1,1,4096]{2,1,0:T(2,128)(2,1)S(1)} %add_convert_fusion), channel_id=1, source_target_pairs={{0,128},{16,144},{32,160},{48,176},{64,192},{80,208},{96,224},{112... | collective-permute-start | bytes 24584 | tf_op jit(solution)/shard_map/ppermute | solution.py:19
  100.9 19.1 %collective-permute-start.35 = (bf16[1,1,4096]{2,1,0:T(2,128)(2,1)S(1)}, bf16[1,1,4096]{2,1,0:T(2,128)(2,1)S(1)}, u32[]{:S(2)}, u32[]{:S(2)}) collective-permute-start(bf16[1,1,4096]{2,1,0:T(2,128)(2,1)S(1)} %add_convert_fusion), channel_id=1, source_target_pairs={{0,64},{16,80},{32,96},{48,112},{64,128},{80,144},{96,160},{112,17... | collective-permute-start | bytes 24584 | tf_op jit(solution)/shard_map/ppermute | solution.py:19
  105.5 16.5 %collective-permute-start.36 = (bf16[1,1,4096]{2,1,0:T(2,128)(2,1)S(1)}, bf16[1,1,4096]{2,1,0:T(2,128)(2,1)S(1)}, u32[]{:S(2)}, u32[]{:S(2)}) collective-permute-start(bf16[1,1,4096]{2,1,0:T(2,128)(2,1)S(1)} %add_convert_fusion), channel_id=1, source_target_pairs={{64,0},{80,16},{96,32},{112,48},{128,64},{144,80},{160,96},{176,11... | collective-permute-start | bytes 24584 | tf_op jit(solution)/shard_map/ppermute | solution.py:19
  111.0 14.3 %collective-permute-start.37 = (bf16[1,1,4096]{2,1,0:T(2,128)(2,1)S(1)}, bf16[1,1,4096]{2,1,0:T(2,128)(2,1)S(1)}, u32[]{:S(2)}, u32[]{:S(2)}) collective-permute-start(bf16[1,1,4096]{2,1,0:T(2,128)(2,1)S(1)} %add_convert_fusion), channel_id=1, source_target_pairs={{128,0},{144,16},{160,32},{176,48},{192,64},{208,80},{224,96},{240... | collective-permute-start | bytes 24584 | tf_op jit(solution)/shard_map/ppermute | solution.py:19
  113.5 35.0 %copy-start.14 = (bf16[5,5]{0,1:T(8,128)(2,1)S(1)}, bf16[5,5]{0,1:T(8,128)(2,1)}, u32[]{:S(2)}) copy-start(bf16[5,5]{0,1:T(8,128)(2,1)} %copy.92) | copy-start | bytes 154
  115.1 16.0 %collective-permute-start.9 = (bf16[2,4,4096]{2,1,0:T(4,128)(2,1)S(1)}, bf16[2,4,4096]{2,1,0:T(4,128)(2,1)S(1)}, u32[]{:S(2)}, u32[]{:S(2)}) collective-permute-start(bf16[2,4,4096]{2,1,0:T(4,128)(2,1)S(1)} %reshape.2171), channel_id=1, source_target_pairs={{16,0},{32,16},{48,32},{64,48},{80,64},{96,80},{112,96},{128,112},... | collective-permute-start | bytes 196616 | tf_op jit(solution)/shard_map/ppermute | solution.py:30
  120.0 65.4 %collective-permute-start.1 = (bf16[1,4,64,512]{3,2,1,0:T(8,128)(2,1)}, bf16[1,4,64,512]{3,2,1,0:T(8,128)(2,1)}, u32[]{:S(2)}, u32[]{:S(2)}) collective-permute-start(bf16[1,4,64,512]{3,2,1,0:T(8,128)(2,1)} %get-tuple-element.118), channel_id=1, source_target_pairs={{16,0},{32,16},{48,32},{64,48},{80,64},{96,80},{112,96},{128,112},... | collective-permute-start | bytes 786440 | tf_op jit(solution)/shard_map/ppermute | solution.py:30
  122.0 62.5 %collective-permute-start = (bf16[1,4,64,512]{3,2,1,0:T(8,128)(2,1)}, bf16[1,4,64,512]{3,2,1,0:T(8,128)(2,1)}, u32[]{:S(2)}, u32[]{:S(2)}) collective-permute-start(bf16[1,4,64,512]{3,2,1,0:T(8,128)(2,1)} %get-tuple-element.119), channel_id=1, source_target_pairs={{0,16},{16,32},{32,48},{48,64},{64,80},{80,96},{96,112},{112,128},... | collective-permute-start | bytes 786440 | tf_op jit(solution)/shard_map/ppermute | solution.py:29
  125.3 9.8 %collective-permute-start.26 = (bf16[1,1,5,4096]{3,2,1,0:T(8,128)(2,1)S(1)}, bf16[1,1,5,4096]{3,2,1,0:T(8,128)(2,1)S(1)}, u32[]{:S(2)}, u32[]{:S(2)}) collective-permute-start(bf16[1,1,5,4096]{3,2,1,0:T(8,128)(2,1)S(1)} %stack.316), channel_id=1, source_target_pairs={{0,4},{1,5},{2,6},{3,7},{4,8},{5,9},{6,10},{7,11},{8,12},{9,13},{1... | collective-permute-start | bytes 122888 | tf_op jit(solution)/shard_map/ppermute | solution.py:19
  128.0 10.2 %collective-permute-start.27 = (bf16[1,1,5,4096]{3,2,1,0:T(8,128)(2,1)S(1)}, bf16[1,1,5,4096]{3,2,1,0:T(8,128)(2,1)S(1)}, u32[]{:S(2)}, u32[]{:S(2)}) collective-permute-start(bf16[1,1,5,4096]{3,2,1,0:T(8,128)(2,1)S(1)} %stack.316), channel_id=1, source_target_pairs={{0,2},{1,3},{2,4},{3,5},{4,6},{5,7},{6,8},{7,9},{8,10},{9,11},{10,... | collective-permute-start | bytes 122888 | tf_op jit(solution)/shard_map/ppermute | solution.py:19
  131.1 9.9 %collective-permute-start.28 = (bf16[1,1,5,4096]{3,2,1,0:T(8,128)(2,1)S(1)}, bf16[1,1,5,4096]{3,2,1,0:T(8,128)(2,1)S(1)}, u32[]{:S(2)}, u32[]{:S(2)}) collective-permute-start(bf16[1,1,5,4096]{3,2,1,0:T(8,128)(2,1)S(1)} %stack.316), channel_id=1, source_target_pairs={{2,0},{3,1},{4,2},{5,3},{6,4},{7,5},{8,6},{9,7},{10,8},{11,9},{12,... | collective-permute-start | bytes 122888 | tf_op jit(solution)/shard_map/ppermute | solution.py:19
  135.1 8.8 %collective-permute-start.29 = (bf16[1,1,5,4096]{3,2,1,0:T(8,128)(2,1)S(1)}, bf16[1,1,5,4096]{3,2,1,0:T(8,128)(2,1)S(1)}, u32[]{:S(2)}, u32[]{:S(2)}) collective-permute-start(bf16[1,1,5,4096]{3,2,1,0:T(8,128)(2,1)S(1)} %stack.316), channel_id=1, source_target_pairs={{4,0},{5,1},{6,2},{7,3},{8,4},{9,5},{10,6},{11,7},{12,8},{13,9},{1... | collective-permute-start | bytes 122888 | tf_op jit(solution)/shard_map/ppermute | solution.py:19
  138.2 12.8 %collective-permute-start.38 = (bf16[1,1,5,4096]{3,2,1,0:T(8,128)(2,1)S(1)}, bf16[1,1,5,4096]{3,2,1,0:T(8,128)(2,1)S(1)}, u32[]{:S(2)}, u32[]{:S(2)}) collective-permute-start(bf16[1,1,5,4096]{3,2,1,0:T(8,128)(2,1)S(1)} %stack.328), channel_id=1, source_target_pairs={{0,8},{1,9},{2,10},{3,11},{4,12},{5,13},{6,14},{7,15},{16,24},{17,... | collective-permute-start | bytes 122888 | tf_op jit(solution)/shard_map/ppermute | solution.py:19
  141.1 11.2 %collective-permute-start.39 = (bf16[1,1,5,4096]{3,2,1,0:T(8,128)(2,1)S(1)}, bf16[1,1,5,4096]{3,2,1,0:T(8,128)(2,1)}, u32[]{:S(2)}, u32[]{:S(2)}) collective-permute-start(bf16[1,1,5,4096]{3,2,1,0:T(8,128)(2,1)S(1)} %stack.328), channel_id=1, source_target_pairs={{0,4},{1,5},{2,6},{3,7},{4,8},{5,9},{6,10},{7,11},{8,12},{9,13},{1... | collective-permute-start | bytes 122888 | tf_op jit(solution)/shard_map/ppermute | solution.py:19
  143.9 23.1 %collective-permute-start.40 = (bf16[1,1,5,4096]{3,2,1,0:T(8,128)(2,1)S(1)}, bf16[1,1,5,4096]{3,2,1,0:T(8,128)(2,1)}, u32[]{:S(2)}, u32[]{:S(2)}) collective-permute-start(bf16[1,1,5,4096]{3,2,1,0:T(8,128)(2,1)S(1)} %stack.328), channel_id=1, source_target_pairs={{4,0},{5,1},{6,2},{7,3},{8,4},{9,5},{10,6},{11,7},{12,8},{13,9},{1... | collective-permute-start | bytes 122888 | tf_op jit(solution)/shard_map/ppermute | solution.py:19
  151.0 18.7 %collective-permute-start.41 = (bf16[1,1,5,4096]{3,2,1,0:T(8,128)(2,1)S(1)}, bf16[1,1,5,4096]{3,2,1,0:T(8,128)(2,1)S(1)}, u32[]{:S(2)}, u32[]{:S(2)}) collective-permute-start(bf16[1,1,5,4096]{3,2,1,0:T(8,128)(2,1)S(1)} %stack.328), channel_id=1, source_target_pairs={{8,0},{9,1},{10,2},{11,3},{12,4},{13,5},{14,6},{15,7},{24,16},{25,... | collective-permute-start | bytes 122888 | tf_op jit(solution)/shard_map/ppermute | solution.py:19
  152.3 19.9 %collective-permute-start.10 = (bf16[6,2,4096]{2,1,0:T(2,128)(2,1)}, bf16[6,2,4096]{2,1,0:T(2,128)(2,1)S(1)}, u32[]{:S(2)}, u32[]{:S(2)}) collective-permute-start(bf16[6,2,4096]{2,1,0:T(2,128)(2,1)} %get-tuple-element.121), channel_id=1, source_target_pairs={{0,1},{1,2},{2,3},{3,4},{4,5},{5,6},{6,7},{7,8},{8,9},{9,10},{10,1... | collective-permute-start | bytes 294920 | tf_op jit(solution)/shard_map/ppermute | solution.py:29
  166.9 7.4 %collective-permute-start.11 = (bf16[6,2,4096]{2,1,0:T(2,128)(2,1)}, bf16[6,2,4096]{2,1,0:T(2,128)(2,1)S(1)}, u32[]{:S(2)}, u32[]{:S(2)}) collective-permute-start(bf16[6,2,4096]{2,1,0:T(2,128)(2,1)} %get-tuple-element.120), channel_id=1, source_target_pairs={{1,0},{2,1},{3,2},{4,3},{5,4},{6,5},{7,6},{8,7},{9,8},{10,9},{11,1... | collective-permute-start | bytes 294920 | tf_op jit(solution)/shard_map/ppermute | solution.py:30
  187.8 11.1 %collective-permute-start.3 = (bf16[4,1,64,512]{3,2,1,0:T(8,128)(2,1)S(1)}, bf16[4,1,64,512]{3,2,1,0:T(8,128)(2,1)S(1)}, u32[]{:S(2)}, u32[]{:S(2)}) collective-permute-start(bf16[4,1,64,512]{3,2,1,0:T(8,128)(2,1)S(1)} %get-tuple-element.113), channel_id=1, source_target_pairs={{1,0},{2,1},{3,2},{4,3},{5,4},{6,5},{7,6},{8,7},{9,8},{10,9},{11,1... | collective-permute-start | bytes 786440 | tf_op jit(solution)/shard_map/ppermute | solution.py:30
  189.7 9.2 %collective-permute-start.2 = (bf16[4,1,64,512]{3,2,1,0:T(8,128)(2,1)S(1)}, bf16[4,1,64,512]{3,2,1,0:T(8,128)(2,1)S(1)}, u32[]{:S(2)}, u32[]{:S(2)}) collective-permute-start(bf16[4,1,64,512]{3,2,1,0:T(8,128)(2,1)S(1)} %get-tuple-element.114), channel_id=1, source_target_pairs={{0,1},{1,2},{2,3},{3,4},{4,5},{5,6},{6,7},{7,8},{8,9},{9,10},{10,1... | collective-permute-start | bytes 786440 | tf_op jit(solution)/shard_map/ppermute | solution.py:29
  201.9 69.1 %copy-start.4 = (bf16[2,4,64,512]{3,2,1,0:T(8,128)(2,1)S(1)}, bf16[2,4,64,512]{3,2,1,0:T(8,128)(2,1)}, u32[]{:S(2)}) copy-start(bf16[2,4,64,512]{3,2,1,0:T(8,128)(2,1)} %param.14) | copy-start | bytes 1572868
  201.9 69.1 %copy-start.6 = (bf16[2,4,64,64]{3,2,1,0:T(8,128)(2,1)S(1)}, bf16[2,4,64,64]{3,2,1,0:T(8,128)(2,1)}, u32[]{:S(2)}) copy-start(bf16[2,4,64,64]{3,2,1,0:T(8,128)(2,1)} %param.18) | copy-start | bytes 196612
  201.9 69.1 %copy-start.11 = (bf16[64,64,1,1]{1,0,3,2:T(8,128)(2,1)S(1)}, bf16[64,64,1,1]{1,0,3,2:T(8,128)(2,1)}, u32[]{:S(2)}) copy-start(bf16[64,64,1,1]{1,0,3,2:T(8,128)(2,1)} %fusion.27) | copy-start | bytes 24580
  (12 other events, 182.4 us)
where the time goes:
time: 276 us; the launch traced here: 273 us
  starting transfers between devices  152 us (55%)
  other arithmetic  51.4 us (19%)
  matrix products  31.1 us (11%)
  local copies, waits for them, and re-layouts  28.5 us (10%)
  waiting for transfers between devices  7.92 us (3%)
    ppermute x24, starting transfers between devices, from_behind(): lax.ppermute(value, axis, [(source, source + steps) for source in range(i...  85.6 us
    ppermute x6, starting transfers between devices, padded(): before = lax.ppermute(last, axis, up)  31.4 us
    while x64, other arithmetic  29.8 us
    ppermute x6, starting transfers between devices, padded(): after = lax.ppermute(initial, axis, down)  17.6 us
    ppermute x6, starting transfers between devices, swapped(): lax.ppermute(array, axis, [(i, i ^ 1 << bit) for i in range(lax.axis_size...  17.3 us
    dot_general x8, matrix products, near_leaf(): jnp.einsum('slp,spq->lq', weighted, tiles, preferred_element_type=jnp.flo...  16.3 us
    another operation x3, local copies, waits for them, and re-layouts, body(): jnp.stack(windows, axis=2)  8.8 us
    convert_element_type x8, other arithmetic, near_tile(): source = source_off.astype(jnp.float32)  6.75 us
  transfers between devices with their start and end apart: 42, of which 4 were waited for; matrix products, arithmetic and copies ran while one was open for 12% of the time, Pallas kernels for 0%

commit v1 on v0

v1 whole, which is shorter than its diff:
```python
import functools

import jax
import jax.numpy as jnp
from jax import lax
from jax.experimental import pallas as pl
from jax.experimental.pallas import tpu as pltpu
from jax.sharding import PartitionSpec as P

PANELS = 512
RANK = 64
LOADS = 64
EPSILON = 0.001
F32 = jnp.float32
BF16 = jnp.bfloat16
NT = (((1,), (1,)), ((), ()))
TN = (((0,), (0,)), ((), ()))
WIDE = 25 * RANK
MIB = 2**20
VMEM = pl.BlockSpec(memory_space=pltpu.VMEM)
SMEM = pl.BlockSpec(memory_space=pltpu.SMEM)

ROW_OFFS, ROW_POLES, ROW_BOX, ROW_ALL = 256, 272, 336, 352
COL_OFFS, COL_POLES, COL_BOX, COL_ALL = 256, 272, 368, 416


def shifted(value, axis, steps):
    count = lax.axis_size(axis)
    initial, last = (max(0, -steps), min(count, count - steps))
    return lax.ppermute(value, axis, [(source, source + steps) for source in range(initial, last)])


def swapped(value, axis, bit):
    return lax.ppermute(value, axis, [(i, i ^ 1 << bit) for i in range(lax.axis_size(axis))])


def kernel_call(body, outs, scratch, name, cost, *args, smem=()):
    return pl.pallas_call(
        body,
        out_shape=outs,
        in_specs=[SMEM if i in smem else VMEM for i in range(len(args))],
        out_specs=jax.tree.map(lambda _: VMEM, outs),
        scratch_shapes=scratch,
        compiler_params=pltpu.CompilerParams(vmem_limit_bytes=40 * MIB),
        cost_estimate=pl.CostEstimate(flops=cost, bytes_accessed=4 * MIB, transcendentals=0),
        name=name,
    )(*args)


def shape(dims, dtype=BF16):
    return jax.ShapeDtypeStruct(dims, dtype)


def fold(matrix):
    return jnp.concatenate([matrix[:32], matrix[32:]], axis=1)


def unfold(folded):
    return jnp.concatenate([folded[:, :64], folded[:, 64:]], axis=0)


def flat(folded):
    return jnp.concatenate([folded[:16], folded[16:]], axis=1)


def unflat(flattened):
    return jnp.concatenate([flattened[:, :128], flattened[:, 128:]], axis=0)


def rows_of(values, count):
    row = lax.broadcasted_iota(jnp.int32, (count, PANELS), 0)
    out = jnp.zeros((count, PANELS), F32)
    for index, value in enumerate(values):
        out = jnp.where(row == index, value, out)
    return out


def three_parts(value):
    high = value.astype(BF16).astype(F32)
    rest = value - high
    middle = rest.astype(BF16).astype(F32)
    low = (rest - middle).astype(BF16).astype(F32)
    return high, middle, low


def target_features(off):
    x, y, z = off[0:1], off[1:2], off[2:3]
    high, middle, low = three_parts(PANELS * (x * x + y * y + z * z + EPSILON))
    return rows_of([x, y, z, x, y, high, middle, low, 1.0, 1.0, 1.0], 16).T.astype(BF16)


def source_features(off, row_off, col_off):
    x, y, z = off[0:1], off[1:2], off[2:3]
    x_moved, y_moved = x + col_off, y + row_off
    high, middle, low = three_parts(PANELS * (x_moved * x_moved + y_moved * y_moved + z * z))
    twice = -2.0 * PANELS
    return rows_of(
        [twice * x, twice * y, twice * z, twice * col_off, twice * row_off, 1.0, 1.0, 1.0, high, middle, low], 16
    ).astype(BF16)


def near_pairs(pairs, mask, listed, target_feats, source_offs, source_charges, acc):
    count = jnp.int32(0)
    for target, slot, source, row_off, col_off in pairs:
        listed[count] = target + 16 * source + 256 * (row_off + 1) + 1024 * (col_off + 1)
        count = count + (1 if slot is None else mask[target, slot])

    def one(index):
        code = listed[index]
        target = code & 15
        source = (code >> 4) & 15
        row_off = ((code >> 8) & 3) - 1
        col_off = ((code >> 10) & 3) - 1
        moved = source_features(source_offs[source, 0:3, :], row_off.astype(F32), col_off.astype(F32))
        squared = jnp.dot(target_feats[target], moved, preferred_element_type=F32)
        tile = lax.rsqrt(squared).astype(BF16)
        acc[target] += lax.dot_general(source_charges[source], tile, NT, preferred_element_type=F32)

    def several(step, carry):
        for k in range(4):
            one(4 * step + k)
        return carry

    def single(step, carry):
        one(step)
        return carry

    fours = count // 4
    lax.fori_loop(0, fours, several, 0)
    lax.fori_loop(4 * fours, count, single, 0)


def slot_of(row_off, col_off):
    place = 3 * (row_off + 1) + col_off + 1
    return None if place == 4 else place - (place > 4)


def inner_pairs(row):
    found = []
    for col in range(4):
        for row_off in (-1, 0, 1):
            for col_off in (-1, 0, 1):
                at_row, at_col = row + row_off, col + col_off
                if 0 <= at_row < 2 and 0 <= at_col < 4:
                    found.append((4 * row + col, slot_of(row_off, col_off), 4 * at_row + at_col, row_off, col_off))
    return found


def row_pairs():
    found = []
    for row, row_off in ((0, -1), (1, 1)):
        for col in range(4):
            for col_off in (-1, 0, 1):
                if 0 <= col + col_off < 4:
                    found.append((4 * row + col, slot_of(row_off, col_off), 4 * row + col + col_off, row_off, col_off))
    return found


def col_pairs():
    found = []
    for side, col, col_off in ((0, 0, -1), (1, 3, 1)):
        for row in range(2):
            for row_off in (-1, 0, 1):
                found.append((4 * row + col, slot_of(row_off, col_off), 4 * side + row + row_off + 1, row_off, col_off))
    return found


def first_kernel(charges, offsets, basis, transfer, parent, up, down, small, poles_out):
    poles = []
    box = jnp.zeros((RANK, LOADS), F32)
    for leaf in range(8):
        pole = lax.dot_general(basis[leaf], charges[leaf], NT, preferred_element_type=F32).astype(BF16)
        poles.append(pole)
        box = box + lax.dot_general(transfer[leaf], pole, TN, preferred_element_type=F32)
    box = box.astype(BF16)
    small[0] = fold(box)
    for level in range(2):
        term = lax.dot_general(parent[level], box, TN, preferred_element_type=F32)
        small[1 + level] = fold(term.astype(BF16))
    pairs = [jnp.concatenate([poles[2 * k], poles[2 * k + 1]], axis=1) for k in range(4)]
    for k in range(4):
        poles_out[k] = pairs[k]
    for row, buffer in ((0, down), (1, up)):
        offs = []
        for col in range(4):
            leaf = 4 * row + col
            buffer[64 * col : 64 * (col + 1), :] = charges[leaf]
            off = offsets[leaf].astype(F32)
            offs += [off[0:1], off[1:2], off[2:3]]
        buffer[ROW_OFFS:ROW_POLES, :] = rows_of(offs, 16).astype(BF16)
        for k in range(4):
            buffer[ROW_POLES:ROW_BOX, 128 * k : 128 * (k + 1)] = pairs[k]
        buffer[ROW_BOX:ROW_ALL, 0:256] = flat(fold(box))
        buffer[ROW_BOX:ROW_ALL, 256:512] = jnp.zeros((16, 256), BF16)


def inner_kernel(row, mask, charges, offsets, out, listed, feats, offs, acc):
    for leaf in range(8):
        offs[leaf, 0:3, :] = offsets[leaf].astype(F32)
    for col in range(4):
        feats[4 * row + col] = target_features(offs[4 * row + col, 0:3, :])
        acc[4 * row + col] = jnp.zeros((LOADS, PANELS), F32)
    near_pairs(inner_pairs(row), mask, listed, feats, offs, charges, acc)
    out[...] = acc[4 * row : 4 * row + 4]


def spread_offsets(packed, offs, base):
    values = packed.astype(F32)
    for leaf in range(4):
        offs[base + leaf, 0:3, :] = values[3 * leaf : 3 * leaf + 3]


def row_kernel(mask, offsets, top, bottom, out, listed, feats, offs, charges, acc):
    for leaf in range(8):
        feats[leaf] = target_features(offsets[leaf].astype(F32))
    for side, buffer in ((0, top), (1, bottom)):
        spread_offsets(buffer[ROW_OFFS:ROW_POLES, :], offs, 4 * side)
        for col in range(4):
            charges[4 * side + col] = buffer[64 * col : 64 * (col + 1), :]
    acc[...] = jnp.zeros_like(acc)
    near_pairs(row_pairs(), mask, listed, feats, offs, charges, acc)
    out[...] = acc[...]


def pack_kernel(charges, offsets, poles, top, bottom, boxes, right, left):
    for buffer, col in ((right, 3), (left, 0)):
        pair = col // 2
        offs = []
        for place, source in enumerate((top, None, None, bottom)):
            if source is None:
                leaf = 4 * (place - 1) + col
                buffer[64 * place : 64 * (place + 1), :] = charges[leaf]
                off = offsets[leaf].astype(F32)
            else:
                buffer[64 * place : 64 * (place + 1), :] = source[64 * col : 64 * (col + 1), :]
                off = source[ROW_OFFS:ROW_POLES, :].astype(F32)[3 * col : 3 * col + 3]
            offs += [off[0:1], off[1:2], off[2:3]]
        buffer[COL_OFFS:COL_POLES, :] = rows_of(offs, 16).astype(BF16)
        for row in range(6):
            if row < 2:
                start = 128 * (2 * row + pair)
                pole = top[ROW_POLES:ROW_BOX, start : start + 128]
            elif row < 4:
                pole = poles[2 * (row - 2) + pair]
            else:
                start = 128 * (2 * (row - 4) + pair)
                pole = bottom[ROW_POLES:ROW_BOX, start : start + 128]
            base, lane = COL_POLES + 32 * (row // 2), 256 * (row % 2)
            buffer[base : base + 32, lane : lane + 128] = pole[:32]
            buffer[base : base + 32, lane + 128 : lane + 256] = pole[32:]
        for row in range(5):
            base, lane = COL_BOX + 16 * (row // 2), 256 * (row % 2)
            buffer[base : base + 16, lane : lane + 256] = flat(boxes[row])
        buffer[COL_BOX + 32 : COL_ALL, 256:512] = jnp.zeros((16, 256), BF16)


def flag_row(flags, which):
    row = lax.broadcasted_iota(jnp.int32, (32, WIDE), 0)
    lane = lax.broadcasted_iota(jnp.int32, (32, WIDE), 1)
    spread = jnp.where((lane >> 6) == row, 1.0, 0.0).astype(BF16)
    return jnp.dot(flags, spread, preferred_element_type=F32)


def box_product(coupling, flags, window):
    return jnp.dot(coupling * flags, window, preferred_element_type=F32)


def edge_kernel(
    mask, offsets, left, right, inner_top, inner_bottom, by_rows, poles, top, bottom, flags, coupling,
    box_coupling, boxes, far_left, far_right,
    out, leaf_out, box_out, listed, feats, offs, charges, acc, table, window,
):
    for col in (0, 3):
        for row in range(2):
            feats[4 * row + col] = target_features(offsets[4 * row + col].astype(F32))
    for side, buffer in ((0, left), (1, right)):
        spread_offsets(buffer[COL_OFFS:COL_POLES, :], offs, 4 * side)
        for place in range(4):
            charges[4 * side + place] = buffer[64 * place : 64 * (place + 1), :]
    acc[0:4] = inner_top[...] + by_rows[0:4]
    acc[4:8] = inner_bottom[...] + by_rows[4:8]
    near_pairs(col_pairs(), mask, listed, feats, offs, charges, acc)
    out[...] = acc[...]
    for row in range(6):
        for pair in range(4):
            if pair in (0, 3):
                buffer = left if pair == 0 else right
                base, lane = COL_POLES + 32 * (row // 2), 256 * (row % 2)
                both = jnp.concatenate(
                    [buffer[base : base + 32, lane : lane + 128], buffer[base : base + 32, lane + 128 : lane + 256]], axis=0
                )
            elif row in (2, 3):
                both = poles[2 * (row - 2) + pair - 1]
            else:
                buffer, at = (top, row) if row < 2 else (bottom, row - 4)
                start = 128 * (2 * at + pair - 1)
                both = buffer[ROW_POLES:ROW_BOX, start : start + 128]
            table[row, 128 * pair : 128 * pair + 64, :] = both[:, :64]
            table[row, 128 * pair + 64 : 128 * pair + 128, :] = both[:, 64:]
    spread = flag_row(flags[...], 0).astype(BF16)
    for row in range(2):
        for col in range(4):
            leaf = 4 * row + col
            seen = jnp.concatenate([table[row + a, 64 * col : 64 * (col + 5), :] for a in range(5)], axis=0)
            leaf_out[leaf] = box_product(coupling[leaf], spread[leaf : leaf + 1], seen)
    for row in range(5):
        base, lane = COL_BOX + 16 * (row // 2), 256 * (row % 2)
        found = (
            far_left[row],
            unflat(left[base : base + 16, lane : lane + 256]),
            boxes[row],
            unflat(right[base : base + 16, lane : lane + 256]),
            far_right[row],
        )
        for col in range(5):
            start = 64 * (5 * row + col)
            window[start : start + 64, :] = unfold(found[col])
    box_out[...] = box_product(box_coupling[0], spread[8:9], window[...])


def last_kernel(
    near, leaf_local, box_one, flags, box_coupling, transfer, basis,
    box2, box2_left, box2_right, box3, box4_left, box4_right, box8, group,
    out, window,
):
    spread = flag_row(flags[...], 0).astype(BF16)
    total = box_one[...]
    lower = (group[0] < 2).astype(BF16)
    upper = (group[0] >= 2).astype(BF16)
    for level in range(2):
        for row in range(5):
            if level == 0:
                found = (box4_left[row], box2_left[5 + row], box2[row], box2_right[5 + row], box4_right[row])
            else:
                found = (box8[row] * upper, box4_left[5 + row], box3[row], box4_right[5 + row], box8[row] * lower)
            for col in range(5):
                start = 64 * (5 * row + col)
                window[start : start + 64, :] = unfold(found[col])
        total = total + box_product(box_coupling[1 + level], spread[9 + level : 10 + level], window[...])
    total = total.astype(BF16)
    for leaf in range(8):
        local = leaf_local[leaf] + jnp.dot(transfer[leaf], total, preferred_element_type=F32)
        far = lax.dot_general(local.astype(BF16), basis[leaf], TN, preferred_element_type=F32)
        out[leaf] = (near[leaf] + far).astype(BF16)


def near_scratch(sources):
    return [
        pltpu.SMEM((32,), jnp.int32),
        pltpu.VMEM((8, PANELS, 16), BF16),
        pltpu.VMEM((8, 8, PANELS), F32),
        *([pltpu.VMEM((8, LOADS, PANELS), BF16)] if sources else []),
        pltpu.VMEM((8, LOADS, PANELS), F32),
    ]


def body(
    charges,
    offsets,
    leaf_basis,
    near_mask,
    leaf_coupling,
    leaf_distant_flags,
    leaf_transfer,
    box_coupling,
    box_far,
    parent_child_transfer,
):
    charges = charges.reshape(8, LOADS, PANELS)
    offsets = offsets.reshape(8, 3, PANELS)
    basis = leaf_basis.reshape(8, RANK, PANELS)
    mask = near_mask.reshape(8, 8)
    coupling = leaf_coupling.reshape(8, RANK, WIDE)
    transfer = leaf_transfer.reshape(8, RANK, RANK)
    box_coupling = box_coupling.reshape(3, RANK, WIDE)
    parent = parent_child_transfer.reshape(2, RANK, RANK)
    flags = jnp.concatenate([leaf_distant_flags.reshape(8, 25), box_far.reshape(3, 25)], axis=0)
    flags = jnp.pad(flags, ((0, 5), (0, 7))).astype(BF16)
    row_at, col_at = lax.axis_index("row"), lax.axis_index("col")

    up, down, small, poles = kernel_call(
        first_kernel,
        (shape((ROW_ALL, 512)), shape((ROW_ALL, 512)), shape((3, 32, 128)), shape((4, 64, 128))),
        [], "first", 10**9, charges, offsets, basis, transfer, parent,
    )
    terms = small[1:3]
    terms_peer = swapped(terms, "row", 0)
    top = shifted(up, "row", 1)
    bottom = shifted(down, "row", -1)
    near_cost = 6 * 10**9
    inner = [
        kernel_call(
            functools.partial(inner_kernel, row), shape((4, LOADS, PANELS), F32), near_scratch(False),
            f"inner{row}", near_cost, mask, charges, offsets, smem=(0,),
        )
        for row in range(2)
    ]
    sums = terms.astype(F32) + terms_peer.astype(F32)
    sums = sums + swapped(sums.astype(BF16), "col", 0).astype(F32)
    box1, sums = small[0], sums.astype(BF16)
    near_by_two = jnp.concatenate([box1[None], sums], axis=0)
    above = shifted(near_by_two, "row", 2)
    below = shifted(near_by_two, "row", -2)
    second_even = (row_at // 2) % 2 == 0
    row3 = sums[1].astype(F32) + jnp.where(second_even, below[2], above[2]).astype(F32)
    row3 = row3.astype(BF16)
    by_four = jnp.stack([sums[0], row3])
    above4, below4 = shifted(by_four, "row", 4), shifted(by_four, "row", -4)
    above8, below8 = shifted(row3, "row", 8), shifted(row3, "row", -8)

    def box_from(buffer):
        flattened = buffer[ROW_BOX:ROW_ALL, 0:256]
        return jnp.concatenate([flattened[:, :128], flattened[:, 128:]], axis=0)

    boxes1 = jnp.stack([above[0], box_from(top), box1, box_from(bottom), below[0]])
    boxes2 = jnp.stack([above4[0], above[1], sums[0], below[1], below4[0]])
    rows3 = jnp.stack([above8, above4[1], row3, below4[1], below8])
    right, left = kernel_call(
        pack_kernel, (shape((COL_ALL, 512)), shape((COL_ALL, 512))), [], "pack", 10**8,
        charges, offsets, poles, top, bottom, boxes1,
    )
    from_left = shifted(right, "col", 1)
    from_right = shifted(left, "col", -1)
    by_rows = kernel_call(
        row_kernel, shape((8, LOADS, PANELS), F32), near_scratch(True), "byrows", near_cost,
        mask, offsets, top, bottom, smem=(0,),
    )
    stacks = jnp.concatenate([boxes1, boxes2, rows3], axis=0)
    stacks_left = shifted(stacks, "col", 2)
    stacks_right = shifted(stacks, "col", -2)
    second_even = (col_at // 2) % 2 == 0
    boxes3 = rows3.astype(F32) + jnp.where(second_even, stacks_right[10:], stacks_left[10:]).astype(F32)
    boxes3 = boxes3.astype(BF16)
    by_four = jnp.concatenate([boxes2, boxes3], axis=0)
    left4, right4 = shifted(by_four, "col", 4), shifted(by_four, "col", -4)
    across = swapped(boxes3, "col", 3)
    near, leaf_local, box_one = kernel_call(
        edge_kernel,
        (shape((8, LOADS, PANELS), F32), shape((8, RANK, LOADS), F32), shape((RANK, LOADS), F32)),
        near_scratch(True) + [pltpu.VMEM((6, 512, LOADS), BF16), pltpu.VMEM((WIDE, LOADS), BF16)],
        "edge", near_cost, mask, offsets, from_left, from_right, inner[0], inner[1], by_rows, poles, top, bottom,
        flags, coupling, box_coupling, boxes1, stacks_left, stacks_right, smem=(0,),
    )
    group = (col_at // 4).astype(jnp.int32).reshape(1)
    out = kernel_call(
        last_kernel, shape((8, LOADS, PANELS)), [pltpu.VMEM((WIDE, LOADS), BF16)], "last", 10**9,
        near, leaf_local, box_one, flags, box_coupling, transfer, basis,
        boxes2, stacks_left, stacks_right, boxes3, left4, right4, across, group, smem=(14,),
    )
    return out.reshape(2, 4, LOADS, PANELS)


def solution(mesh):
    return jax.shard_map(
        body,
        mesh=mesh,
        in_specs=(
            P("row", "col", None, None),
            P("row", "col", None, None),
            P("row", "col", None, None),
            P("row", "col", None),
            P("row", "col", None, None),
            P("row", "col", None),
            P("row", "col", None, None),
            P("row", "col", None, None, None),
            P("row", "col", None, None),
            P("row", "col", None, None, None),
        ),
        out_specs=P("row", "col", None, None),
        check_vma=False,
    )
```

time: 276 us -> 108 us (0.39)
  the two profiles are of different devices: /device:TPU:29 before, /device:TPU:4 now
where the time goes in v1:
time: 108 us; the launch traced here: 107 us
  starting transfers between devices  72.1 us (67%)
  Pallas kernels  26.7 us (25%)
  local copies, waits for them, and re-layouts  4.7 us (4%)
  waiting for transfers between devices  3.18 us (3%)
    ppermute x14, starting transfers between devices, shifted(): lax.ppermute(value, axis, [(source, source + steps) for source in range(i...  56.7 us
    pallas_call x7, Pallas kernels, kernel_call(): pl.pallas_call(body, out_shape=outs, in_specs=[SMEM if i in smem else VME...  26.7 us
    ppermute x3, starting transfers between devices, swapped(): lax.ppermute(value, axis, [(i, i ^ 1 << bit) for i in range(lax.axis_size...  15.3 us
    unnamed x41, local copies, waits for them, and re-layouts  4.68 us
    ppermute x14, waiting for transfers between devices, shifted(): lax.ppermute(value, axis, [(source, source + steps) for source in range(i...  3.17 us
  transfers between devices with their start and end apart: 17, of which 3 were waited for; matrix products, arithmetic and copies ran while one was open for 0% of the time, Pallas kernels for 21%

profile of v1, /device:TPU:4, one launch (start us, length us, event | category | flops | bytes accessed | tf_op | source)
XLA Modules:
  0.0 107.3 jit_solution(8853896773733330744)
XLA Ops:
  0.0 0.8 copy.11
  0.8 0.0 copy-start
  0.8 1.0 copy-done
  1.8 1.0 copy-done.4
  2.8 0.9 copy-done.6
  3.7 0.8 copy-done.8
  4.5 0.9 first.1
  5.4 4.3 %collective-permute-start = (bf16[352,512]{1,0:T(8,128)(2,1)S(1)}, bf16[352,512]{1,0:T(8,128)(2,1)S(1)}, u32[]{:S(2)}, u32[]{:S(2)}) collective-permute-start(bf16[352,512]{1,0:T(8,128)(2,1)S(1)} %get-tuple-element.15), channel_id=1, source_target_pairs={{0,16},{16,32},{32,48},{48,64},{64,80},{80,96},{96,112},{112,128},... | collective-permute-start | bytes 1081352 | tf_op jit(solution)/shard_map/ppermute | solution.py:30
  9.7 8.6 %collective-permute-start.1 = (bf16[352,512]{1,0:T(8,128)(2,1)S(1)}, bf16[352,512]{1,0:T(8,128)(2,1)S(1)}, u32[]{:S(2)}, u32[]{:S(2)}) collective-permute-start(bf16[352,512]{1,0:T(8,128)(2,1)S(1)} %get-tuple-element.16), channel_id=1, source_target_pairs={{16,0},{32,16},{48,32},{64,48},{80,64},{96,80},{112,96},{128,112},... | collective-permute-start | bytes 1081352 | tf_op jit(solution)/shard_map/ppermute | solution.py:30
  18.3 1.9 %collective-permute-start.2 = (bf16[2,32,128]{2,1,0:T(8,128)(2,1)S(1)}, bf16[2,32,128]{2,1,0:T(8,128)(2,1)S(1)}, u32[]{:S(2)}, u32[]{:S(2)}) collective-permute-start(bf16[2,32,128]{2,1,0:T(8,128)(2,1)S(1)} %slice.68), channel_id=1, source_target_pairs={{0,16},{16,0},{32,48},{48,32},{64,80},{80,64},{96,112},{112,96},{1... | collective-permute-start | bytes 49160 | tf_op jit(solution)/shard_map/ppermute | solution.py:34
  20.2 5.0 %inner0.1.inner_top = f32[4,64,512]{2,1,0:T(8,128)S(1)} custom-call(s32[8,8]{1,0:T(8,128)S(1)} %bitcast.51, bf16[8,64,512]{2,1,0:T(8,128)(2,1)S(1)} %bitcast.34, bf16[8,3,512]{2,1,0:T(4,128)(2,1)S(1)} %bitcast.38), custom_call_target="tpu_custom_call" | custom-call | flops 6000000000 | bytes 4194304 | tf_op jit(solution)/shard_map/inner0/pallas_call | solution.py:38
  25.3 0.0 collective-permute-done.2
  25.3 0.0 copy-start.11
  25.3 0.0 copy-start.10
  25.3 0.0 copy-start.1
  25.3 2.1 %collective-permute-start.3 = (bf16[2,32,128]{2,1,0:T(8,128)(2,1)S(1)}, bf16[2,32,128]{2,1,0:T(8,128)(2,1)S(1)}, u32[]{:S(2)}, u32[]{:S(2)}) collective-permute-start(bf16[2,32,128]{2,1,0:T(8,128)(2,1)S(1)} %fusion), channel_id=1, source_target_pairs={{0,1},{1,0},{2,3},{3,2},{4,5},{5,4},{6,7},{7,6},{8,9},{9,8},{10,11... | collective-permute-start | bytes 49160 | tf_op jit(solution)/shard_map/ppermute | solution.py:34
  27.4 6.6 %inner1.1.inner_bottom = f32[4,64,512]{2,1,0:T(8,128)S(1)} custom-call(s32[8,8]{1,0:T(8,128)S(1)} %bitcast.52, bf16[8,64,512]{2,1,0:T(8,128)(2,1)S(1)} %bitcast.35, bf16[8,3,512]{2,1,0:T(4,128)(2,1)S(1)} %bitcast.39), custom_call_target="tpu_custom_call" | custom-call | flops 6000000000 | bytes 4194304 | tf_op jit(solution)/shard_map/inner1/pallas_call | solution.py:38
  34.1 0.0 collective-permute-done.3
  34.1 2.9 %collective-permute-start.4 = (bf16[3,32,128]{2,1,0:T(8,128)(2,1)S(1)}, bf16[3,32,128]{2,1,0:T(8,128)(2,1)S(1)}, u32[]{:S(2)}, u32[]{:S(2)}) collective-permute-start(bf16[3,32,128]{2,1,0:T(8,128)(2,1)S(1)} %pad_maximum_fusion), channel_id=1, source_target_pairs={{0,32},{16,48},{32,64},{48,80},{64,96},{80,112},{96,128},{112,144}... | collective-permute-start | bytes 73736 | tf_op jit(solution)/shard_map/ppermute | solution.py:30
  37.0 5.9 %collective-permute-start.5 = (bf16[3,32,128]{2,1,0:T(8,128)(2,1)S(1)}, bf16[3,32,128]{2,1,0:T(8,128)(2,1)S(1)}, u32[]{:S(2)}, u32[]{:S(2)}) collective-permute-start(bf16[3,32,128]{2,1,0:T(8,128)(2,1)S(1)} %pad_maximum_fusion), channel_id=1, source_target_pairs={{32,0},{48,16},{64,32},{80,48},{96,64},{112,80},{128,96},{144,112}... | collective-permute-start | bytes 73736 | tf_op jit(solution)/shard_map/ppermute | solution.py:30
  43.1 1.4 %collective-permute-done.5 = bf16[3,32,128]{2,1,0:T(8,128)(2,1)S(1)} collective-permute-done((bf16[3,32,128]{2,1,0:T(8,128)(2,1)S(1)}, bf16[3,32,128]{2,1,0:T(8,128)(2,1)S(1)}, u32[]{:S(2)}, u32[]{:S(2)}) %collective-permute-start.5) | collective-permute-done | bytes 24608 | tf_op jit(solution)/shard_map/ppermute | solution.py:30
  44.5 2.3 %collective-permute-start.10 = (bf16[32,128]{1,0:T(8,128)(2,1)S(1)}, bf16[32,128]{1,0:T(8,128)(2,1)S(1)}, u32[]{:S(2)}, u32[]{:S(2)}) collective-permute-start(bf16[32,128]{1,0:T(8,128)(2,1)S(1)} %bitcast.55), channel_id=1, source_target_pairs={{0,128},{16,144},{32,160},{48,176},{64,192},{80,208},{96,224},{112... | collective-permute-start | bytes 24584 | tf_op jit(solution)/shard_map/ppermute | solution.py:30
  46.8 6.4 %collective-permute-start.8 = (bf16[2,32,128]{2,1,0:T(8,128)(2,1)S(1)}, bf16[2,32,128]{2,1,0:T(8,128)(2,1)S(1)}, u32[]{:S(2)}, u32[]{:S(2)}) collective-permute-start(bf16[2,32,128]{2,1,0:T(8,128)(2,1)S(1)} %pad_maximum_fusion.1), channel_id=1, source_target_pairs={{0,64},{16,80},{32,96},{48,112},{64,128},{80,144},{96,160},{112,17... | collective-permute-start | bytes 49160 | tf_op jit(solution)/shard_map/ppermute | solution.py:30
  53.3 4.2 %collective-permute-start.9 = (bf16[2,32,128]{2,1,0:T(8,128)(2,1)S(1)}, bf16[2,32,128]{2,1,0:T(8,128)(2,1)S(1)}, u32[]{:S(2)}, u32[]{:S(2)}) collective-permute-start(bf16[2,32,128]{2,1,0:T(8,128)(2,1)S(1)} %pad_maximum_fusion.1), channel_id=1, source_target_pairs={{64,0},{80,16},{96,32},{112,48},{128,64},{144,80},{160,96},{176,11... | collective-permute-start | bytes 49160 | tf_op jit(solution)/shard_map/ppermute | solution.py:30
  57.5 3.5 %collective-permute-start.11 = (bf16[32,128]{1,0:T(8,128)(2,1)S(1)}, bf16[32,128]{1,0:T(8,128)(2,1)S(1)}, u32[]{:S(2)}, u32[]{:S(2)}) collective-permute-start(bf16[32,128]{1,0:T(8,128)(2,1)S(1)} %bitcast.56), channel_id=1, source_target_pairs={{128,0},{144,16},{160,32},{176,48},{192,64},{208,80},{224,96},{240... | collective-permute-start | bytes 24584 | tf_op jit(solution)/shard_map/ppermute | solution.py:30
  61.3 1.5 %collective-permute-done.9 = bf16[2,32,128]{2,1,0:T(8,128)(2,1)S(1)} collective-permute-done((bf16[2,32,128]{2,1,0:T(8,128)(2,1)S(1)}, bf16[2,32,128]{2,1,0:T(8,128)(2,1)S(1)}, u32[]{:S(2)}, u32[]{:S(2)}) %collective-permute-start.9) | collective-permute-done | bytes 16416 | tf_op jit(solution)/shard_map/ppermute | solution.py:30
  62.8 0.2 collective-permute-done.11
  63.1 4.2 %collective-permute-start.12 = (bf16[15,32,128]{2,1,0:T(8,128)(2,1)S(1)}, bf16[15,32,128]{2,1,0:T(8,128)(2,1)S(1)}, u32[]{:S(2)}, u32[]{:S(2)}) collective-permute-start(bf16[15,32,128]{2,1,0:T(8,128)(2,1)S(1)} %get-tuple-element.49), channel_id=1, source_target_pairs={{0,2},{1,3},{2,4},{3,5},{4,6},{5,7},{6,8},{7,9},{8,10},{9,11},{10,... | collective-permute-start | bytes 368648 | tf_op jit(solution)/shard_map/ppermute | solution.py:30
  67.2 1.3 %collective-permute-start.13 = (bf16[15,32,128]{2,1,0:T(8,128)(2,1)S(1)}, bf16[15,32,128]{2,1,0:T(8,128)(2,1)S(1)}, u32[]{:S(2)}, u32[]{:S(2)}) collective-permute-start(bf16[15,32,128]{2,1,0:T(8,128)(2,1)S(1)} %get-tuple-element.49), channel_id=1, source_target_pairs={{2,0},{3,1},{4,2},{5,3},{6,4},{7,5},{8,6},{9,7},{10,8},{11,9},{12,... | collective-permute-start | bytes 368648 | tf_op jit(solution)/shard_map/ppermute | solution.py:30
  68.6 0.1 pack.1
  68.7 1.3 %collective-permute-start.6 = (bf16[416,512]{1,0:T(8,128)(2,1)S(1)}, bf16[416,512]{1,0:T(8,128)(2,1)S(1)}, u32[]{:S(2)}, u32[]{:S(2)}) collective-permute-start(bf16[416,512]{1,0:T(8,128)(2,1)S(1)} %get-tuple-element.18), channel_id=1, source_target_pairs={{0,1},{1,2},{2,3},{3,4},{4,5},{5,6},{6,7},{7,8},{8,9},{9,10},{10,1... | collective-permute-start | bytes 1277960 | tf_op jit(solution)/shard_map/ppermute | solution.py:30
  70.0 0.0 copy-start.2
  70.0 0.0 copy-start.3
  70.0 1.4 %collective-permute-start.7 = (bf16[416,512]{1,0:T(8,128)(2,1)S(1)}, bf16[416,512]{1,0:T(8,128)(2,1)S(1)}, u32[]{:S(2)}, u32[]{:S(2)}) collective-permute-start(bf16[416,512]{1,0:T(8,128)(2,1)S(1)} %get-tuple-element.19), channel_id=1, source_target_pairs={{1,0},{2,1},{3,2},{4,3},{5,4},{6,5},{7,6},{8,7},{9,8},{10,9},{11,1... | collective-permute-start | bytes 1277960 | tf_op jit(solution)/shard_map/ppermute | solution.py:30
  71.4 6.3 %byrows.1.by_rows = f32[8,64,512]{2,1,0:T(8,128)S(1)} custom-call(s32[8,8]{1,0:T(8,128)S(1)} %bitcast.53, bf16[8,3,512]{2,1,0:T(4,128)(2,1)S(1)} %bitcast.41, bf16[352,512]{1,0:T(8,128)(2,1)S(1)} %collective-permute-done.top, bf16[352,512]{1,0:T(8,128)(2,1)S(1)} %collective-permute-done.1.bottom), custom_call_target="tpu_custom_call" | custom-call | flops 6000000000 | bytes 4194304 | tf_op jit(solution)/shard_map/byrows/pallas_call | solution.py:38
  77.7 0.0 collective-permute-done.12.far_left.box2_left
  77.7 0.0 collective-permute-done.13.far_right.box2_right
  77.8 9.1 %collective-permute-start.14 = (bf16[10,32,128]{2,1,0:T(8,128)(2,1)S(1)}, bf16[10,32,128]{2,1,0:T(8,128)(2,1)S(1)}, u32[]{:S(2)}, u32[]{:S(2)}) collective-permute-start(bf16[10,32,128]{2,1,0:T(8,128)(2,1)S(1)} %get-tuple-element.23), channel_id=1, source_target_pairs={{0,4},{1,5},{2,6},{3,7},{4,8},{5,9},{6,10},{7,11},{8,12},{9,13},{1... | collective-permute-start | bytes 245768 | tf_op jit(solution)/shard_map/ppermute | solution.py:30
  86.8 1.3 %collective-permute-start.15 = (bf16[10,32,128]{2,1,0:T(8,128)(2,1)S(1)}, bf16[10,32,128]{2,1,0:T(8,128)(2,1)S(1)}, u32[]{:S(2)}, u32[]{:S(2)}) collective-permute-start(bf16[10,32,128]{2,1,0:T(8,128)(2,1)S(1)} %get-tuple-element.23), channel_id=1, source_target_pairs={{4,0},{5,1},{6,2},{7,3},{8,4},{9,5},{10,6},{11,7},{12,8},{13,9},{1... | collective-permute-start | bytes 245768 | tf_op jit(solution)/shard_map/ppermute | solution.py:30
  88.1 11.3 %collective-permute-start.16 = (bf16[5,32,128]{2,1,0:T(8,128)(2,1)S(1)}, bf16[5,32,128]{2,1,0:T(8,128)(2,1)S(1)}, u32[]{:S(2)}, u32[]{:S(2)}) collective-permute-start(bf16[5,32,128]{2,1,0:T(8,128)(2,1)S(1)} %get-tuple-element.24.box3), channel_id=1, source_target_pairs={{0,8},{1,9},{2,10},{3,11},{4,12},{5,13},{6,14},{7,15},{8,0},{9,1},... | collective-permute-start | bytes 122888 | tf_op jit(solution)/shard_map/ppermute | solution.py:34
  99.4 0.0 collective-permute-done.6.left
  99.5 0.0 collective-permute-done.7.right
  99.5 0.0 copy-start.5
  99.5 0.0 copy-start.7
  99.5 4.8 %edge.1 = (f32[8,64,512]{2,1,0:T(8,128)S(1)}, f32[8,64,64]{2,1,0:T(8,128)S(1)}, f32[64,64]{1,0:T(8,128)S(1)}) custom-call(s32[8,8]{1,0:T(8,128)S(1)} %bitcast.54, bf16[8,3,512]{2,1,0:T(4,128)(2,1)S(1)} %bitcast.42, bf16[416,512]{1,0:T(8,128)(2,1)S(1)} %collective-permute-done.6.left, bf16[416,512]{1,0:T(8,128)(2,1)S(1)} %collective-permute-done.7.right, ...), custom_call_target="tpu_custom_call" | custom-call | flops 6000000000 | bytes 4194304 | tf_op jit(solution)/shard_map/edge/pallas_call | solution.py:38
  104.3 0.0 collective-permute-done.14.box4_left
  104.4 0.0 collective-permute-done.15.box4_right
  104.4 3.0 %last.1 = bf16[8,64,512]{2,1,0:T(8,128)(2,1)} custom-call(f32[8,64,512]{2,1,0:T(8,128)S(1)} %get-tuple-element.20.near, f32[8,64,64]{2,1,0:T(8,128)S(1)} %get-tuple-element.21.leaf_local, f32[64,64]{1,0:T(8,128)S(1)} %get-tuple-element.22.box_one, bf16[16,32]{1,0:T(8,128)(2,1)S(1)} %fusion.6.flags, bf16[3,64,1600]{2,1,0:T(8,128)(2,1)S(1)} %bitcast.45, ...), custom_call_target="tpu_custom_call" | custom-call | flops 1000000000 | bytes 4194304 | tf_op jit(solution)/shard_map/last/pallas_call | solution.py:38
  (51 shorter events, 0.3 us)
Async XLA Ops:
  0.8 1.0 copy-start
  1.8 1.0 copy-start.4
  2.8 0.9 copy-start.6
  3.7 0.8 copy-start.8
  4.5 15.7 %copy-start.9 = (s32[2,4,8]{2,1,0:T(4,128)S(1)}, s32[2,4,8]{2,1,0:T(4,128)}, u32[]{:S(2)}) copy-start(s32[2,4,8]{2,1,0:T(4,128)} %param.13) | copy-start | bytes 772
  5.4 55.7 %collective-permute-start = (bf16[352,512]{1,0:T(8,128)(2,1)S(1)}, bf16[352,512]{1,0:T(8,128)(2,1)S(1)}, u32[]{:S(2)}, u32[]{:S(2)}) collective-permute-start(bf16[352,512]{1,0:T(8,128)(2,1)S(1)} %get-tuple-element.15), channel_id=1, source_target_pairs={{0,16},{16,32},{32,48},{48,64},{64,80},{80,96},{96,112},{112,128},... | collective-permute-start | bytes 1081352 | tf_op jit(solution)/shard_map/ppermute | solution.py:30
  9.7 51.5 %collective-permute-start.1 = (bf16[352,512]{1,0:T(8,128)(2,1)S(1)}, bf16[352,512]{1,0:T(8,128)(2,1)S(1)}, u32[]{:S(2)}, u32[]{:S(2)}) collective-permute-start(bf16[352,512]{1,0:T(8,128)(2,1)S(1)} %get-tuple-element.16), channel_id=1, source_target_pairs={{16,0},{32,16},{48,32},{64,48},{80,64},{96,80},{112,96},{128,112},... | collective-permute-start | bytes 1081352 | tf_op jit(solution)/shard_map/ppermute | solution.py:30
  18.3 7.0 %collective-permute-start.2 = (bf16[2,32,128]{2,1,0:T(8,128)(2,1)S(1)}, bf16[2,32,128]{2,1,0:T(8,128)(2,1)S(1)}, u32[]{:S(2)}, u32[]{:S(2)}) collective-permute-start(bf16[2,32,128]{2,1,0:T(8,128)(2,1)S(1)} %slice.68), channel_id=1, source_target_pairs={{0,16},{16,0},{32,48},{48,32},{64,80},{80,64},{96,112},{112,96},{1... | collective-permute-start | bytes 49160 | tf_op jit(solution)/shard_map/ppermute | solution.py:34
  25.3 8.7 %copy-start.11 = (s32[1,1,3,25]{3,1,2,0:T(1,128)S(1)}, s32[1,1,3,25]{3,1,2,0:T(1,128)}, u32[]{:S(2)}) copy-start(s32[1,1,3,25]{3,1,2,0:T(1,128)} %param.18) | copy-start | bytes 904
  25.3 8.7 %copy-start.10 = (s32[2,4,25]{2,1,0:T(4,128)S(1)}, s32[2,4,25]{2,1,0:T(4,128)}, u32[]{:S(2)}) copy-start(s32[2,4,25]{2,1,0:T(4,128)} %param.15) | copy-start | bytes 2404
  25.3 43.2 %copy-start.1 = (bf16[2,4,64,512]{3,2,1,0:T(8,128)(2,1)S(1)}, bf16[2,4,64,512]{3,2,1,0:T(8,128)(2,1)}, u32[]{:S(2)}) copy-start(bf16[2,4,64,512]{3,2,1,0:T(8,128)(2,1)} %param.10) | copy-start | bytes 1572868
  25.3 8.7 %collective-permute-start.3 = (bf16[2,32,128]{2,1,0:T(8,128)(2,1)S(1)}, bf16[2,32,128]{2,1,0:T(8,128)(2,1)S(1)}, u32[]{:S(2)}, u32[]{:S(2)}) collective-permute-start(bf16[2,32,128]{2,1,0:T(8,128)(2,1)S(1)} %fusion), channel_id=1, source_target_pairs={{0,1},{1,0},{2,3},{3,2},{4,5},{5,4},{6,7},{7,6},{8,9},{9,8},{10,11... | collective-permute-start | bytes 49160 | tf_op jit(solution)/shard_map/ppermute | solution.py:34
  34.1 9.0 %collective-permute-start.4 = (bf16[3,32,128]{2,1,0:T(8,128)(2,1)S(1)}, bf16[3,32,128]{2,1,0:T(8,128)(2,1)S(1)}, u32[]{:S(2)}, u32[]{:S(2)}) collective-permute-start(bf16[3,32,128]{2,1,0:T(8,128)(2,1)S(1)} %pad_maximum_fusion), channel_id=1, source_target_pairs={{0,32},{16,48},{32,64},{48,80},{64,96},{80,112},{96,128},{112,144}... | collective-permute-start | bytes 73736 | tf_op jit(solution)/shard_map/ppermute | solution.py:30
  37.0 7.5 %collective-permute-start.5 = (bf16[3,32,128]{2,1,0:T(8,128)(2,1)S(1)}, bf16[3,32,128]{2,1,0:T(8,128)(2,1)S(1)}, u32[]{:S(2)}, u32[]{:S(2)}) collective-permute-start(bf16[3,32,128]{2,1,0:T(8,128)(2,1)S(1)} %pad_maximum_fusion), channel_id=1, source_target_pairs={{32,0},{48,16},{64,32},{80,48},{96,64},{112,80},{128,96},{144,112}... | collective-permute-start | bytes 73736 | tf_op jit(solution)/shard_map/ppermute | solution.py:30
  44.5 13.0 %collective-permute-start.10 = (bf16[32,128]{1,0:T(8,128)(2,1)S(1)}, bf16[32,128]{1,0:T(8,128)(2,1)S(1)}, u32[]{:S(2)}, u32[]{:S(2)}) collective-permute-start(bf16[32,128]{1,0:T(8,128)(2,1)S(1)} %bitcast.55), channel_id=1, source_target_pairs={{0,128},{16,144},{32,160},{48,176},{64,192},{80,208},{96,224},{112... | collective-permute-start | bytes 24584 | tf_op jit(solution)/shard_map/ppermute | solution.py:30
  46.8 14.2 %collective-permute-start.8 = (bf16[2,32,128]{2,1,0:T(8,128)(2,1)S(1)}, bf16[2,32,128]{2,1,0:T(8,128)(2,1)S(1)}, u32[]{:S(2)}, u32[]{:S(2)}) collective-permute-start(bf16[2,32,128]{2,1,0:T(8,128)(2,1)S(1)} %pad_maximum_fusion.1), channel_id=1, source_target_pairs={{0,64},{16,80},{32,96},{48,112},{64,128},{80,144},{96,160},{112,17... | collective-permute-start | bytes 49160 | tf_op jit(solution)/shard_map/ppermute | solution.py:30
  53.3 9.5 %collective-permute-start.9 = (bf16[2,32,128]{2,1,0:T(8,128)(2,1)S(1)}, bf16[2,32,128]{2,1,0:T(8,128)(2,1)S(1)}, u32[]{:S(2)}, u32[]{:S(2)}) collective-permute-start(bf16[2,32,128]{2,1,0:T(8,128)(2,1)S(1)} %pad_maximum_fusion.1), channel_id=1, source_target_pairs={{64,0},{80,16},{96,32},{112,48},{128,64},{144,80},{160,96},{176,11... | collective-permute-start | bytes 49160 | tf_op jit(solution)/shard_map/ppermute | solution.py:30
  57.5 5.5 %collective-permute-start.11 = (bf16[32,128]{1,0:T(8,128)(2,1)S(1)}, bf16[32,128]{1,0:T(8,128)(2,1)S(1)}, u32[]{:S(2)}, u32[]{:S(2)}) collective-permute-start(bf16[32,128]{1,0:T(8,128)(2,1)S(1)} %bitcast.56), channel_id=1, source_target_pairs={{128,0},{144,16},{160,32},{176,48},{192,64},{208,80},{224,96},{240... | collective-permute-start | bytes 24584 | tf_op jit(solution)/shard_map/ppermute | solution.py:30
  63.1 14.7 %collective-permute-start.12 = (bf16[15,32,128]{2,1,0:T(8,128)(2,1)S(1)}, bf16[15,32,128]{2,1,0:T(8,128)(2,1)S(1)}, u32[]{:S(2)}, u32[]{:S(2)}) collective-permute-start(bf16[15,32,128]{2,1,0:T(8,128)(2,1)S(1)} %get-tuple-element.49), channel_id=1, source_target_pairs={{0,2},{1,3},{2,4},{3,5},{4,6},{5,7},{6,8},{7,9},{8,10},{9,11},{10,... | collective-permute-start | bytes 368648 | tf_op jit(solution)/shard_map/ppermute | solution.py:30
  67.2 10.5 %collective-permute-start.13 = (bf16[15,32,128]{2,1,0:T(8,128)(2,1)S(1)}, bf16[15,32,128]{2,1,0:T(8,128)(2,1)S(1)}, u32[]{:S(2)}, u32[]{:S(2)}) collective-permute-start(bf16[15,32,128]{2,1,0:T(8,128)(2,1)S(1)} %get-tuple-element.49), channel_id=1, source_target_pairs={{2,0},{3,1},{4,2},{5,3},{6,4},{7,5},{8,6},{9,7},{10,8},{11,9},{12,... | collective-permute-start | bytes 368648 | tf_op jit(solution)/shard_map/ppermute | solution.py:30
  68.7 30.8 %collective-permute-start.6 = (bf16[416,512]{1,0:T(8,128)(2,1)S(1)}, bf16[416,512]{1,0:T(8,128)(2,1)S(1)}, u32[]{:S(2)}, u32[]{:S(2)}) collective-permute-start(bf16[416,512]{1,0:T(8,128)(2,1)S(1)} %get-tuple-element.18), channel_id=1, source_target_pairs={{0,1},{1,2},{2,3},{3,4},{4,5},{5,6},{6,7},{7,8},{8,9},{9,10},{10,1... | collective-permute-start | bytes 1277960 | tf_op jit(solution)/shard_map/ppermute | solution.py:30
  70.0 29.5 %copy-start.2 = (bf16[2,4,64,1600]{3,2,1,0:T(8,128)(2,1)S(1)}, bf16[2,4,64,1600]{3,2,1,0:T(8,128)(2,1)}, u32[]{:S(2)}) copy-start(bf16[2,4,64,1600]{3,2,1,0:T(8,128)(2,1)} %param.14) | copy-start | bytes 4915204
  70.0 29.5 %copy-start.3 = (bf16[1,1,3,64,1600]{4,3,2,1,0:T(8,128)(2,1)S(1)}, bf16[1,1,3,64,1600]{4,3,2,1,0:T(8,128)(2,1)}, u32[]{:S(2)}) copy-start(bf16[1,1,3,64,1600]{4,3,2,1,0:T(8,128)(2,1)} %param.17) | copy-start | bytes 1843204
  70.0 29.4 %collective-permute-start.7 = (bf16[416,512]{1,0:T(8,128)(2,1)S(1)}, bf16[416,512]{1,0:T(8,128)(2,1)S(1)}, u32[]{:S(2)}, u32[]{:S(2)}) collective-permute-start(bf16[416,512]{1,0:T(8,128)(2,1)S(1)} %get-tuple-element.19), channel_id=1, source_target_pairs={{1,0},{2,1},{3,2},{4,3},{5,4},{6,5},{7,6},{8,7},{9,8},{10,9},{11,1... | collective-permute-start | bytes 1277960 | tf_op jit(solution)/shard_map/ppermute | solution.py:30
  77.8 26.6 %collective-permute-start.14 = (bf16[10,32,128]{2,1,0:T(8,128)(2,1)S(1)}, bf16[10,32,128]{2,1,0:T(8,128)(2,1)S(1)}, u32[]{:S(2)}, u32[]{:S(2)}) collective-permute-start(bf16[10,32,128]{2,1,0:T(8,128)(2,1)S(1)} %get-tuple-element.23), channel_id=1, source_target_pairs={{0,4},{1,5},{2,6},{3,7},{4,8},{5,9},{6,10},{7,11},{8,12},{9,13},{1... | collective-permute-start | bytes 245768 | tf_op jit(solution)/shard_map/ppermute | solution.py:30
  86.8 17.5 %collective-permute-start.15 = (bf16[10,32,128]{2,1,0:T(8,128)(2,1)S(1)}, bf16[10,32,128]{2,1,0:T(8,128)(2,1)S(1)}, u32[]{:S(2)}, u32[]{:S(2)}) collective-permute-start(bf16[10,32,128]{2,1,0:T(8,128)(2,1)S(1)} %get-tuple-element.23), channel_id=1, source_target_pairs={{4,0},{5,1},{6,2},{7,3},{8,4},{9,5},{10,6},{11,7},{12,8},{13,9},{1... | collective-permute-start | bytes 245768 | tf_op jit(solution)/shard_map/ppermute | solution.py:30
  88.1 16.2 %collective-permute-start.16 = (bf16[5,32,128]{2,1,0:T(8,128)(2,1)S(1)}, bf16[5,32,128]{2,1,0:T(8,128)(2,1)S(1)}, u32[]{:S(2)}, u32[]{:S(2)}) collective-permute-start(bf16[5,32,128]{2,1,0:T(8,128)(2,1)S(1)} %get-tuple-element.24.box3), channel_id=1, source_target_pairs={{0,8},{1,9},{2,10},{3,11},{4,12},{5,13},{6,14},{7,15},{8,0},{9,1},... | collective-permute-start | bytes 122888 | tf_op jit(solution)/shard_map/ppermute | solution.py:34
  99.5 4.9 %copy-start.5 = (bf16[2,4,64,512]{3,2,1,0:T(8,128)(2,1)S(1)}, bf16[2,4,64,512]{3,2,1,0:T(8,128)(2,1)}, u32[]{:S(2)}) copy-start(bf16[2,4,64,512]{3,2,1,0:T(8,128)(2,1)} %param.12) | copy-start | bytes 1572868
  99.5 4.9 %copy-start.7 = (bf16[2,4,64,64]{3,2,1,0:T(8,128)(2,1)S(1)}, bf16[2,4,64,64]{3,2,1,0:T(8,128)(2,1)}, u32[]{:S(2)}) copy-start(bf16[2,4,64,64]{3,2,1,0:T(8,128)(2,1)} %param.16) | copy-start | bytes 196612

commit v2 on v1

v2 whole, which is shorter than its diff:
```python
import functools

import jax
import jax.numpy as jnp
from jax import lax
from jax.experimental import pallas as pl
from jax.experimental.pallas import tpu as pltpu
from jax.sharding import PartitionSpec as P

PANELS = 512
RANK = 64
LOADS = 64
EPSILON = 0.001
F32 = jnp.float32
BF16 = jnp.bfloat16
NT = (((1,), (1,)), ((), ()))
TN = (((0,), (0,)), ((), ()))
WIDE = 25 * RANK
MIB = 2**20
VMEM = pl.BlockSpec(memory_space=pltpu.VMEM)
SMEM = pl.BlockSpec(memory_space=pltpu.SMEM)
HBM = pl.BlockSpec(memory_space=pltpu.HBM)

ROW_OFFS, ROW_POLES, ROW_ALL = 256, 272, 336
COL_OFFS, COL_POLES, COL_BOX, COL_ALL = 256, 272, 368, 416
SUMS = 80


def paired(value, axis, distance):
    return lax.ppermute(value, axis, [(i, i ^ distance) for i in range(lax.axis_size(axis))])


def paired_across(value, axis, distance):
    count = lax.axis_size(axis)
    moves = [(i, i + distance if i & distance else i - distance) for i in range(count)]
    return lax.ppermute(value, axis, [(i, j) for i, j in moves if 0 <= j < count])


def kernel_call(body, outs, scratch, name, cost, *args, smem=(), hbm=(), after=(), limit=40):
    count = len(args)

    def with_order(*refs):
        body(*refs[:count], *refs[count + len(after) :])

    spaces = [SMEM if i in smem else HBM if i in hbm else VMEM for i in range(count)]
    return pl.pallas_call(
        with_order,
        out_shape=outs,
        in_specs=spaces + [VMEM] * len(after),
        out_specs=jax.tree.map(lambda _: VMEM, outs),
        scratch_shapes=scratch,
        compiler_params=pltpu.CompilerParams(vmem_limit_bytes=limit * MIB),
        cost_estimate=pl.CostEstimate(flops=cost, bytes_accessed=4 * MIB, transcendentals=0),
        name=name,
    )(*[pltpu.with_memory_space_constraint(arg, pltpu.HBM) if i in hbm else arg for i, arg in enumerate(args)], *after)


def shape(dims, dtype=BF16):
    return jax.ShapeDtypeStruct(dims, dtype)


def fold(matrix):
    return jnp.concatenate([matrix[:32], matrix[32:]], axis=1)


def unfold(folded):
    return jnp.concatenate([folded[:, :64], folded[:, 64:]], axis=0)


def place_bits():
    row, col = lax.axis_index("row"), lax.axis_index("col")
    return [value & 1 for value in (row, col, row >> 1, row >> 2, row >> 3, col >> 1, col >> 2, col >> 3)]


def flat(folded):
    return jnp.concatenate([folded[:16], folded[16:]], axis=1)


def unflat(flattened):
    return jnp.concatenate([flattened[:, :128], flattened[:, 128:]], axis=0)


def rows_of(values, count):
    row = lax.broadcasted_iota(jnp.int32, (count, PANELS), 0)
    out = jnp.zeros((count, PANELS), F32)
    for index, value in enumerate(values):
        out = jnp.where(row == index, value, out)
    return out


def three_parts(value):
    high = value.astype(BF16).astype(F32)
    rest = value - high
    middle = rest.astype(BF16).astype(F32)
    low = (rest - middle).astype(BF16).astype(F32)
    return high, middle, low


def target_features(off):
    x, y, z = off[0:1], off[1:2], off[2:3]
    high, middle, low = three_parts(PANELS * (x * x + y * y + z * z + EPSILON))
    return rows_of([x, y, z, x, y, high, middle, low, 1.0, 1.0, 1.0], 16).T.astype(BF16)


def source_features(off, row_off, col_off):
    x, y, z = off[0:1], off[1:2], off[2:3]
    x_moved, y_moved = x + col_off, y + row_off
    high, middle, low = three_parts(PANELS * (x_moved * x_moved + y_moved * y_moved + z * z))
    twice = -2.0 * PANELS
    return rows_of(
        [twice * x, twice * y, twice * z, twice * col_off, twice * row_off, 1.0, 1.0, 1.0, high, middle, low], 16
    ).astype(BF16)


def near_pairs(pairs, mask, listed, target_feats, source_offs, source_charges, acc):
    count = jnp.int32(0)
    for target, slot, source, row_off, col_off in pairs:
        listed[count] = target + 16 * source + 256 * (row_off + 1) + 1024 * (col_off + 1)
        count = count + (1 if slot is None else mask[target, slot])

    def one(index):
        code = listed[index]
        target = code & 15
        source = (code >> 4) & 15
        row_off = ((code >> 8) & 3) - 1
        col_off = ((code >> 10) & 3) - 1
        moved = source_features(source_offs[source, 0:3, :], row_off.astype(F32), col_off.astype(F32))
        squared = jnp.dot(target_feats[target], moved, preferred_element_type=F32)
        tile = lax.rsqrt(squared).astype(BF16)
        acc[target] += lax.dot_general(source_charges[source], tile, NT, preferred_element_type=F32)

    def several(step, carry):
        for k in range(4):
            one(4 * step + k)
        return carry

    def single(step, carry):
        one(step)
        return carry

    fours = count // 4
    lax.fori_loop(0, fours, several, 0)
    lax.fori_loop(4 * fours, count, single, 0)


def slot_of(row_off, col_off):
    place = 3 * (row_off + 1) + col_off + 1
    return None if place == 4 else place - (place > 4)


def inner_pairs(targets):
    found = []
    for target in targets:
        row, col = divmod(target, 4)
        for row_off in (-1, 0, 1):
            for col_off in (-1, 0, 1):
                at_row, at_col = row + row_off, col + col_off
                if 0 <= at_row < 2 and 0 <= at_col < 4:
                    found.append((target, slot_of(row_off, col_off), 4 * at_row + at_col, row_off, col_off))
    return found


def row_pairs():
    found = []
    for row, row_off in ((0, -1), (1, 1)):
        for col in range(4):
            for col_off in (-1, 0, 1):
                if 0 <= col + col_off < 4:
                    found.append((4 * row + col, slot_of(row_off, col_off), 4 * row + col + col_off, row_off, col_off))
    return found


def col_pairs():
    found = []
    for side, col, col_off in ((0, 0, -1), (1, 3, 1)):
        for row in range(2):
            for row_off in (-1, 0, 1):
                found.append((4 * row + col, slot_of(row_off, col_off), 4 * side + row + row_off + 1, row_off, col_off))
    return found


def first_kernel(
    charges_hbm, offsets_hbm, basis_hbm, transfer_hbm, parent_hbm,
    with_pair, across, small, poles_out,
    charges, offsets, basis, transfer, parent, sems,
):
    side = place_bits()[0]
    loads = []
    for k in range(4):
        rows = pl.ds(2 * k, 2)
        loads.append(pltpu.make_async_copy(charges_hbm.at[rows], charges.at[rows], sems.at[k]))
        loads.append(pltpu.make_async_copy(basis_hbm.at[rows], basis.at[rows], sems.at[4 + k]))
    loads.append(pltpu.make_async_copy(transfer_hbm, transfer, sems.at[8]))
    loads.append(pltpu.make_async_copy(parent_hbm, parent, sems.at[9]))
    loads.append(pltpu.make_async_copy(offsets_hbm, offsets, sems.at[10]))
    for load in loads:
        load.start()
    loads[10].wait()
    offs = [[offsets[row, k].astype(F32) for k in range(3)] for row in range(2)]
    halves = [rows_of([offs[row][k % 3][k // 3 : k // 3 + 1] for k in range(12)], 16).astype(BF16) for row in range(2)]
    with_pair[ROW_OFFS:ROW_POLES, :] = jnp.where(side == 0, halves[1], halves[0])
    across[ROW_OFFS:ROW_POLES, :] = jnp.where(side == 0, halves[0], halves[1])
    poles = []
    for k in range(4):
        loads[2 * k].wait()
        loads[2 * k + 1].wait()
        for leaf in (2 * k, 2 * k + 1):
            poles.append(lax.dot_general(basis[leaf], charges[leaf], NT, preferred_element_type=F32).astype(BF16))
    loads[8].wait()
    box = jnp.zeros((RANK, LOADS), F32)
    for leaf in range(8):
        box = box + lax.dot_general(transfer[leaf], poles[leaf], TN, preferred_element_type=F32)
    box = box.astype(BF16)
    small[0] = fold(box)
    loads[9].wait()
    for level in range(2):
        term = lax.dot_general(parent[level], box, TN, preferred_element_type=F32)
        small[1 + level] = fold(term.astype(BF16))
    pairs = [jnp.concatenate([poles[2 * k], poles[2 * k + 1]], axis=1) for k in range(4)]
    for k in range(4):
        poles_out[k] = pairs[k]
    for buffer, row in ((with_pair, 1 - side), (across, side)):
        for col in range(4):
            buffer[64 * col : 64 * (col + 1), :] = charges[4 * row + col]
        for k in range(4):
            buffer[ROW_POLES:ROW_ALL, 128 * k : 128 * (k + 1)] = pairs[k]


def own_offsets(offsets, offs):
    for row in range(2):
        for k in range(3):
            values = offsets[row, k].astype(F32)
            for col in range(4):
                offs[4 * row + col, k : k + 1, :] = values[col : col + 1]


def inner_kernel(targets, mask, charges, offsets, out, listed, feats, offs, acc):
    own_offsets(offsets, offs)
    for target in targets:
        feats[target] = target_features(offs[target, 0:3, :])
        acc[target] = jnp.zeros((LOADS, PANELS), F32)
    near_pairs(inner_pairs(targets), mask, listed, feats, offs, charges, acc)
    out[...] = acc[targets[0] : targets[-1] + 1]


def spread_offsets(packed, offs, base):
    values = packed.astype(F32)
    for leaf in range(4):
        offs[base + leaf, 0:3, :] = values[3 * leaf : 3 * leaf + 3]


def row_kernel(mask, offsets, paired_rows, across_rows, out, listed, feats, offs, charges, acc):
    place = place_bits()
    own_offsets(offsets, offs)
    for leaf in range(8):
        feats[leaf] = target_features(offs[leaf, 0:3, :])
    for side, buffer in ((1 - place[0], paired_rows), (place[0], across_rows)):
        spread_offsets(buffer[ROW_OFFS:ROW_POLES, :], offs, 4 * side)
        for col in range(4):
            charges[4 * side + col] = buffer[64 * col : 64 * (col + 1), :]
    acc[...] = jnp.zeros_like(acc)
    near_pairs(row_pairs(), mask, listed, feats, offs, charges, acc)
    out[...] = acc[...]


def pack_kernel(
    charges, offsets, poles, paired_rows, across_rows, small, pair1, pair2, pair4, pair8, across8,
    with_pair, across, boxes_out, sums_out,
):
    place = place_bits()
    bit0, bit1, bit2 = place[0], place[2], place[3]
    at = bit0 == 0
    minus8, plus8 = [[jnp.where(place[4] == want, pair8[k], across8[k]) for k in range(6)] for want in (1, 0)]
    low2, low4 = bit1 == 0, bit2 == 0
    minus2, plus2 = [], []
    for k in range(3):
        other = jnp.where(low2 != low4, pair4[2 + k], jnp.where(low2, minus8[3 + k], plus8[3 + k]))
        minus2.append(jnp.where(low2, other, pair2[k]))
        plus2.append(jnp.where(low2, pair2[k], other))
    boxes = [
        minus2[0],
        jnp.where(at, minus2[1], pair1[0]),
        small[0],
        jnp.where(at, pair1[0], plus2[1]),
        plus2[0],
    ]
    own2 = (small[1].astype(F32) + pair1[1].astype(F32)).astype(BF16)
    own3 = (small[2].astype(F32) + pair1[2].astype(F32) + pair2[3].astype(F32)).astype(BF16)
    second = [
        jnp.where(low4, minus8[2], pair4[0]),
        minus2[2],
        own2,
        plus2[2],
        jnp.where(low4, pair4[0], plus8[2]),
    ]
    third = [
        minus8[0],
        jnp.where(low4, minus8[1], pair4[1]),
        own3,
        jnp.where(low4, pair4[1], plus8[1]),
        plus8[0],
    ]
    for row in range(5):
        base, lane = 16 * (row // 2), 256 * (row % 2)
        piece = flat(boxes[row])
        boxes_out[base : base + 16, lane : lane + 256] = piece
        for buffer in (with_pair, across):
            buffer[COL_BOX + base : COL_BOX + base + 16, lane : lane + 256] = piece
        for half, found in enumerate((second, third)):
            piece = flat(found[row])
            sums_out[16 * row : 16 * row + 16, 256 * half : 256 * half + 256] = piece
            with_pair[COL_ALL + 16 * row : COL_ALL + 16 * row + 16, 256 * half : 256 * half + 256] = piece
    blank = jnp.zeros((16, 256), BF16)
    boxes_out[32:48, 256:512] = blank
    for buffer in (with_pair, across):
        buffer[COL_BOX + 32 : COL_ALL, 256:512] = blank

    def fill(buffer, col, top, bottom):
        pair = col // 2
        offs = []
        for spot, source in enumerate((top, None, None, bottom)):
            if source is None:
                leaf = 4 * (spot - 1) + col
                buffer[64 * spot : 64 * (spot + 1), :] = charges[leaf]
                offs += [offsets[spot - 1, k].astype(F32)[col : col + 1] for k in range(3)]
            else:
                buffer[64 * spot : 64 * (spot + 1), :] = source[64 * col : 64 * (col + 1), :]
                off = source[ROW_OFFS:ROW_POLES, :].astype(F32)[3 * col : 3 * col + 3]
                offs += [off[0:1], off[1:2], off[2:3]]
        buffer[COL_OFFS:COL_POLES, :] = rows_of(offs, 16).astype(BF16)
        for row in range(6):
            if row in (2, 3):
                pole = poles[2 * (row - 2) + pair]
            else:
                source = top if row < 2 else bottom
                start = 128 * (2 * (row % 4) + pair)
                pole = source[ROW_POLES:ROW_ALL, start : start + 128]
            base, lane = COL_POLES + 32 * (row // 2), 256 * (row % 2)
            buffer[base : base + 32, lane : lane + 128] = pole[:32]
            buffer[base : base + 32, lane + 128 : lane + 256] = pole[32:]

    for row_side in range(2):
        for col_side in range(2):

            @pl.when((place[0] == row_side) & (place[1] == col_side))
            def _():
                top, bottom = (across_rows, paired_rows) if row_side == 0 else (paired_rows, across_rows)
                fill(with_pair, 0 if col_side else 3, top, bottom)
                fill(across, 3 if col_side else 0, top, bottom)


def flag_row(flags):
    row = lax.broadcasted_iota(jnp.int32, (32, WIDE), 0)
    lane = lax.broadcasted_iota(jnp.int32, (32, WIDE), 1)
    spread = jnp.where((lane >> 6) == row, 1.0, 0.0).astype(BF16)
    return jnp.dot(flags, spread, preferred_element_type=F32).astype(BF16)


def box_product(coupling, flags, window):
    return jnp.dot(coupling * flags, window, preferred_element_type=F32)


def edge_kernel(
    mask, offsets, paired_cols, across_cols, inner0, inner1, by_rows, poles, paired_rows, across_rows, flags, coupling,
    out, leaf_out, listed, feats, offs, charges, acc, table,
):
    place = place_bits()
    own_offsets(offsets, offs)
    for leaf in (0, 3, 4, 7):
        feats[leaf] = target_features(offs[leaf, 0:3, :])
    for side, buffer in ((1 - place[1], paired_cols), (place[1], across_cols)):
        spread_offsets(buffer[COL_OFFS:COL_POLES, :], offs, 4 * side)
        for spot in range(4):
            charges[4 * side + spot] = buffer[64 * spot : 64 * (spot + 1), :]
    acc[0:3] = inner0[...] + by_rows[0:3]
    acc[3:6] = inner1[...] + by_rows[3:6]
    acc[6:8] = by_rows[6:8]
    near_pairs(col_pairs(), mask, listed, feats, offs, charges, acc)
    out[...] = acc[...]

    def put(row, pair, both):
        table[row, 128 * pair : 128 * pair + 64, :] = both[:, :64]
        table[row, 128 * pair + 64 : 128 * pair + 128, :] = both[:, 64:]

    for row in (2, 3):
        for pair in (1, 2):
            put(row, pair, poles[2 * (row - 2) + pair - 1])
    for side in range(2):

        @pl.when(place[0] == side)
        def _():
            for base, buffer in ((4 - 4 * side, paired_rows), (4 * side, across_rows)):
                for row in range(2):
                    for pair in (1, 2):
                        start = 128 * (2 * row + pair - 1)
                        put(base + row, pair, buffer[ROW_POLES:ROW_ALL, start : start + 128])

        @pl.when(place[1] == side)
        def _():
            for pair, buffer in ((3 - 3 * side, paired_cols), (3 * side, across_cols)):
                for row in range(6):
                    base, lane = COL_POLES + 32 * (row // 2), 256 * (row % 2)
                    put(row, pair, unflat(buffer[base : base + 32, lane : lane + 256]))

    spread = flag_row(flags[...])
    for row in range(2):
        for col in range(4):
            leaf = 4 * row + col
            seen = jnp.concatenate([table[row + a, 64 * col : 64 * (col + 5), :] for a in range(5)], axis=0)
            leaf_out[leaf] = box_product(coupling[leaf], spread[leaf : leaf + 1], seen)


def inner_box_kernel(
    targets, mask, charges, offsets, flags, box_coupling, boxes, paired_cols, across_cols, pair2, across2,
    out, box_out, listed, feats, offs, acc, window,
):
    inner_kernel(targets, mask, charges, offsets, out, listed, feats, offs, acc)
    place = place_bits()
    low1, low2 = place[1] == 0, place[5] == 0
    for row in range(5):
        base, lane = 16 * (row // 2), 256 * (row % 2)
        pair_1 = paired_cols[COL_BOX + base : COL_BOX + base + 16, lane : lane + 256]
        across_1 = across_cols[COL_BOX + base : COL_BOX + base + 16, lane : lane + 256]
        pair_2, across_2 = [ref[base : base + 16, lane : lane + 256] for ref in (pair2, across2)]
        found = (
            jnp.where(low2, across_2, pair_2),
            jnp.where(low1, across_1, pair_1),
            boxes[base : base + 16, lane : lane + 256],
            jnp.where(low1, pair_1, across_1),
            jnp.where(low2, pair_2, across_2),
        )
        for col in range(5):
            start = 64 * (5 * row + col)
            window[start : start + 64, :] = unfold(unflat(found[col]))
    box_out[...] = box_product(box_coupling[0], flag_row(flags[...])[8:9], window[...])


def last_kernel(
    near, inner2, leaf_local, box_one, flags, box_coupling, transfer, basis,
    sums, pair2, across2, boxes3, pair4, across4, pair8,
    out, window,
):
    place = place_bits()
    spread = flag_row(flags[...])
    total = box_one[...]
    low2, low4, low8 = place[5] == 0, place[6] == 0, place[7] == 0
    blank = jnp.zeros((16, 256), BF16)
    for level in range(2):
        lanes = slice(256 * level, 256 * level + 256)
        for row in range(5):
            rows = slice(16 * row, 16 * row + 16)
            later = slice(48 + 16 * row, 64 + 16 * row)
            pair_4, across_4 = pair4[rows, lanes], across4[rows, lanes]
            minus4, plus4 = jnp.where(low4, across_4, pair_4), jnp.where(low4, pair_4, across_4)
            if level == 0:
                pair_2, across_2 = pair2[later, lanes], across2[later, lanes]
                minus2, plus2 = jnp.where(low2, across_2, pair_2), jnp.where(low2, pair_2, across_2)
                found = (minus4, minus2, sums[rows, lanes], plus2, plus4)
            else:
                far = pair8[rows, :]
                found = (jnp.where(low8, blank, far), minus4, boxes3[rows, :], plus4, jnp.where(low8, far, blank))
            for col in range(5):
                start = 64 * (5 * row + col)
                window[start : start + 64, :] = unfold(unflat(found[col]))
        total = total + box_product(box_coupling[1 + level], spread[9 + level : 10 + level], window[...])
    total = total.astype(BF16)
    for leaf in range(8):
        local = leaf_local[leaf] + jnp.dot(transfer[leaf], total, preferred_element_type=F32)
        far = lax.dot_general(local.astype(BF16), basis[leaf], TN, preferred_element_type=F32)
        direct = near[leaf] + inner2[leaf - 6] if leaf >= 6 else near[leaf]
        out[leaf] = (direct + far).astype(BF16)


def near_scratch(sources):
    return [
        pltpu.SMEM((32,), jnp.int32),
        pltpu.VMEM((8, PANELS, 16), BF16),
        pltpu.VMEM((8, 8, PANELS), F32),
        *([pltpu.VMEM((8, LOADS, PANELS), BF16)] if sources else []),
        pltpu.VMEM((8, LOADS, PANELS), F32),
    ]


def body(
    charges,
    offsets,
    leaf_basis,
    near_mask,
    leaf_coupling,
    leaf_distant_flags,
    leaf_transfer,
    box_coupling,
    box_far,
    parent_child_transfer,
):
    charges = charges.reshape(8, LOADS, PANELS)
    offsets = offsets.transpose(0, 2, 1, 3)
    basis = leaf_basis.reshape(8, RANK, PANELS)
    mask = near_mask.reshape(8, 8)
    coupling = leaf_coupling.reshape(8, RANK, WIDE)
    transfer = leaf_transfer.reshape(8, RANK, RANK)
    box_coupling = box_coupling.reshape(3, RANK, WIDE)
    parent = parent_child_transfer.reshape(2, RANK, RANK)
    flags = jnp.concatenate([leaf_distant_flags.reshape(8, 25), box_far.reshape(3, 25)], axis=0)
    flags = jnp.pad(flags, ((0, 5), (0, 7))).astype(BF16)
    near_cost = 6 * 10**9
    rows_pair, rows_across, small, poles = kernel_call(
        first_kernel,
        (shape((ROW_ALL, 512)), shape((ROW_ALL, 512)), shape((3, 32, 128)), shape((4, 64, 128))),
        [
            pltpu.VMEM((8, LOADS, PANELS), BF16),
            pltpu.VMEM((2, 3, 4, PANELS), BF16),
            pltpu.VMEM((8, RANK, PANELS), BF16),
            pltpu.VMEM((8, RANK, RANK), BF16),
            pltpu.VMEM((2, RANK, RANK), BF16),
            pltpu.SemaphoreType.DMA((11,)),
        ],
        "first", 10**9, charges, offsets, basis, transfer, parent, hbm=(0, 1, 2, 3, 4),
    )

    pair1 = paired(small, "row", 1)
    paired_rows = paired(rows_pair, "row", 1)
    across_rows = paired_across(rows_across, "row", 1)
    halves = (small[1:3].astype(F32) + pair1[1:3].astype(F32)).astype(BF16)
    payload = jnp.concatenate([small[:1], pair1[:1], halves], axis=0)
    pair2 = paired(payload, "row", 2)
    inner0 = kernel_call(
        functools.partial(inner_kernel, (0, 1, 2)), shape((3, LOADS, PANELS), F32), near_scratch(False), "inner0",
        near_cost, mask, charges, offsets, smem=(0,), after=(payload,),
    )
    pair2, inner0 = lax.optimization_barrier((pair2, inner0))
    quarter = (small[2].astype(F32) + pair1[2].astype(F32) + pair2[3].astype(F32)).astype(BF16)
    payload = jnp.concatenate([halves[:1], quarter[None], pair2[:3]], axis=0)
    pair4 = paired(payload, "row", 4)
    inner1 = kernel_call(
        functools.partial(inner_kernel, (3, 4, 5)), shape((3, LOADS, PANELS), F32), near_scratch(False), "inner1",
        near_cost, mask, charges, offsets, smem=(0,), after=(payload,),
    )
    pair4, inner1 = lax.optimization_barrier((pair4, inner1))
    payload = jnp.concatenate([quarter[None], pair4[1:2], pair4[0:1], pair4[2:5]], axis=0)
    pair8, across8 = paired(payload, "row", 8), paired_across(payload, "row", 8)
    by_rows = kernel_call(
        row_kernel, shape((8, LOADS, PANELS), F32), near_scratch(True), "byrows", near_cost,
        mask, offsets, paired_rows, across_rows, smem=(0,), after=(payload,),
    )

    pair8, across8, by_rows = lax.optimization_barrier((pair8, across8, by_rows))

    cols_pair, cols_across, boxes1, row_sums = kernel_call(
        pack_kernel,
        (shape((COL_ALL + SUMS, 512)), shape((COL_ALL, 512)), shape((48, 512)), shape((SUMS, 512))),
        [], "pack", 10**8, charges, offsets, poles, paired_rows, across_rows,
        small, pair1, pair2, pair4, pair8, across8,
    )
    paired_cols = paired(cols_pair, "col", 1)
    across_cols = paired_across(cols_across, "col", 1)
    sums = (row_sums.astype(F32) + paired_cols[COL_ALL:].astype(F32)).astype(BF16)
    payload = jnp.concatenate([boxes1, sums], axis=0)
    col_pair2, col_across2 = paired(payload, "col", 2), paired_across(payload, "col", 2)
    near, leaf_local = kernel_call(
        edge_kernel,
        (shape((8, LOADS, PANELS), F32), shape((8, RANK, LOADS), F32)),
        near_scratch(True) + [pltpu.VMEM((6, 512, LOADS), BF16)], "edge", near_cost,
        mask, offsets, paired_cols, across_cols, inner0, inner1, by_rows, poles, paired_rows, across_rows,
        flags, coupling, smem=(0,), after=(payload,),
    )
    boxes3 = (sums[:, 256:].astype(F32) + col_pair2[48:, 256:].astype(F32)).astype(BF16)
    payload = jnp.concatenate([sums[:, :256], boxes3], axis=1)
    col_pair4, col_across4 = paired(payload, "col", 4), paired_across(payload, "col", 4)
    col_pair8 = paired(boxes3, "col", 8)
    inner2, box_one = kernel_call(
        functools.partial(inner_box_kernel, (6, 7)),
        (shape((2, LOADS, PANELS), F32), shape((RANK, LOADS), F32)),
        near_scratch(False) + [pltpu.VMEM((WIDE, LOADS), BF16)], "inner2", near_cost,
        mask, charges, offsets, flags, box_coupling, boxes1, paired_cols, across_cols, col_pair2, col_across2,
        smem=(0,), after=(payload,),
    )
    out = kernel_call(
        last_kernel, shape((8, LOADS, PANELS)), [pltpu.VMEM((WIDE, LOADS), BF16)], "last", 10**9,
        near, inner2, leaf_local, box_one, flags, box_coupling, transfer, basis,
        sums, col_pair2, col_across2, boxes3, col_pair4, col_across4, col_pair8,
    )
    return out.reshape(2, 4, LOADS, PANELS)


def solution(mesh):
    return jax.shard_map(
        body,
        mesh=mesh,
        in_specs=(
            P("row", "col", None, None),
            P("row", "col", None, None),
            P("row", "col", None, None),
            P("row", "col", None),
            P("row", "col", None, None),
            P("row", "col", None),
            P("row", "col", None, None),
            P("row", "col", None, None, None),
            P("row", "col", None, None),
            P("row", "col", None, None, None),
        ),
        out_specs=P("row", "col", None, None),
        check_vma=False,
    )
```

time: 108 us -> 87.3 us (0.81)
  the two profiles are of different devices: /device:TPU:4 before, /device:TPU:10 now
where the time goes in v2:
time: 87.3 us; the launch traced here: 86.8 us
  starting transfers between devices  54 us (62%)
  Pallas kernels  29.5 us (34%)
  waiting for transfers between devices  2.61 us (3%)
    ppermute x9, starting transfers between devices, paired(): lax.ppermute(value, axis, [(i, i ^ distance) for i in range(lax.axis_size...  32.2 us
    pallas_call x8, Pallas kernels, kernel_call(): pl.pallas_call(with_order, out_shape=outs, in_specs=spaces + [VMEM] * len...  29.5 us
    ppermute x5, starting transfers between devices, paired_across(): lax.ppermute(value, axis, [(i, j) for i, j in moves if 0 <= j < count])  21.8 us
    ppermute x5, waiting for transfers between devices, paired_across(): lax.ppermute(value, axis, [(i, j) for i, j in moves if 0 <= j < count])  2.49 us
  transfers between devices with their start and end apart: 14, of which 2 were waited for; matrix products, arithmetic and copies ran while one was open for 0% of the time, Pallas kernels for 27%

profile of v2, /device:TPU:10, one launch (start us, length us, event | category | flops | bytes accessed | tf_op | source)
XLA Modules:
  0.0 86.8 jit_solution(12072490753986923882)
XLA Ops:
  0.0 2.7 %first.1 = (bf16[336,512]{1,0:T(8,128)(2,1)S(1)}, bf16[336,512]{1,0:T(8,128)(2,1)S(1)}, bf16[3,32,128]{2,1,0:T(8,128)(2,1)S(1)}, bf16[4,64,128]{2,1,0:T(8,128)(2,1)S(1)}) custom-call(bf16[8,64,512]{2,1,0:T(8,128)(2,1)} %bitcast.15, bf16[2,3,4,512]{3,2,1,0:T(4,128)(2,1)} %bitcast.24, bf16[8,64,512]{2,1,0:T(8,128)(2,1)} %bitcast.20, ...), custom_call_target="tpu_custom_call" | custom-call | flops 1000000000 | bytes 4194304 | tf_op jit(solution)/shard_map/first/pallas_call | solution.py:46
  2.7 4.3 %collective-permute-start.2 = (bf16[3,32,128]{2,1,0:T(8,128)(2,1)S(1)}, bf16[3,32,128]{2,1,0:T(8,128)(2,1)S(1)}, u32[]{:S(2)}, u32[]{:S(2)}) collective-permute-start(bf16[3,32,128]{2,1,0:T(8,128)(2,1)S(1)} %get-tuple-element.27.refs_5_), channel_id=1, source_target_pairs={{0,16},{16,0},{32,48},{48,32},{64,80},{80,64},{96,112},{112,96},{1... | collective-permute-start | bytes 73736 | tf_op jit(solution)/shard_map/ppermute | solution.py:30
  7.0 1.9 %collective-permute-start = (bf16[336,512]{1,0:T(8,128)(2,1)S(1)}, bf16[336,512]{1,0:T(8,128)(2,1)S(1)}, u32[]{:S(2)}, u32[]{:S(2)}) collective-permute-start(bf16[336,512]{1,0:T(8,128)(2,1)S(1)} %get-tuple-element.25), channel_id=1, source_target_pairs={{0,16},{16,0},{32,48},{48,32},{64,80},{80,64},{96,112},{112,96},{1... | collective-permute-start | bytes 1032200 | tf_op jit(solution)/shard_map/ppermute | solution.py:30
  9.0 10.6 %collective-permute-start.1 = (bf16[336,512]{1,0:T(8,128)(2,1)S(1)}, bf16[336,512]{1,0:T(8,128)(2,1)S(1)}, u32[]{:S(2)}, u32[]{:S(2)}) collective-permute-start(bf16[336,512]{1,0:T(8,128)(2,1)S(1)} %get-tuple-element.26), channel_id=1, source_target_pairs={{16,32},{32,16},{48,64},{64,48},{80,96},{96,80},{112,128},{128,112... | collective-permute-start | bytes 1032200 | tf_op jit(solution)/shard_map/ppermute | solution.py:36
  19.5 0.0 collective-permute-done.2.refs_6_
  19.6 1.9 %collective-permute-start.3 = (bf16[4,32,128]{2,1,0:T(8,128)(2,1)S(1)}, bf16[4,32,128]{2,1,0:T(8,128)(2,1)S(1)}, u32[]{:S(2)}, u32[]{:S(2)}) collective-permute-start(bf16[4,32,128]{2,1,0:T(8,128)(2,1)S(1)} %pad_maximum_fusion.4.refs_3_), channel_id=1, source_target_pairs={{0,32},{16,48},{32,0},{48,16},{64,96},{80,112},{96,64},{112,80},{1... | collective-permute-start | bytes 98312 | tf_op jit(solution)/shard_map/ppermute | solution.py:30
  21.5 0.0 copy-done.1
  21.5 0.0 copy-done.4
  21.5 0.0 copy-done.6
  21.5 4.6 %inner0.1.refs_4_ = f32[3,64,512]{2,1,0:T(8,128)S(1)} custom-call(s32[8,8]{1,0:T(8,128)S(1)} %bitcast.32, bf16[8,64,512]{2,1,0:T(8,128)(2,1)S(1)} %bitcast.16, bf16[2,3,4,512]{3,2,1,0:T(4,128)(2,1)S(1)} %bitcast.25, bf16[4,32,128]{2,1,0:T(8,128)(2,1)S(1)} %pad_maximum_fusion.4.refs_3_), custom_call_target="tpu_custom_call" | custom-call | flops 6000000000 | bytes 4194304 | tf_op jit(solution)/shard_map/inner0/pallas_call | solution.py:46
  26.2 0.1 collective-permute-done.3.refs_7_
  26.3 6.7 %collective-permute-start.4 = (bf16[5,32,128]{2,1,0:T(8,128)(2,1)S(1)}, bf16[5,32,128]{2,1,0:T(8,128)(2,1)S(1)}, u32[]{:S(2)}, u32[]{:S(2)}) collective-permute-start(bf16[5,32,128]{2,1,0:T(8,128)(2,1)S(1)} %pad_maximum_fusion.3.refs_3_), channel_id=1, source_target_pairs={{0,64},{16,80},{32,96},{48,112},{64,0},{80,16},{96,32},{112,48},{1... | collective-permute-start | bytes 122888 | tf_op jit(solution)/shard_map/ppermute | solution.py:30
  33.0 4.1 %inner1.1.refs_5_ = f32[3,64,512]{2,1,0:T(8,128)S(1)} custom-call(s32[8,8]{1,0:T(8,128)S(1)} %bitcast.33, bf16[8,64,512]{2,1,0:T(8,128)(2,1)S(1)} %bitcast.17, bf16[2,3,4,512]{3,2,1,0:T(4,128)(2,1)S(1)} %bitcast.26, bf16[5,32,128]{2,1,0:T(8,128)(2,1)S(1)} %pad_maximum_fusion.3.refs_3_), custom_call_target="tpu_custom_call" | custom-call | flops 6000000000 | bytes 4194304 | tf_op jit(solution)/shard_map/inner1/pallas_call | solution.py:46
  37.1 0.0 collective-permute-done.4.refs_8_
  37.2 0.0 copy-start.8
  37.2 0.0 copy-start.7
  37.2 1.9 %collective-permute-start.5 = (bf16[6,32,128]{2,1,0:T(8,128)(2,1)S(1)}, bf16[6,32,128]{2,1,0:T(8,128)(2,1)S(1)}, u32[]{:S(2)}, u32[]{:S(2)}) collective-permute-start(bf16[6,32,128]{2,1,0:T(8,128)(2,1)S(1)} %pad_maximum_fusion.2.refs_4_), channel_id=1, source_target_pairs={{0,128},{16,144},{32,160},{48,176},{64,192},{80,208},{96,224},{112... | collective-permute-start | bytes 147464 | tf_op jit(solution)/shard_map/ppermute | solution.py:30
  39.1 4.2 %collective-permute-start.6 = (bf16[6,32,128]{2,1,0:T(8,128)(2,1)S(1)}, bf16[6,32,128]{2,1,0:T(8,128)(2,1)S(1)}, u32[]{:S(2)}, u32[]{:S(2)}) collective-permute-start(bf16[6,32,128]{2,1,0:T(8,128)(2,1)S(1)} %pad_maximum_fusion.2.refs_4_), channel_id=1, source_target_pairs={{128,256},{144,272},{160,288},{176,304},{192,320},{208,336},{224,3... | collective-permute-start | bytes 147464 | tf_op jit(solution)/shard_map/ppermute | solution.py:36
  43.4 0.0 collective-permute-done.refs_2_.refs_3_.refs_8_
  43.4 0.0 collective-permute-done.1.refs_3_.refs_4_.refs_9_
  43.4 5.8 %byrows.1.refs_6_ = f32[8,64,512]{2,1,0:T(8,128)S(1)} custom-call(s32[8,8]{1,0:T(8,128)S(1)} %bitcast.34, bf16[2,3,4,512]{3,2,1,0:T(4,128)(2,1)S(1)} %bitcast.27, bf16[336,512]{1,0:T(8,128)(2,1)S(1)} %collective-permute-done.refs_2_.refs_3_.refs_8_, bf16[336,512]{1,0:T(8,128)(2,1)S(1)} %collective-permute-done.1.refs_3_.refs_4_.refs_9_, ...), custom_call_target="tpu_custom_call" | custom-call | flops 6000000000 | bytes 4194304 | tf_op jit(solution)/shard_map/byrows/pallas_call | solution.py:46
  49.2 0.0 copy-start.5
  49.2 0.0 collective-permute-done.5.refs_9_
  49.2 0.0 collective-permute-done.6.refs_10_
  49.2 0.2 pack.1
  49.4 2.1 %collective-permute-start.7 = (bf16[496,512]{1,0:T(8,128)(2,1)S(1)}, bf16[496,512]{1,0:T(8,128)(2,1)S(1)}, u32[]{:S(2)}, u32[]{:S(2)}) collective-permute-start(bf16[496,512]{1,0:T(8,128)(2,1)S(1)} %get-tuple-element.32), channel_id=1, source_target_pairs={{0,1},{1,0},{2,3},{3,2},{4,5},{5,4},{6,7},{7,6},{8,9},{9,8},{10,11... | collective-permute-start | bytes 1523720 | tf_op jit(solution)/shard_map/ppermute | solution.py:30
  51.4 0.0 copy-done.8
  51.5 0.0 copy-done.7
  51.5 1.9 %collective-permute-start.8 = (bf16[416,512]{1,0:T(8,128)(2,1)S(1)}, bf16[416,512]{1,0:T(8,128)(2,1)S(1)}, u32[]{:S(2)}, u32[]{:S(2)}) collective-permute-start(bf16[416,512]{1,0:T(8,128)(2,1)S(1)} %get-tuple-element.33), channel_id=1, source_target_pairs={{1,2},{2,1},{3,4},{4,3},{5,6},{6,5},{7,8},{8,7},{9,10},{10,9},{11,... | collective-permute-start | bytes 1277960 | tf_op jit(solution)/shard_map/ppermute | solution.py:36
  53.4 0.0 collective-permute-done.7.refs_2_.refs_6_
  53.5 1.9 %collective-permute-start.9 = (bf16[128,512]{1,0:T(8,128)(2,1)S(1)}, bf16[128,512]{1,0:T(8,128)(2,1)S(1)}, u32[]{:S(2)}, u32[]{:S(2)}) collective-permute-start(bf16[128,512]{1,0:T(8,128)(2,1)S(1)} %pad_maximum_fusion.refs_12_), channel_id=1, source_target_pairs={{0,2},{1,3},{2,0},{3,1},{4,6},{5,7},{6,4},{7,5},{8,10},{9,11},{10,... | collective-permute-start | bytes 393224 | tf_op jit(solution)/shard_map/ppermute | solution.py:30
  55.4 4.4 %collective-permute-start.10 = (bf16[128,512]{1,0:T(8,128)(2,1)S(1)}, bf16[128,512]{1,0:T(8,128)(2,1)S(1)}, u32[]{:S(2)}, u32[]{:S(2)}) collective-permute-start(bf16[128,512]{1,0:T(8,128)(2,1)S(1)} %pad_maximum_fusion.refs_12_), channel_id=1, source_target_pairs={{2,4},{3,5},{4,2},{5,3},{6,8},{7,9},{8,6},{9,7},{10,12},{11,13},{1... | collective-permute-start | bytes 393224 | tf_op jit(solution)/shard_map/ppermute | solution.py:36
  59.9 2.5 %collective-permute-done.8.refs_3_.refs_7_ = bf16[416,512]{1,0:T(8,128)(2,1)S(1)} collective-permute-done((bf16[416,512]{1,0:T(8,128)(2,1)S(1)}, bf16[416,512]{1,0:T(8,128)(2,1)S(1)}, u32[]{:S(2)}, u32[]{:S(2)}) %collective-permute-start.8) | collective-permute-done | bytes 426016 | tf_op jit(solution)/shard_map/ppermute | solution.py:36
  62.3 0.0 copy-done.5
  62.4 5.0 %edge.1 = (f32[8,64,512]{2,1,0:T(8,128)S(1)}, f32[8,64,64]{2,1,0:T(8,128)S(1)}) custom-call(s32[8,8]{1,0:T(8,128)S(1)} %bitcast.35, bf16[2,3,4,512]{3,2,1,0:T(4,128)(2,1)S(1)} %bitcast.29, bf16[496,512]{1,0:T(8,128)(2,1)S(1)} %collective-permute-done.7.refs_2_.refs_6_, bf16[416,512]{1,0:T(8,128)(2,1)S(1)} %collective-permute-done.8.refs_3_.refs_7_, ...), custom_call_target="tpu_custom_call" | custom-call | flops 6000000000 | bytes 4194304 | tf_op jit(solution)/shard_map/edge/pallas_call | solution.py:46
  67.4 0.0 collective-permute-done.9.refs_8_.refs_9_
  67.5 3.0 %collective-permute-start.11 = (bf16[80,512]{1,0:T(8,128)(2,1)S(1)}, bf16[80,512]{1,0:T(8,128)(2,1)S(1)}, u32[]{:S(2)}, u32[]{:S(2)}) collective-permute-start(bf16[80,512]{1,0:T(8,128)(2,1)S(1)} %pad_maximum_fusion.1.refs_10_), channel_id=1, source_target_pairs={{0,4},{1,5},{2,6},{3,7},{4,0},{5,1},{6,2},{7,3},{8,12},{9,13},{10,... | collective-permute-start | bytes 245768 | tf_op jit(solution)/shard_map/ppermute | solution.py:30
  70.4 0.7 collective-permute-start.12
  71.1 8.6 %collective-permute-start.13 = (bf16[80,256]{1,0:T(8,128)(2,1)S(1)}, bf16[80,256]{1,0:T(8,128)(2,1)S(1)}, u32[]{:S(2)}, u32[]{:S(2)}) collective-permute-start(bf16[80,256]{1,0:T(8,128)(2,1)S(1)} %add_convert_fusion.1.refs_11_), channel_id=1, source_target_pairs={{0,8},{1,9},{2,10},{3,11},{4,12},{5,13},{6,14},{7,15},{8,0},{9,1},... | collective-permute-start | bytes 122888 | tf_op jit(solution)/shard_map/ppermute | solution.py:30
  79.7 0.0 collective-permute-done.10.refs_9_.refs_10_
  79.7 0.0 copy-done
  79.7 0.0 copy-start.2
  79.7 0.0 copy-start.3
  79.7 4.1 %inner2.1 = (f32[2,64,512]{2,1,0:T(8,128)S(1)}, f32[64,64]{1,0:T(8,128)S(1)}) custom-call(s32[8,8]{1,0:T(8,128)S(1)} %bitcast.36, bf16[8,64,512]{2,1,0:T(8,128)(2,1)S(1)} %bitcast.19, bf16[2,3,4,512]{3,2,1,0:T(4,128)(2,1)S(1)} %bitcast.30, bf16[16,32]{1,0:T(8,128)(2,1)S(1)} %fusion.5.refs_10_.refs_3_.refs_4_, bf16[3,64,1600]{2,1,0:T(8,128)(2,1)S(1)} %bitcast.13, ...), custom_call_target="tpu_custom_call" | custom-call | flops 6000000000 | bytes 4194304 | tf_op jit(solution)/shard_map/inner2/pallas_call | solution.py:46
  83.8 0.0 collective-permute-done.13.refs_14_
  83.8 0.0 collective-permute-done.11.refs_12_
  83.8 0.0 collective-permute-done.12.refs_13_
  83.9 2.9 %last.1 = bf16[8,64,512]{2,1,0:T(8,128)(2,1)} custom-call(f32[8,64,512]{2,1,0:T(8,128)S(1)} %get-tuple-element.39.refs_0_, f32[2,64,512]{2,1,0:T(8,128)S(1)} %get-tuple-element.40.refs_1_, f32[8,64,64]{2,1,0:T(8,128)S(1)} %get-tuple-element.41.refs_2_, f32[64,64]{1,0:T(8,128)S(1)} %get-tuple-element.42.refs_3_, ...), custom_call_target="tpu_custom_call" | custom-call | flops 1000000000 | bytes 4194304 | tf_op jit(solution)/shard_map/last/pallas_call | solution.py:46
  (26 shorter events, 0.2 us)
Async XLA Ops:
  0.0 21.5 %copy-start.1 = (bf16[2,4,64,512]{3,2,1,0:T(8,128)(2,1)S(1)}, bf16[2,4,64,512]{3,2,1,0:T(8,128)(2,1)}, u32[]{:S(2)}) copy-start(bf16[2,4,64,512]{3,2,1,0:T(8,128)(2,1)} %param.10) | copy-start | bytes 1572868
  0.0 21.5 %copy-start.4 = (bf16[2,4,3,512]{3,1,2,0:T(4,128)(2,1)S(1)}, bf16[2,4,3,512]{3,1,2,0:T(4,128)(2,1)}, u32[]{:S(2)}) copy-start(bf16[2,4,3,512]{3,1,2,0:T(4,128)(2,1)} %param.11) | copy-start | bytes 73732
  0.0 21.5 %copy-start.6 = (s32[2,4,8]{2,1,0:T(4,128)S(1)}, s32[2,4,8]{2,1,0:T(4,128)}, u32[]{:S(2)}) copy-start(s32[2,4,8]{2,1,0:T(4,128)} %param.13) | copy-start | bytes 772
  2.7 16.8 %collective-permute-start.2 = (bf16[3,32,128]{2,1,0:T(8,128)(2,1)S(1)}, bf16[3,32,128]{2,1,0:T(8,128)(2,1)S(1)}, u32[]{:S(2)}, u32[]{:S(2)}) collective-permute-start(bf16[3,32,128]{2,1,0:T(8,128)(2,1)S(1)} %get-tuple-element.27.refs_5_), channel_id=1, source_target_pairs={{0,16},{16,0},{32,48},{48,32},{64,80},{80,64},{96,112},{112,96},{1... | collective-permute-start | bytes 73736 | tf_op jit(solution)/shard_map/ppermute | solution.py:30
  7.0 36.3 %collective-permute-start = (bf16[336,512]{1,0:T(8,128)(2,1)S(1)}, bf16[336,512]{1,0:T(8,128)(2,1)S(1)}, u32[]{:S(2)}, u32[]{:S(2)}) collective-permute-start(bf16[336,512]{1,0:T(8,128)(2,1)S(1)} %get-tuple-element.25), channel_id=1, source_target_pairs={{0,16},{16,0},{32,48},{48,32},{64,80},{80,64},{96,112},{112,96},{1... | collective-permute-start | bytes 1032200 | tf_op jit(solution)/shard_map/ppermute | solution.py:30
  9.0 34.4 %collective-permute-start.1 = (bf16[336,512]{1,0:T(8,128)(2,1)S(1)}, bf16[336,512]{1,0:T(8,128)(2,1)S(1)}, u32[]{:S(2)}, u32[]{:S(2)}) collective-permute-start(bf16[336,512]{1,0:T(8,128)(2,1)S(1)} %get-tuple-element.26), channel_id=1, source_target_pairs={{16,32},{32,16},{48,64},{64,48},{80,96},{96,80},{112,128},{128,112... | collective-permute-start | bytes 1032200 | tf_op jit(solution)/shard_map/ppermute | solution.py:36
  19.6 6.7 %collective-permute-start.3 = (bf16[4,32,128]{2,1,0:T(8,128)(2,1)S(1)}, bf16[4,32,128]{2,1,0:T(8,128)(2,1)S(1)}, u32[]{:S(2)}, u32[]{:S(2)}) collective-permute-start(bf16[4,32,128]{2,1,0:T(8,128)(2,1)S(1)} %pad_maximum_fusion.4.refs_3_), channel_id=1, source_target_pairs={{0,32},{16,48},{32,0},{48,16},{64,96},{80,112},{96,64},{112,80},{1... | collective-permute-start | bytes 98312 | tf_op jit(solution)/shard_map/ppermute | solution.py:30
  26.3 10.8 %collective-permute-start.4 = (bf16[5,32,128]{2,1,0:T(8,128)(2,1)S(1)}, bf16[5,32,128]{2,1,0:T(8,128)(2,1)S(1)}, u32[]{:S(2)}, u32[]{:S(2)}) collective-permute-start(bf16[5,32,128]{2,1,0:T(8,128)(2,1)S(1)} %pad_maximum_fusion.3.refs_3_), channel_id=1, source_target_pairs={{0,64},{16,80},{32,96},{48,112},{64,0},{80,16},{96,32},{112,48},{1... | collective-permute-start | bytes 122888 | tf_op jit(solution)/shard_map/ppermute | solution.py:30
  37.2 14.3 %copy-start.8 = (s32[1,1,3,25]{3,1,2,0:T(1,128)S(1)}, s32[1,1,3,25]{3,1,2,0:T(1,128)}, u32[]{:S(2)}) copy-start(s32[1,1,3,25]{3,1,2,0:T(1,128)} %param.18) | copy-start | bytes 904
  37.2 14.3 %copy-start.7 = (s32[2,4,25]{2,1,0:T(4,128)S(1)}, s32[2,4,25]{2,1,0:T(4,128)}, u32[]{:S(2)}) copy-start(s32[2,4,25]{2,1,0:T(4,128)} %param.15) | copy-start | bytes 2404
  37.2 12.0 %collective-permute-start.5 = (bf16[6,32,128]{2,1,0:T(8,128)(2,1)S(1)}, bf16[6,32,128]{2,1,0:T(8,128)(2,1)S(1)}, u32[]{:S(2)}, u32[]{:S(2)}) collective-permute-start(bf16[6,32,128]{2,1,0:T(8,128)(2,1)S(1)} %pad_maximum_fusion.2.refs_4_), channel_id=1, source_target_pairs={{0,128},{16,144},{32,160},{48,176},{64,192},{80,208},{96,224},{112... | collective-permute-start | bytes 147464 | tf_op jit(solution)/shard_map/ppermute | solution.py:30
  39.1 10.1 %collective-permute-start.6 = (bf16[6,32,128]{2,1,0:T(8,128)(2,1)S(1)}, bf16[6,32,128]{2,1,0:T(8,128)(2,1)S(1)}, u32[]{:S(2)}, u32[]{:S(2)}) collective-permute-start(bf16[6,32,128]{2,1,0:T(8,128)(2,1)S(1)} %pad_maximum_fusion.2.refs_4_), channel_id=1, source_target_pairs={{128,256},{144,272},{160,288},{176,304},{192,320},{208,336},{224,3... | collective-permute-start | bytes 147464 | tf_op jit(solution)/shard_map/ppermute | solution.py:36
  49.2 13.2 %copy-start.5 = (bf16[2,4,64,1600]{3,2,1,0:T(8,128)(2,1)S(1)}, bf16[2,4,64,1600]{3,2,1,0:T(8,128)(2,1)}, u32[]{:S(2)}) copy-start(bf16[2,4,64,1600]{3,2,1,0:T(8,128)(2,1)} %param.14) | copy-start | bytes 4915204
  49.4 4.1 %collective-permute-start.7 = (bf16[496,512]{1,0:T(8,128)(2,1)S(1)}, bf16[496,512]{1,0:T(8,128)(2,1)S(1)}, u32[]{:S(2)}, u32[]{:S(2)}) collective-permute-start(bf16[496,512]{1,0:T(8,128)(2,1)S(1)} %get-tuple-element.32), channel_id=1, source_target_pairs={{0,1},{1,0},{2,3},{3,2},{4,5},{5,4},{6,7},{7,6},{8,9},{9,8},{10,11... | collective-permute-start | bytes 1523720 | tf_op jit(solution)/shard_map/ppermute | solution.py:30
  51.5 10.9 %collective-permute-start.8 = (bf16[416,512]{1,0:T(8,128)(2,1)S(1)}, bf16[416,512]{1,0:T(8,128)(2,1)S(1)}, u32[]{:S(2)}, u32[]{:S(2)}) collective-permute-start(bf16[416,512]{1,0:T(8,128)(2,1)S(1)} %get-tuple-element.33), channel_id=1, source_target_pairs={{1,2},{2,1},{3,4},{4,3},{5,6},{6,5},{7,8},{8,7},{9,10},{10,9},{11,... | collective-permute-start | bytes 1277960 | tf_op jit(solution)/shard_map/ppermute | solution.py:36
  53.5 13.9 %collective-permute-start.9 = (bf16[128,512]{1,0:T(8,128)(2,1)S(1)}, bf16[128,512]{1,0:T(8,128)(2,1)S(1)}, u32[]{:S(2)}, u32[]{:S(2)}) collective-permute-start(bf16[128,512]{1,0:T(8,128)(2,1)S(1)} %pad_maximum_fusion.refs_12_), channel_id=1, source_target_pairs={{0,2},{1,3},{2,0},{3,1},{4,6},{5,7},{6,4},{7,5},{8,10},{9,11},{10,... | collective-permute-start | bytes 393224 | tf_op jit(solution)/shard_map/ppermute | solution.py:30
  55.4 24.3 %collective-permute-start.10 = (bf16[128,512]{1,0:T(8,128)(2,1)S(1)}, bf16[128,512]{1,0:T(8,128)(2,1)S(1)}, u32[]{:S(2)}, u32[]{:S(2)}) collective-permute-start(bf16[128,512]{1,0:T(8,128)(2,1)S(1)} %pad_maximum_fusion.refs_12_), channel_id=1, source_target_pairs={{2,4},{3,5},{4,2},{5,3},{6,8},{7,9},{8,6},{9,7},{10,12},{11,13},{1... | collective-permute-start | bytes 393224 | tf_op jit(solution)/shard_map/ppermute | solution.py:36
  62.4 17.4 %copy-start = (bf16[1,1,3,64,1600]{4,3,2,1,0:T(8,128)(2,1)S(1)}, bf16[1,1,3,64,1600]{4,3,2,1,0:T(8,128)(2,1)}, u32[]{:S(2)}) copy-start(bf16[1,1,3,64,1600]{4,3,2,1,0:T(8,128)(2,1)} %param.17) | copy-start | bytes 1843204
  67.5 16.4 %collective-permute-start.11 = (bf16[80,512]{1,0:T(8,128)(2,1)S(1)}, bf16[80,512]{1,0:T(8,128)(2,1)S(1)}, u32[]{:S(2)}, u32[]{:S(2)}) collective-permute-start(bf16[80,512]{1,0:T(8,128)(2,1)S(1)} %pad_maximum_fusion.1.refs_10_), channel_id=1, source_target_pairs={{0,4},{1,5},{2,6},{3,7},{4,0},{5,1},{6,2},{7,3},{8,12},{9,13},{10,... | collective-permute-start | bytes 245768 | tf_op jit(solution)/shard_map/ppermute | solution.py:30
  70.4 13.4 %collective-permute-start.12 = (bf16[80,512]{1,0:T(8,128)(2,1)S(1)}, bf16[80,512]{1,0:T(8,128)(2,1)S(1)}, u32[]{:S(2)}, u32[]{:S(2)}) collective-permute-start(bf16[80,512]{1,0:T(8,128)(2,1)S(1)} %pad_maximum_fusion.1.refs_10_), channel_id=1, source_target_pairs={{4,8},{5,9},{6,10},{7,11},{8,4},{9,5},{10,6},{11,7},{20,24},{21,25... | collective-permute-start | bytes 245768 | tf_op jit(solution)/shard_map/ppermute | solution.py:36
  71.1 12.7 %collective-permute-start.13 = (bf16[80,256]{1,0:T(8,128)(2,1)S(1)}, bf16[80,256]{1,0:T(8,128)(2,1)S(1)}, u32[]{:S(2)}, u32[]{:S(2)}) collective-permute-start(bf16[80,256]{1,0:T(8,128)(2,1)S(1)} %add_convert_fusion.1.refs_11_), channel_id=1, source_target_pairs={{0,8},{1,9},{2,10},{3,11},{4,12},{5,13},{6,14},{7,15},{8,0},{9,1},... | collective-permute-start | bytes 122888 | tf_op jit(solution)/shard_map/ppermute | solution.py:30
  79.7 4.1 %copy-start.2 = (bf16[2,4,64,512]{3,2,1,0:T(8,128)(2,1)S(1)}, bf16[2,4,64,512]{3,2,1,0:T(8,128)(2,1)}, u32[]{:S(2)}) copy-start(bf16[2,4,64,512]{3,2,1,0:T(8,128)(2,1)} %param.12) | copy-start | bytes 1572868
  79.7 4.1 %copy-start.3 = (bf16[2,4,64,64]{3,2,1,0:T(8,128)(2,1)S(1)}, bf16[2,4,64,64]{3,2,1,0:T(8,128)(2,1)}, u32[]{:S(2)}) copy-start(bf16[2,4,64,64]{3,2,1,0:T(8,128)(2,1)} %param.16) | copy-start | bytes 196612

commit v3 on v2

--- a/solution.py
+++ b/solution.py
@@ -17,6 +17,7 @@
 TN = (((0,), (0,)), ((), ()))
 WIDE = 25 * RANK
 MIB = 2**20
+AT_ONCE = (8, 4, 2, 1)
 VMEM = pl.BlockSpec(memory_space=pltpu.VMEM)
 SMEM = pl.BlockSpec(memory_space=pltpu.SMEM)
 HBM = pl.BlockSpec(memory_space=pltpu.HBM)
@@ -36,7 +37,7 @@
     return lax.ppermute(value, axis, [(i, j) for i, j in moves if 0 <= j < count])
 
 
-def kernel_call(body, outs, scratch, name, cost, *args, smem=(), hbm=(), after=(), limit=40):
+def kernel_call(body, outs, scratch, name, cost, *args, smem=(), hbm=(), after=(), out_space=VMEM):
     count = len(args)
 
     def with_order(*refs):
@@ -47,9 +48,9 @@
         with_order,
         out_shape=outs,
         in_specs=spaces + [VMEM] * len(after),
-        out_specs=jax.tree.map(lambda _: VMEM, outs),
+        out_specs=jax.tree.map(lambda _: out_space, outs),
         scratch_shapes=scratch,
-        compiler_params=pltpu.CompilerParams(vmem_limit_bytes=limit * MIB),
+        compiler_params=pltpu.CompilerParams(vmem_limit_bytes=40 * MIB),
         cost_estimate=pl.CostEstimate(flops=cost, bytes_accessed=4 * MIB, transcendentals=0),
         name=name,
     )(*[pltpu.with_memory_space_constraint(arg, pltpu.HBM) if i in hbm else arg for i, arg in enumerate(args)], *after)
@@ -97,7 +98,7 @@
 
 
 def target_features(off):
-    x, y, z = off[0:1], off[1:2], off[2:3]
+    x, y, z = off
     high, middle, low = three_parts(PANELS * (x * x + y * y + z * z + EPSILON))
     return rows_of([x, y, z, x, y, high, middle, low, 1.0, 1.0, 1.0], 16).T.astype(BF16)
 
@@ -129,18 +130,17 @@
         tile = lax.rsqrt(squared).astype(BF16)
         acc[target] += lax.dot_general(source_charges[source], tile, NT, preferred_element_type=F32)
 
-    def several(step, carry):
-        for k in range(4):
-            one(4 * step + k)
-        return carry
-
-    def single(step, carry):
-        one(step)
-        return carry
-
-    fours = count // 4
-    lax.fori_loop(0, fours, several, 0)
-    lax.fori_loop(4 * fours, count, single, 0)
+    done = jnp.int32(0)
+    for at_once in AT_ONCE:
+        steps = (count - done) // at_once
+
+        def several(step, carry, done=done, at_once=at_once):
+            for k in range(at_once):
+                one(done + step * at_once + k)
+            return carry
+
+        lax.fori_loop(0, steps, several, 0)
+        done = done + steps * at_once
 
 
 def slot_of(row_off, col_off):
@@ -181,7 +181,7 @@
 
 def first_kernel(
     charges_hbm, offsets_hbm, basis_hbm, transfer_hbm, parent_hbm,
-    with_pair, across, small, poles_out,
+    with_pair, across, small, poles_out, feats,
     charges, offsets, basis, transfer, parent, sems,
 ):
     side = place_bits()[0]
@@ -200,6 +200,9 @@
     halves = [rows_of([offs[row][k % 3][k // 3 : k // 3 + 1] for k in range(12)], 16).astype(BF16) for row in range(2)]
     with_pair[ROW_OFFS:ROW_POLES, :] = jnp.where(side == 0, halves[1], halves[0])
     across[ROW_OFFS:ROW_POLES, :] = jnp.where(side == 0, halves[0], halves[1])
+    for leaf in range(8):
+        row, col = divmod(leaf, 4)
+        feats[leaf] = target_features([offs[row][k][col : col + 1] for k in range(3)])
     poles = []
     for k in range(4):
         loads[2 * k].wait()
@@ -234,10 +237,9 @@
                 offs[4 * row + col, k : k + 1, :] = values[col : col + 1]
 
 
-def inner_kernel(targets, mask, charges, offsets, out, listed, feats, offs, acc):
+def inner_kernel(targets, mask, charges, offsets, feats, out, listed, offs, acc):
     own_offsets(offsets, offs)
     for target in targets:
-        feats[target] = target_features(offs[target, 0:3, :])
         acc[target] = jnp.zeros((LOADS, PANELS), F32)
     near_pairs(inner_pairs(targets), mask, listed, feats, offs, charges, acc)
     out[...] = acc[targets[0] : targets[-1] + 1]
@@ -249,11 +251,8 @@
         offs[base + leaf, 0:3, :] = values[3 * leaf : 3 * leaf + 3]
 
 
-def row_kernel(mask, offsets, paired_rows, across_rows, out, listed, feats, offs, charges, acc):
+def row_kernel(mask, feats, paired_rows, across_rows, out, listed, offs, charges, acc):
     place = place_bits()
-    own_offsets(offsets, offs)
-    for leaf in range(8):
-        feats[leaf] = target_features(offs[leaf, 0:3, :])
     for side, buffer in ((1 - place[0], paired_rows), (place[0], across_rows)):
         spread_offsets(buffer[ROW_OFFS:ROW_POLES, :], offs, 4 * side)
         for col in range(4):
@@ -361,22 +360,19 @@
 
 
 def edge_kernel(
-    mask, offsets, paired_cols, across_cols, inner0, inner1, by_rows, poles, paired_rows, across_rows, flags, coupling,
-    out, leaf_out, listed, feats, offs, charges, acc, table,
+    mask, feats, paired_cols, across_cols, inner0, inner1, inner2, by_rows, poles, paired_rows, across_rows, flags, coupling,
+    box_coupling, boxes, pair2, across2, transfer, basis,
+    out, box_out, moved_basis, listed, offs, charges, acc, table, window, local,
 ):
     place = place_bits()
-    own_offsets(offsets, offs)
-    for leaf in (0, 3, 4, 7):
-        feats[leaf] = target_features(offs[leaf, 0:3, :])
     for side, buffer in ((1 - place[1], paired_cols), (place[1], across_cols)):
         spread_offsets(buffer[COL_OFFS:COL_POLES, :], offs, 4 * side)
         for spot in range(4):
             charges[4 * side + spot] = buffer[64 * spot : 64 * (spot + 1), :]
     acc[0:3] = inner0[...] + by_rows[0:3]
     acc[3:6] = inner1[...] + by_rows[3:6]
-    acc[6:8] = by_rows[6:8]
+    acc[6:8] = inner2[...] + by_rows[6:8]
     near_pairs(col_pairs(), mask, listed, feats, offs, charges, acc)
-    out[...] = acc[...]
 
     def put(row, pair, both):
         table[row, 128 * pair : 128 * pair + 64, :] = both[:, :64]
@@ -402,20 +398,6 @@
                     base, lane = COL_POLES + 32 * (row // 2), 256 * (row % 2)
                     put(row, pair, unflat(buffer[base : base + 32, lane : lane + 256]))
 
-    spread = flag_row(flags[...])
-    for row in range(2):
-        for col in range(4):
-            leaf = 4 * row + col
-            seen = jnp.concatenate([table[row + a, 64 * col : 64 * (col + 5), :] for a in range(5)], axis=0)
-            leaf_out[leaf] = box_product(coupling[leaf], spread[leaf : leaf + 1], seen)
-
-
-def inner_box_kernel(
-    targets, mask, charges, offsets, flags, box_coupling, boxes, paired_cols, across_cols, pair2, across2,
-    out, box_out, listed, feats, offs, acc, window,
-):
-    inner_kernel(targets, mask, charges, offsets, out, listed, feats, offs, acc)
-    place = place_bits()
     low1, low2 = place[1] == 0, place[5] == 0
     for row in range(5):
         base, lane = 16 * (row // 2), 256 * (row % 2)
@@ -432,13 +414,25 @@
         for col in range(5):
             start = 64 * (5 * row + col)
             window[start : start + 64, :] = unfold(unflat(found[col]))
-    box_out[...] = box_product(box_coupling[0], flag_row(flags[...])[8:9], window[...])
+    spread = flag_row(flags[...])
+    for row in range(2):
+        for col in range(4):
+            leaf = 4 * row + col
+            seen = jnp.concatenate([table[row + a, 64 * col : 64 * (col + 5), :] for a in range(5)], axis=0)
+            local[leaf] = box_product(coupling[leaf], spread[leaf : leaf + 1], seen).astype(BF16)
+    box_out[...] = box_product(box_coupling[0], spread[8:9], window[...])
+    for leaf in range(8):
+        moved = lax.dot_general(transfer[leaf], basis[leaf], TN, preferred_element_type=F32)
+        moved_basis[leaf] = moved.astype(BF16)
+    for leaf in range(8):
+        far = lax.dot_general(local[leaf], basis[leaf], TN, preferred_element_type=F32)
+        out[leaf] = acc[leaf] + far
 
 
 def last_kernel(
-    near, inner2, leaf_local, box_one, flags, box_coupling, transfer, basis,
+    near, box_one, flags, box_coupling, moved_basis,
     sums, pair2, across2, boxes3, pair4, across4, pair8,
-    out, window,
+    out_hbm, window, out, sems,
 ):
     place = place_bits()
     spread = flag_row(flags[...])
@@ -463,18 +457,19 @@
                 start = 64 * (5 * row + col)
                 window[start : start + 64, :] = unfold(unflat(found[col]))
         total = total + box_product(box_coupling[1 + level], spread[9 + level : 10 + level], window[...])
-    total = total.astype(BF16)
+    total = total.T.astype(BF16)
+    stores = [pltpu.make_async_copy(out.at[leaf], out_hbm.at[leaf], sems.at[leaf]) for leaf in range(8)]
     for leaf in range(8):
-        local = leaf_local[leaf] + jnp.dot(transfer[leaf], total, preferred_element_type=F32)
-        far = lax.dot_general(local.astype(BF16), basis[leaf], TN, preferred_element_type=F32)
-        direct = near[leaf] + inner2[leaf - 6] if leaf >= 6 else near[leaf]
-        out[leaf] = (direct + far).astype(BF16)
+        far = jnp.dot(total, moved_basis[leaf], preferred_element_type=F32)
+        out[leaf] = (near[leaf] + far).astype(BF16)
+        stores[leaf].start()
+    for store in stores:
+        store.wait()
 
 
 def near_scratch(sources):
     return [
         pltpu.SMEM((32,), jnp.int32),
-        pltpu.VMEM((8, PANELS, 16), BF16),
         pltpu.VMEM((8, 8, PANELS), F32),
         *([pltpu.VMEM((8, LOADS, PANELS), BF16)] if sources else []),
         pltpu.VMEM((8, LOADS, PANELS), F32),
@@ -504,9 +499,9 @@
     flags = jnp.concatenate([leaf_distant_flags.reshape(8, 25), box_far.reshape(3, 25)], axis=0)
     flags = jnp.pad(flags, ((0, 5), (0, 7))).astype(BF16)
     near_cost = 6 * 10**9
-    rows_pair, rows_across, small, poles = kernel_call(
+    rows_pair, rows_across, small, poles, feats = kernel_call(
         first_kernel,
-        (shape((ROW_ALL, 512)), shape((ROW_ALL, 512)), shape((3, 32, 128)), shape((4, 64, 128))),
+        (shape((ROW_ALL, 512)), shape((ROW_ALL, 512)), shape((3, 32, 128)), shape((4, 64, 128)), shape((8, PANELS, 16))),
         [
             pltpu.VMEM((8, LOADS, PANELS), BF16),
             pltpu.VMEM((2, 3, 4, PANELS), BF16),
@@ -520,28 +515,31 @@
 
     pair1 = paired(small, "row", 1)
     paired_rows = paired(rows_pair, "row", 1)
-    across_rows = paired_across(rows_across, "row", 1)
+    near_args = (mask, charges, offsets, feats)
+
+    def inner_call(targets, name, after):
+        return kernel_call(
+            functools.partial(inner_kernel, targets), shape((len(targets), LOADS, PANELS), F32),
+            near_scratch(False), name, near_cost, *near_args, smem=(0,), after=after,
+        )
+
     halves = (small[1:3].astype(F32) + pair1[1:3].astype(F32)).astype(BF16)
     payload = jnp.concatenate([small[:1], pair1[:1], halves], axis=0)
     pair2 = paired(payload, "row", 2)
-    inner0 = kernel_call(
-        functools.partial(inner_kernel, (0, 1, 2)), shape((3, LOADS, PANELS), F32), near_scratch(False), "inner0",
-        near_cost, mask, charges, offsets, smem=(0,), after=(payload,),
-    )
+    inner0 = inner_call((0, 1, 2), "inner0", (payload,))
     pair2, inner0 = lax.optimization_barrier((pair2, inner0))
     quarter = (small[2].astype(F32) + pair1[2].astype(F32) + pair2[3].astype(F32)).astype(BF16)
-    payload = jnp.concatenate([halves[:1], quarter[None], pair2[:3]], axis=0)
-    pair4 = paired(payload, "row", 4)
-    inner1 = kernel_call(
-        functools.partial(inner_kernel, (3, 4, 5)), shape((3, LOADS, PANELS), F32), near_scratch(False), "inner1",
-        near_cost, mask, charges, offsets, smem=(0,), after=(payload,),
-    )
+    payload = jnp.concatenate([pair2[2:3], quarter[None], small[:1], pair1[:1], halves[:1]], axis=0)
+    pair4 = paired(payload, "row", 6)
+    payload, rows_across = lax.optimization_barrier((payload, rows_across))
+    across_rows = paired_across(rows_across, "row", 1)
+    inner1 = inner_call((3, 4, 5), "inner1", (payload,))
     pair4, inner1 = lax.optimization_barrier((pair4, inner1))
     payload = jnp.concatenate([quarter[None], pair4[1:2], pair4[0:1], pair4[2:5]], axis=0)
     pair8, across8 = paired(payload, "row", 8), paired_across(payload, "row", 8)
     by_rows = kernel_call(
         row_kernel, shape((8, LOADS, PANELS), F32), near_scratch(True), "byrows", near_cost,
-        mask, offsets, paired_rows, across_rows, smem=(0,), after=(payload,),
+        mask, feats, paired_rows, across_rows, smem=(0,), after=(payload,),
     )
 
     pair8, across8, by_rows = lax.optimization_barrier((pair8, across8, by_rows))
@@ -557,28 +555,26 @@
     sums = (row_sums.astype(F32) + paired_cols[COL_ALL:].astype(F32)).astype(BF16)
     payload = jnp.concatenate([boxes1, sums], axis=0)
     col_pair2, col_across2 = paired(payload, "col", 2), paired_across(payload, "col", 2)
-    near, leaf_local = kernel_call(
-        edge_kernel,
-        (shape((8, LOADS, PANELS), F32), shape((8, RANK, LOADS), F32)),
-        near_scratch(True) + [pltpu.VMEM((6, 512, LOADS), BF16)], "edge", near_cost,
-        mask, offsets, paired_cols, across_cols, inner0, inner1, by_rows, poles, paired_rows, across_rows,
-        flags, coupling, smem=(0,), after=(payload,),
-    )
+    inner2 = inner_call((6, 7), "inner2", (payload,))
+    col_pair2, inner2 = lax.optimization_barrier((col_pair2, inner2))
     boxes3 = (sums[:, 256:].astype(F32) + col_pair2[48:, 256:].astype(F32)).astype(BF16)
     payload = jnp.concatenate([sums[:, :256], boxes3], axis=1)
     col_pair4, col_across4 = paired(payload, "col", 4), paired_across(payload, "col", 4)
-    col_pair8 = paired(boxes3, "col", 8)
-    inner2, box_one = kernel_call(
-        functools.partial(inner_box_kernel, (6, 7)),
-        (shape((2, LOADS, PANELS), F32), shape((RANK, LOADS), F32)),
-        near_scratch(False) + [pltpu.VMEM((WIDE, LOADS), BF16)], "inner2", near_cost,
-        mask, charges, offsets, flags, box_coupling, boxes1, paired_cols, across_cols, col_pair2, col_across2,
+    col_pair8 = paired(boxes3, "col", 10)
+    direct, box_one, moved_basis = kernel_call(
+        edge_kernel,
+        (shape((8, LOADS, PANELS), F32), shape((RANK, LOADS), F32), shape((8, RANK, PANELS))),
+        near_scratch(True)
+        + [pltpu.VMEM((6, 512, LOADS), BF16), pltpu.VMEM((WIDE, LOADS), BF16), pltpu.VMEM((8, RANK, LOADS), BF16)],
+        "edge", near_cost, mask, feats, paired_cols, across_cols, inner0, inner1, inner2, by_rows, poles,
+        paired_rows, across_rows, flags, coupling, box_coupling, boxes1, col_pair2, col_across2, transfer, basis,
         smem=(0,), after=(payload,),
     )
     out = kernel_call(
-        last_kernel, shape((8, LOADS, PANELS)), [pltpu.VMEM((WIDE, LOADS), BF16)], "last", 10**9,
-        near, inner2, leaf_local, box_one, flags, box_coupling, transfer, basis,
-        sums, col_pair2, col_across2, boxes3, col_pair4, col_across4, col_pair8,
+        last_kernel, shape((8, LOADS, PANELS)),
+        [pltpu.VMEM((WIDE, LOADS), BF16), pltpu.VMEM((8, LOADS, PANELS), BF16), pltpu.SemaphoreType.DMA((8,))], "last", 10**9,
+        direct, box_one, flags, box_coupling, moved_basis,
+        sums, col_pair2, col_across2, boxes3, col_pair4, col_across4, col_pair8, out_space=HBM,
     )
     return out.reshape(2, 4, LOADS, PANELS)
 

time: 87.3 us -> 81.7 us (0.936)
  the two profiles are of different devices: /device:TPU:10 before, /device:TPU:1 now
where the time goes in v3:
time: 81.7 us; the launch traced here: 81.2 us
  starting transfers between devices  53.9 us (66%)
  Pallas kernels  25.2 us (31%)
  waiting for transfers between devices  1.16 us (1%)
    ppermute x9, starting transfers between devices, paired(): lax.ppermute(value, axis, [(i, i ^ distance) for i in range(lax.axis_size...  48.2 us
    pallas_call x8, Pallas kernels, kernel_call(): pl.pallas_call(with_order, out_shape=outs, in_specs=spaces + [VMEM] * len...  25.2 us
    ppermute x5, starting transfers between devices, paired_across(): lax.ppermute(value, axis, [(i, j) for i, j in moves if 0 <= j < count])  5.77 us
  transfers between devices with their start and end apart: 14, of which 1 were waited for; matrix products, arithmetic and copies ran while one was open for 0% of the time, Pallas kernels for 25%

profile of v3, /device:TPU:1, one launch (start us, length us, event | category | flops | bytes accessed | tf_op | source)
XLA Modules:
  0.0 81.2 jit_solution(11322197617668826962)
XLA Ops:
  0.0 3.1 %first.1 = (bf16[336,512]{1,0:T(8,128)(2,1)S(1)}, bf16[336,512]{1,0:T(8,128)(2,1)S(1)}, bf16[3,32,128]{2,1,0:T(8,128)(2,1)S(1)}, bf16[4,64,128]{2,1,0:T(8,128)(2,1)S(1)}, bf16[8,512,16]{2,1,0:T(8,128)(2,1)S(1)}) custom-call(bf16[8,64,512]{2,1,0:T(8,128)(2,1)} %bitcast.13, bf16[2,3,4,512]{3,2,1,0:T(4,128)(2,1)} %bitcast.18, bf16[8,64,512]{2,1,0:T(8,128)(2,1)} %bitcast.26, ...), custom_call_target="tpu_custom_call" | custom-call | flops 1000000000 | bytes 4194304 | tf_op jit(solution)/shard_map/first/pallas_call | solution.py:47
  3.1 4.8 %collective-permute-start.1 = (bf16[3,32,128]{2,1,0:T(8,128)(2,1)S(1)}, bf16[3,32,128]{2,1,0:T(8,128)(2,1)S(1)}, u32[]{:S(2)}, u32[]{:S(2)}) collective-permute-start(bf16[3,32,128]{2,1,0:T(8,128)(2,1)S(1)} %get-tuple-element.31.refs_5_), channel_id=1, source_target_pairs={{0,16},{16,0},{32,48},{48,32},{64,80},{80,64},{96,112},{112,96},{1... | collective-permute-start | bytes 73736 | tf_op jit(solution)/shard_map/ppermute | solution.py:31
  7.9 1.9 %collective-permute-start = (bf16[336,512]{1,0:T(8,128)(2,1)S(1)}, bf16[336,512]{1,0:T(8,128)(2,1)S(1)}, u32[]{:S(2)}, u32[]{:S(2)}) collective-permute-start(bf16[336,512]{1,0:T(8,128)(2,1)S(1)} %get-tuple-element.30), channel_id=1, source_target_pairs={{0,16},{16,0},{32,48},{48,32},{64,80},{80,64},{96,112},{112,96},{1... | collective-permute-start | bytes 1032200 | tf_op jit(solution)/shard_map/ppermute | solution.py:31
  9.9 0.0 collective-permute-done.1.refs_6_
  9.9 5.8 %collective-permute-start.2 = (bf16[4,32,128]{2,1,0:T(8,128)(2,1)S(1)}, bf16[4,32,128]{2,1,0:T(8,128)(2,1)S(1)}, u32[]{:S(2)}, u32[]{:S(2)}) collective-permute-start(bf16[4,32,128]{2,1,0:T(8,128)(2,1)S(1)} %pad_maximum_fusion.3.refs_4_), channel_id=1, source_target_pairs={{0,32},{16,48},{32,0},{48,16},{64,96},{80,112},{96,64},{112,80},{1... | collective-permute-start | bytes 98312 | tf_op jit(solution)/shard_map/ppermute | solution.py:31
  15.7 0.0 copy-done
  15.7 0.0 copy-done.1
  15.8 3.4 %inner0.1.refs_4_ = f32[3,64,512]{2,1,0:T(8,128)S(1)} custom-call(s32[8,8]{1,0:T(8,128)S(1)} %bitcast.30, bf16[8,64,512]{2,1,0:T(8,128)(2,1)S(1)} %bitcast.14, bf16[2,3,4,512]{3,2,1,0:T(4,128)(2,1)S(1)} %bitcast.19, bf16[8,512,16]{2,1,0:T(8,128)(2,1)S(1)} %get-tuple-element.28.refs_3_.refs_1_, bf16[4,32,128]{2,1,0:T(8,128)(2,1)S(1)} %pad_maximum_fusion.3.refs_4_), custom_call_target="tpu_custom_call" | custom-call | flops 6000000000 | bytes 4194304 | tf_op jit(solution)/shard_map/inner0/pallas_call | solution.py:47
  19.1 0.0 collective-permute-done.2.refs_7_
  19.2 8.5 %collective-permute-start.4 = (bf16[5,32,128]{2,1,0:T(8,128)(2,1)S(1)}, bf16[5,32,128]{2,1,0:T(8,128)(2,1)S(1)}, u32[]{:S(2)}, u32[]{:S(2)}) collective-permute-start(bf16[5,32,128]{2,1,0:T(8,128)(2,1)S(1)} %constant_dynamic-update-slice_fusion.refs_4_), channel_id=1, source_target_pairs={{0,96},{16,112},{32,64},{48,80},{64,32},{80,48},{96,0},{112,16},{1... | collective-permute-start | bytes 122888 | tf_op jit(solution)/shard_map/ppermute | solution.py:31
  27.7 0.7 collective-permute-start.3
  28.4 3.4 %inner1.1.refs_5_ = f32[3,64,512]{2,1,0:T(8,128)S(1)} custom-call(s32[8,8]{1,0:T(8,128)S(1)} %bitcast.31, bf16[8,64,512]{2,1,0:T(8,128)(2,1)S(1)} %bitcast.15, bf16[2,3,4,512]{3,2,1,0:T(4,128)(2,1)S(1)} %bitcast.20, bf16[8,512,16]{2,1,0:T(8,128)(2,1)S(1)} %get-tuple-element.28.refs_3_.refs_1_, bf16[5,32,128]{2,1,0:T(8,128)(2,1)S(1)} %constant_dynamic-update-slice_fusion.refs_4_), custom_call_target="tpu_custom_call" | custom-call | flops 6000000000 | bytes 4194304 | tf_op jit(solution)/shard_map/inner1/pallas_call | solution.py:47
  31.8 0.0 collective-permute-done.4.refs_8_
  31.9 0.0 copy-start.8
  31.9 0.0 copy-start.7
  31.9 0.7 collective-permute-start.6
  32.5 6.7 %collective-permute-start.5 = (bf16[6,32,128]{2,1,0:T(8,128)(2,1)S(1)}, bf16[6,32,128]{2,1,0:T(8,128)(2,1)S(1)}, u32[]{:S(2)}, u32[]{:S(2)}) collective-permute-start(bf16[6,32,128]{2,1,0:T(8,128)(2,1)S(1)} %pad_maximum_fusion.2.refs_4_), channel_id=1, source_target_pairs={{0,128},{16,144},{32,160},{48,176},{64,192},{80,208},{96,224},{112... | collective-permute-start | bytes 147464 | tf_op jit(solution)/shard_map/ppermute | solution.py:31
  39.2 0.0 collective-permute-done.refs_2_.refs_3_.refs_9_
  39.2 0.0 collective-permute-done.3.refs_3_.refs_4_.refs_10_
  39.2 5.4 %byrows.1.refs_7_ = f32[8,64,512]{2,1,0:T(8,128)S(1)} custom-call(s32[8,8]{1,0:T(8,128)S(1)} %bitcast.32, bf16[8,512,16]{2,1,0:T(8,128)(2,1)S(1)} %get-tuple-element.28.refs_3_.refs_1_, bf16[336,512]{1,0:T(8,128)(2,1)S(1)} %collective-permute-done.refs_2_.refs_3_.refs_9_, bf16[336,512]{1,0:T(8,128)(2,1)S(1)} %collective-permute-done.3.refs_3_.refs_4_.refs_10_, ...), custom_call_target="tpu_custom_call" | custom-call | flops 6000000000 | bytes 4194304 | tf_op jit(solution)/shard_map/byrows/pallas_call | solution.py:47
  44.7 0.0 collective-permute-done.6.refs_10_
  44.7 0.0 collective-permute-done.5.refs_9_
  44.7 0.2 pack.1
  44.9 3.7 %collective-permute-start.7 = (bf16[496,512]{1,0:T(8,128)(2,1)S(1)}, bf16[496,512]{1,0:T(8,128)(2,1)S(1)}, u32[]{:S(2)}, u32[]{:S(2)}) collective-permute-start(bf16[496,512]{1,0:T(8,128)(2,1)S(1)} %get-tuple-element.39), channel_id=1, source_target_pairs={{0,1},{1,0},{2,3},{3,2},{4,5},{5,4},{6,7},{7,6},{8,9},{9,8},{10,11... | collective-permute-start | bytes 1523720 | tf_op jit(solution)/shard_map/ppermute | solution.py:31
  48.6 3.0 %collective-permute-start.8 = (bf16[416,512]{1,0:T(8,128)(2,1)S(1)}, bf16[416,512]{1,0:T(8,128)(2,1)S(1)}, u32[]{:S(2)}, u32[]{:S(2)}) collective-permute-start(bf16[416,512]{1,0:T(8,128)(2,1)S(1)} %get-tuple-element.40), channel_id=1, source_target_pairs={{1,2},{2,1},{3,4},{4,3},{5,6},{6,5},{7,8},{8,7},{9,10},{10,9},{11,... | collective-permute-start | bytes 1277960 | tf_op jit(solution)/shard_map/ppermute | solution.py:37
  51.6 0.0 collective-permute-done.7.refs_2_
  51.7 0.0 copy-start.2
  51.7 0.0 copy-start.3
  51.7 0.0 copy-start.4
  51.7 0.0 copy-start.5
  51.7 0.8 collective-permute-start.10
  52.5 5.4 %collective-permute-start.9 = (bf16[128,512]{1,0:T(8,128)(2,1)S(1)}, bf16[128,512]{1,0:T(8,128)(2,1)S(1)}, u32[]{:S(2)}, u32[]{:S(2)}) collective-permute-start(bf16[128,512]{1,0:T(8,128)(2,1)S(1)} %pad_maximum_fusion.refs_4_), channel_id=1, source_target_pairs={{0,2},{1,3},{2,0},{3,1},{4,6},{5,7},{6,4},{7,5},{8,10},{9,11},{10,... | collective-permute-start | bytes 393224 | tf_op jit(solution)/shard_map/ppermute | solution.py:31
  57.9 2.6 %inner2.1.refs_6_ = f32[2,64,512]{2,1,0:T(8,128)S(1)} custom-call(s32[8,8]{1,0:T(8,128)S(1)} %bitcast.33, bf16[8,64,512]{2,1,0:T(8,128)(2,1)S(1)} %bitcast.17, bf16[2,3,4,512]{3,2,1,0:T(4,128)(2,1)S(1)} %bitcast.22, bf16[8,512,16]{2,1,0:T(8,128)(2,1)S(1)} %get-tuple-element.28.refs_3_.refs_1_, bf16[128,512]{1,0:T(8,128)(2,1)S(1)} %pad_maximum_fusion.refs_4_), custom_call_target="tpu_custom_call" | custom-call | flops 6000000000 | bytes 4194304 | tf_op jit(solution)/shard_map/inner2/pallas_call | solution.py:47
  60.5 1.1 %collective-permute-done.9.refs_15_.refs_6_ = bf16[128,512]{1,0:T(8,128)(2,1)S(1)} collective-permute-done((bf16[128,512]{1,0:T(8,128)(2,1)S(1)}, bf16[128,512]{1,0:T(8,128)(2,1)S(1)}, u32[]{:S(2)}, u32[]{:S(2)}) %collective-permute-start.9) | collective-permute-done | bytes 131104 | tf_op jit(solution)/shard_map/ppermute | solution.py:31
  61.6 7.6 %collective-permute-start.13 = (bf16[80,256]{1,0:T(8,128)(2,1)S(1)}, bf16[80,256]{1,0:T(8,128)(2,1)S(1)}, u32[]{:S(2)}, u32[]{:S(2)}) collective-permute-start(bf16[80,256]{1,0:T(8,128)(2,1)S(1)} %add_convert_fusion.1.refs_8_), channel_id=1, source_target_pairs={{0,10},{1,11},{2,8},{3,9},{4,14},{5,15},{6,12},{7,13},{8,2},{9,3},... | collective-permute-start | bytes 122888 | tf_op jit(solution)/shard_map/ppermute | solution.py:31
  69.2 0.7 collective-permute-start.12
  69.9 3.8 %collective-permute-start.11 = (bf16[80,512]{1,0:T(8,128)(2,1)S(1)}, bf16[80,512]{1,0:T(8,128)(2,1)S(1)}, u32[]{:S(2)}, u32[]{:S(2)}) collective-permute-start(bf16[80,512]{1,0:T(8,128)(2,1)S(1)} %pad_maximum_fusion.1.refs_19_), channel_id=1, source_target_pairs={{0,4},{1,5},{2,6},{3,7},{4,0},{5,1},{6,2},{7,3},{8,12},{9,13},{10,... | collective-permute-start | bytes 245768 | tf_op jit(solution)/shard_map/ppermute | solution.py:31
  73.7 0.0 collective-permute-done.8.refs_3_
  73.7 0.0 collective-permute-done.10.refs_16_.refs_7_
  73.7 0.0 copy-done.2
  73.7 0.0 copy-done.3
  73.8 0.0 copy-done.4
  73.8 0.0 copy-done.5
  73.8 5.7 %edge.1 = (f32[8,64,512]{2,1,0:T(8,128)S(1)}, f32[64,64]{1,0:T(8,128)S(1)}, bf16[8,64,512]{2,1,0:T(8,128)(2,1)S(1)}) custom-call(s32[8,8]{1,0:T(8,128)S(1)} %bitcast.34, bf16[8,512,16]{2,1,0:T(8,128)(2,1)S(1)} %get-tuple-element.28.refs_3_.refs_1_, bf16[496,512]{1,0:T(8,128)(2,1)S(1)} %collective-permute-done.7.refs_2_, ...), custom_call_target="tpu_custom_call" | custom-call | flops 6000000000 | bytes 4194304 | tf_op jit(solution)/shard_map/edge/pallas_call | solution.py:47
  79.5 0.0 collective-permute-done.13.refs_11_
  79.5 0.0 collective-permute-done.12.refs_10_
  79.5 0.0 collective-permute-done.11.refs_9_
  79.5 1.6 %last.1 = bf16[8,64,512]{2,1,0:T(8,128)(2,1)} custom-call(f32[8,64,512]{2,1,0:T(8,128)S(1)} %get-tuple-element.48.refs_0_, f32[64,64]{1,0:T(8,128)S(1)} %get-tuple-element.49.refs_1_, bf16[16,32]{1,0:T(8,128)(2,1)S(1)} %fusion.5.refs_11_.refs_2_, bf16[3,64,1600]{2,1,0:T(8,128)(2,1)S(1)} %bitcast.25, bf16[8,64,512]{2,1,0:T(8,128)(2,1)S(1)} %get-tuple-element.50.refs_4_, ...), custom_call_target="tpu_custom_call" | custom-call | flops 1000000000 | bytes 4194304 | tf_op jit(solution)/shard_map/last/pallas_call | solution.py:47
  (27 shorter events, 0.2 us)
Async XLA Ops:
  0.0 15.7 %copy-start = (bf16[2,4,64,512]{3,2,1,0:T(8,128)(2,1)S(1)}, bf16[2,4,64,512]{3,2,1,0:T(8,128)(2,1)}, u32[]{:S(2)}) copy-start(bf16[2,4,64,512]{3,2,1,0:T(8,128)(2,1)} %param.10) | copy-start | bytes 1572868
  0.0 15.7 %copy-start.1 = (bf16[2,4,3,512]{3,1,2,0:T(4,128)(2,1)S(1)}, bf16[2,4,3,512]{3,1,2,0:T(4,128)(2,1)}, u32[]{:S(2)}) copy-start(bf16[2,4,3,512]{3,1,2,0:T(4,128)(2,1)} %param.11) | copy-start | bytes 73732
  0.0 15.7 %copy-start.6 = (s32[2,4,8]{2,1,0:T(4,128)S(1)}, s32[2,4,8]{2,1,0:T(4,128)}, u32[]{:S(2)}) copy-start(s32[2,4,8]{2,1,0:T(4,128)} %param.13) | copy-start | bytes 772
  3.1 6.8 %collective-permute-start.1 = (bf16[3,32,128]{2,1,0:T(8,128)(2,1)S(1)}, bf16[3,32,128]{2,1,0:T(8,128)(2,1)S(1)}, u32[]{:S(2)}, u32[]{:S(2)}) collective-permute-start(bf16[3,32,128]{2,1,0:T(8,128)(2,1)S(1)} %get-tuple-element.31.refs_5_), channel_id=1, source_target_pairs={{0,16},{16,0},{32,48},{48,32},{64,80},{80,64},{96,112},{112,96},{1... | collective-permute-start | bytes 73736 | tf_op jit(solution)/shard_map/ppermute | solution.py:31
  7.9 31.3 %collective-permute-start = (bf16[336,512]{1,0:T(8,128)(2,1)S(1)}, bf16[336,512]{1,0:T(8,128)(2,1)S(1)}, u32[]{:S(2)}, u32[]{:S(2)}) collective-permute-start(bf16[336,512]{1,0:T(8,128)(2,1)S(1)} %get-tuple-element.30), channel_id=1, source_target_pairs={{0,16},{16,0},{32,48},{48,32},{64,80},{80,64},{96,112},{112,96},{1... | collective-permute-start | bytes 1032200 | tf_op jit(solution)/shard_map/ppermute | solution.py:31
  9.9 9.2 %collective-permute-start.2 = (bf16[4,32,128]{2,1,0:T(8,128)(2,1)S(1)}, bf16[4,32,128]{2,1,0:T(8,128)(2,1)S(1)}, u32[]{:S(2)}, u32[]{:S(2)}) collective-permute-start(bf16[4,32,128]{2,1,0:T(8,128)(2,1)S(1)} %pad_maximum_fusion.3.refs_4_), channel_id=1, source_target_pairs={{0,32},{16,48},{32,0},{48,16},{64,96},{80,112},{96,64},{112,80},{1... | collective-permute-start | bytes 98312 | tf_op jit(solution)/shard_map/ppermute | solution.py:31
  19.2 12.6 %collective-permute-start.4 = (bf16[5,32,128]{2,1,0:T(8,128)(2,1)S(1)}, bf16[5,32,128]{2,1,0:T(8,128)(2,1)S(1)}, u32[]{:S(2)}, u32[]{:S(2)}) collective-permute-start(bf16[5,32,128]{2,1,0:T(8,128)(2,1)S(1)} %constant_dynamic-update-slice_fusion.refs_4_), channel_id=1, source_target_pairs={{0,96},{16,112},{32,64},{48,80},{64,32},{80,48},{96,0},{112,16},{1... | collective-permute-start | bytes 122888 | tf_op jit(solution)/shard_map/ppermute | solution.py:31
  27.7 11.5 %collective-permute-start.3 = (bf16[336,512]{1,0:T(8,128)(2,1)S(1)}, bf16[336,512]{1,0:T(8,128)(2,1)S(1)}, u32[]{:S(2)}, u32[]{:S(2)}) collective-permute-start(bf16[336,512]{1,0:T(8,128)(2,1)S(1)} %get-tuple-element.34), channel_id=1, source_target_pairs={{16,32},{32,16},{48,64},{64,48},{80,96},{96,80},{112,128},{128,112... | collective-permute-start | bytes 1032200 | tf_op jit(solution)/shard_map/ppermute | solution.py:37
  31.9 16.7 %copy-start.8 = (s32[1,1,3,25]{3,1,2,0:T(1,128)S(1)}, s32[1,1,3,25]{3,1,2,0:T(1,128)}, u32[]{:S(2)}) copy-start(s32[1,1,3,25]{3,1,2,0:T(1,128)} %param.18) | copy-start | bytes 904
  31.9 16.7 %copy-start.7 = (s32[2,4,25]{2,1,0:T(4,128)S(1)}, s32[2,4,25]{2,1,0:T(4,128)}, u32[]{:S(2)}) copy-start(s32[2,4,25]{2,1,0:T(4,128)} %param.15) | copy-start | bytes 2404
  31.9 12.8 %collective-permute-start.6 = (bf16[6,32,128]{2,1,0:T(8,128)(2,1)S(1)}, bf16[6,32,128]{2,1,0:T(8,128)(2,1)S(1)}, u32[]{:S(2)}, u32[]{:S(2)}) collective-permute-start(bf16[6,32,128]{2,1,0:T(8,128)(2,1)S(1)} %pad_maximum_fusion.2.refs_4_), channel_id=1, source_target_pairs={{128,256},{144,272},{160,288},{176,304},{192,320},{208,336},{224,3... | collective-permute-start | bytes 147464 | tf_op jit(solution)/shard_map/ppermute | solution.py:37
  32.5 12.1 %collective-permute-start.5 = (bf16[6,32,128]{2,1,0:T(8,128)(2,1)S(1)}, bf16[6,32,128]{2,1,0:T(8,128)(2,1)S(1)}, u32[]{:S(2)}, u32[]{:S(2)}) collective-permute-start(bf16[6,32,128]{2,1,0:T(8,128)(2,1)S(1)} %pad_maximum_fusion.2.refs_4_), channel_id=1, source_target_pairs={{0,128},{16,144},{32,160},{48,176},{64,192},{80,208},{96,224},{112... | collective-permute-start | bytes 147464 | tf_op jit(solution)/shard_map/ppermute | solution.py:31
  44.9 6.7 %collective-permute-start.7 = (bf16[496,512]{1,0:T(8,128)(2,1)S(1)}, bf16[496,512]{1,0:T(8,128)(2,1)S(1)}, u32[]{:S(2)}, u32[]{:S(2)}) collective-permute-start(bf16[496,512]{1,0:T(8,128)(2,1)S(1)} %get-tuple-element.39), channel_id=1, source_target_pairs={{0,1},{1,0},{2,3},{3,2},{4,5},{5,4},{6,7},{7,6},{8,9},{9,8},{10,11... | collective-permute-start | bytes 1523720 | tf_op jit(solution)/shard_map/ppermute | solution.py:31
  48.6 25.1 %collective-permute-start.8 = (bf16[416,512]{1,0:T(8,128)(2,1)S(1)}, bf16[416,512]{1,0:T(8,128)(2,1)S(1)}, u32[]{:S(2)}, u32[]{:S(2)}) collective-permute-start(bf16[416,512]{1,0:T(8,128)(2,1)S(1)} %get-tuple-element.40), channel_id=1, source_target_pairs={{1,2},{2,1},{3,4},{4,3},{5,6},{6,5},{7,8},{8,7},{9,10},{10,9},{11,... | collective-permute-start | bytes 1277960 | tf_op jit(solution)/shard_map/ppermute | solution.py:37
  51.7 22.1 %copy-start.2 = (bf16[2,4,64,1600]{3,2,1,0:T(8,128)(2,1)S(1)}, bf16[2,4,64,1600]{3,2,1,0:T(8,128)(2,1)}, u32[]{:S(2)}) copy-start(bf16[2,4,64,1600]{3,2,1,0:T(8,128)(2,1)} %param.14) | copy-start | bytes 4915204
  51.7 22.1 %copy-start.3 = (bf16[1,1,3,64,1600]{4,3,2,1,0:T(8,128)(2,1)S(1)}, bf16[1,1,3,64,1600]{4,3,2,1,0:T(8,128)(2,1)}, u32[]{:S(2)}) copy-start(bf16[1,1,3,64,1600]{4,3,2,1,0:T(8,128)(2,1)} %param.17) | copy-start | bytes 1843204
  51.7 22.1 %copy-start.4 = (bf16[2,4,64,512]{3,2,1,0:T(8,128)(2,1)S(1)}, bf16[2,4,64,512]{3,2,1,0:T(8,128)(2,1)}, u32[]{:S(2)}) copy-start(bf16[2,4,64,512]{3,2,1,0:T(8,128)(2,1)} %param.12) | copy-start | bytes 1572868
  51.7 22.1 %copy-start.5 = (bf16[2,4,64,64]{3,2,1,0:T(8,128)(2,1)S(1)}, bf16[2,4,64,64]{3,2,1,0:T(8,128)(2,1)}, u32[]{:S(2)}) copy-start(bf16[2,4,64,64]{3,2,1,0:T(8,128)(2,1)} %param.16) | copy-start | bytes 196612
  51.7 22.0 %collective-permute-start.10 = (bf16[128,512]{1,0:T(8,128)(2,1)S(1)}, bf16[128,512]{1,0:T(8,128)(2,1)S(1)}, u32[]{:S(2)}, u32[]{:S(2)}) collective-permute-start(bf16[128,512]{1,0:T(8,128)(2,1)S(1)} %pad_maximum_fusion.refs_4_), channel_id=1, source_target_pairs={{2,4},{3,5},{4,2},{5,3},{6,8},{7,9},{8,6},{9,7},{10,12},{11,13},{1... | collective-permute-start | bytes 393224 | tf_op jit(solution)/shard_map/ppermute | solution.py:37
  52.5 9.1 %collective-permute-start.9 = (bf16[128,512]{1,0:T(8,128)(2,1)S(1)}, bf16[128,512]{1,0:T(8,128)(2,1)S(1)}, u32[]{:S(2)}, u32[]{:S(2)}) collective-permute-start(bf16[128,512]{1,0:T(8,128)(2,1)S(1)} %pad_maximum_fusion.refs_4_), channel_id=1, source_target_pairs={{0,2},{1,3},{2,0},{3,1},{4,6},{5,7},{6,4},{7,5},{8,10},{9,11},{10,... | collective-permute-start | bytes 393224 | tf_op jit(solution)/shard_map/ppermute | solution.py:31
  61.6 17.8 %collective-permute-start.13 = (bf16[80,256]{1,0:T(8,128)(2,1)S(1)}, bf16[80,256]{1,0:T(8,128)(2,1)S(1)}, u32[]{:S(2)}, u32[]{:S(2)}) collective-permute-start(bf16[80,256]{1,0:T(8,128)(2,1)S(1)} %add_convert_fusion.1.refs_8_), channel_id=1, source_target_pairs={{0,10},{1,11},{2,8},{3,9},{4,14},{5,15},{6,12},{7,13},{8,2},{9,3},... | collective-permute-start | bytes 122888 | tf_op jit(solution)/shard_map/ppermute | solution.py:31
  69.2 10.2 %collective-permute-start.12 = (bf16[80,512]{1,0:T(8,128)(2,1)S(1)}, bf16[80,512]{1,0:T(8,128)(2,1)S(1)}, u32[]{:S(2)}, u32[]{:S(2)}) collective-permute-start(bf16[80,512]{1,0:T(8,128)(2,1)S(1)} %pad_maximum_fusion.1.refs_19_), channel_id=1, source_target_pairs={{4,8},{5,9},{6,10},{7,11},{8,4},{9,5},{10,6},{11,7},{20,24},{21,25... | collective-permute-start | bytes 245768 | tf_op jit(solution)/shard_map/ppermute | solution.py:37
  69.9 9.6 %collective-permute-start.11 = (bf16[80,512]{1,0:T(8,128)(2,1)S(1)}, bf16[80,512]{1,0:T(8,128)(2,1)S(1)}, u32[]{:S(2)}, u32[]{:S(2)}) collective-permute-start(bf16[80,512]{1,0:T(8,128)(2,1)S(1)} %pad_maximum_fusion.1.refs_19_), channel_id=1, source_target_pairs={{0,4},{1,5},{2,6},{3,7},{4,0},{5,1},{6,2},{7,3},{8,12},{9,13},{10,... | collective-permute-start | bytes 245768 | tf_op jit(solution)/shard_map/ppermute | solution.py:31

commit v4 on v3

--- a/solution.py
+++ b/solution.py
@@ -113,7 +113,8 @@
     ).astype(BF16)
 
 
-def near_pairs(pairs, mask, listed, target_feats, source_offs, source_charges, acc):
+def near_pairs(pairs, mask_copy, mask, listed, target_feats, source_offs, source_charges, acc):
+    mask_copy.wait()
     count = jnp.int32(0)
     for target, slot, source, row_off, col_off in pairs:
         listed[count] = target + 16 * source + 256 * (row_off + 1) + 1024 * (col_off + 1)
@@ -192,10 +193,11 @@
         loads.append(pltpu.make_async_copy(basis_hbm.at[rows], basis.at[rows], sems.at[4 + k]))
     loads.append(pltpu.make_async_copy(transfer_hbm, transfer, sems.at[8]))
     loads.append(pltpu.make_async_copy(parent_hbm, parent, sems.at[9]))
-    loads.append(pltpu.make_async_copy(offsets_hbm, offsets, sems.at[10]))
+    load_offsets = pltpu.make_async_copy(offsets_hbm, offsets, sems.at[10])
+    load_offsets.start()
     for load in loads:
         load.start()
-    loads[10].wait()
+    load_offsets.wait()
     offs = [[offsets[row, k].astype(F32) for k in range(3)] for row in range(2)]
     halves = [rows_of([offs[row][k % 3][k // 3 : k // 3 + 1] for k in range(12)], 16).astype(BF16) for row in range(2)]
     with_pair[ROW_OFFS:ROW_POLES, :] = jnp.where(side == 0, halves[1], halves[0])
@@ -237,12 +239,41 @@
                 offs[4 * row + col, k : k + 1, :] = values[col : col + 1]
 
 
-def inner_kernel(targets, mask, charges, offsets, feats, out, listed, offs, acc):
+def inner_kernel(targets, mask_in, charges, offsets, feats, out, mask, sem, listed, offs, acc):
+    mask_copy = pltpu.make_async_copy(mask_in, mask, sem)
+    mask_copy.start()
     own_offsets(offsets, offs)
     for target in targets:
         acc[target] = jnp.zeros((LOADS, PANELS), F32)
-    near_pairs(inner_pairs(targets), mask, listed, feats, offs, charges, acc)
+    near_pairs(inner_pairs(targets), mask_copy, mask, listed, feats, offs, charges, acc)
     out[...] = acc[targets[0] : targets[-1] + 1]
+
+
+def earliness():
+    row = lax.axis_index("row")
+    return jnp.where(row & 7 == 0, 2, jnp.where(row & 4 == 0, 1, 0))
+
+
+def early_inner_kernel(mask_in, charges, offsets, feats, out, *scratch):
+    ahead = earliness()
+    for count, targets in enumerate(((0, 1, 2), (0, 1, 2, 3, 4, 5), (0, 1, 2, 3, 4, 5, 6, 7))):
+
+        @pl.when(ahead == count)
+        def _():
+            inner_kernel(targets, mask_in, charges, offsets, feats, out.at[0 : len(targets)], *scratch)
+
+
+def late_inner_kernel(targets, limit, *refs):
+    @pl.when(earliness() < limit)
+    def _():
+        inner_kernel(targets, *refs)
+
+
+def inner_basis_kernel(mask_in, charges, offsets, feats, transfer, basis, out, moved_basis, *scratch):
+    for leaf in range(8):
+        moved = lax.dot_general(transfer[leaf], basis[leaf], TN, preferred_element_type=F32)
+        moved_basis[leaf] = moved.astype(BF16)
+    late_inner_kernel((6, 7), 2, mask_in, charges, offsets, feats, out, *scratch)
 
 
 def spread_offsets(packed, offs, base):
@@ -251,14 +282,16 @@
         offs[base + leaf, 0:3, :] = values[3 * leaf : 3 * leaf + 3]
 
 
-def row_kernel(mask, feats, paired_rows, across_rows, out, listed, offs, charges, acc):
+def row_kernel(mask_in, feats, paired_rows, across_rows, out, mask, sem, listed, offs, charges, acc):
+    mask_copy = pltpu.make_async_copy(mask_in, mask, sem)
+    mask_copy.start()
     place = place_bits()
     for side, buffer in ((1 - place[0], paired_rows), (place[0], across_rows)):
         spread_offsets(buffer[ROW_OFFS:ROW_POLES, :], offs, 4 * side)
         for col in range(4):
             charges[4 * side + col] = buffer[64 * col : 64 * (col + 1), :]
     acc[...] = jnp.zeros_like(acc)
-    near_pairs(row_pairs(), mask, listed, feats, offs, charges, acc)
+    near_pairs(row_pairs(), mask_copy, mask, listed, feats, offs, charges, acc)
     out[...] = acc[...]
 
 
@@ -360,19 +393,29 @@
 
 
 def edge_kernel(
-    mask, feats, paired_cols, across_cols, inner0, inner1, inner2, by_rows, poles, paired_rows, across_rows, flags, coupling,
-    box_coupling, boxes, pair2, across2, transfer, basis,
-    out, box_out, moved_basis, listed, offs, charges, acc, table, window, local,
+    mask_in, feats, paired_cols, across_cols, inner0, inner1, inner2, by_rows, poles, paired_rows, across_rows, flags, coupling,
+    box_coupling, boxes, pair2, across2, basis,
+    out, box_out, mask, sem, listed, offs, charges, acc, table, window, local,
 ):
+    mask_copy = pltpu.make_async_copy(mask_in, mask, sem)
+    mask_copy.start()
     place = place_bits()
     for side, buffer in ((1 - place[1], paired_cols), (place[1], across_cols)):
         spread_offsets(buffer[COL_OFFS:COL_POLES, :], offs, 4 * side)
         for spot in range(4):
             charges[4 * side + spot] = buffer[64 * spot : 64 * (spot + 1), :]
-    acc[0:3] = inner0[...] + by_rows[0:3]
-    acc[3:6] = inner1[...] + by_rows[3:6]
-    acc[6:8] = inner2[...] + by_rows[6:8]
-    near_pairs(col_pairs(), mask, listed, feats, offs, charges, acc)
+    acc[0:3] = inner0[0:3] + by_rows[0:3]
+
+    for first, last, late, limit in ((3, 6, inner1, 1), (6, 8, inner2, 2)):
+
+        @pl.when(earliness() >= limit)
+        def _():
+            acc[first:last] = inner0[first:last] + by_rows[first:last]
+
+        @pl.when(earliness() < limit)
+        def _():
+            acc[first:last] = late[...] + by_rows[first:last]
+
 
     def put(row, pair, both):
         table[row, 128 * pair : 128 * pair + 64, :] = both[:, :64]
@@ -421,9 +464,7 @@
             seen = jnp.concatenate([table[row + a, 64 * col : 64 * (col + 5), :] for a in range(5)], axis=0)
             local[leaf] = box_product(coupling[leaf], spread[leaf : leaf + 1], seen).astype(BF16)
     box_out[...] = box_product(box_coupling[0], spread[8:9], window[...])
-    for leaf in range(8):
-        moved = lax.dot_general(transfer[leaf], basis[leaf], TN, preferred_element_type=F32)
-        moved_basis[leaf] = moved.astype(BF16)
+    near_pairs(col_pairs(), mask_copy, mask, listed, feats, offs, charges, acc)
     for leaf in range(8):
         far = lax.dot_general(local[leaf], basis[leaf], TN, preferred_element_type=F32)
         out[leaf] = acc[leaf] + far
@@ -469,6 +510,8 @@
 
 def near_scratch(sources):
     return [
+        pltpu.SMEM((8, 8), jnp.int32),
+        pltpu.SemaphoreType.DMA(()),
         pltpu.SMEM((32,), jnp.int32),
         pltpu.VMEM((8, 8, PANELS), F32),
         *([pltpu.VMEM((8, LOADS, PANELS), BF16)] if sources else []),
@@ -517,29 +560,29 @@
     paired_rows = paired(rows_pair, "row", 1)
     near_args = (mask, charges, offsets, feats)
 
-    def inner_call(targets, name, after):
+    def inner_call(kernel, count, name, after):
         return kernel_call(
-            functools.partial(inner_kernel, targets), shape((len(targets), LOADS, PANELS), F32),
-            near_scratch(False), name, near_cost, *near_args, smem=(0,), after=after,
+            kernel, shape((count, LOADS, PANELS), F32),
+            near_scratch(False), name, near_cost, *near_args, after=after,
         )
 
     halves = (small[1:3].astype(F32) + pair1[1:3].astype(F32)).astype(BF16)
     payload = jnp.concatenate([small[:1], pair1[:1], halves], axis=0)
     pair2 = paired(payload, "row", 2)
-    inner0 = inner_call((0, 1, 2), "inner0", (payload,))
+    inner0 = inner_call(early_inner_kernel, 8, "inner0", (payload,))
     pair2, inner0 = lax.optimization_barrier((pair2, inner0))
     quarter = (small[2].astype(F32) + pair1[2].astype(F32) + pair2[3].astype(F32)).astype(BF16)
     payload = jnp.concatenate([pair2[2:3], quarter[None], small[:1], pair1[:1], halves[:1]], axis=0)
     pair4 = paired(payload, "row", 6)
     payload, rows_across = lax.optimization_barrier((payload, rows_across))
     across_rows = paired_across(rows_across, "row", 1)
-    inner1 = inner_call((3, 4, 5), "inner1", (payload,))
+    inner1 = inner_call(functools.partial(late_inner_kernel, (3, 4, 5), 1), 3, "inner1", (payload,))
     pair4, inner1 = lax.optimization_barrier((pair4, inner1))
     payload = jnp.concatenate([quarter[None], pair4[1:2], pair4[0:1], pair4[2:5]], axis=0)
     pair8, across8 = paired(payload, "row", 8), paired_across(payload, "row", 8)
     by_rows = kernel_call(
         row_kernel, shape((8, LOADS, PANELS), F32), near_scratch(True), "byrows", near_cost,
-        mask, feats, paired_rows, across_rows, smem=(0,), after=(payload,),
+        mask, feats, paired_rows, across_rows, after=(payload,),
     )
 
     pair8, across8, by_rows = lax.optimization_barrier((pair8, across8, by_rows))
@@ -555,20 +598,23 @@
     sums = (row_sums.astype(F32) + paired_cols[COL_ALL:].astype(F32)).astype(BF16)
     payload = jnp.concatenate([boxes1, sums], axis=0)
     col_pair2, col_across2 = paired(payload, "col", 2), paired_across(payload, "col", 2)
-    inner2 = inner_call((6, 7), "inner2", (payload,))
+    inner2, moved_basis = kernel_call(
+        inner_basis_kernel, (shape((2, LOADS, PANELS), F32), shape((8, RANK, PANELS))), near_scratch(False), "inner2",
+        near_cost, *near_args, transfer, basis, after=(payload,),
+    )
     col_pair2, inner2 = lax.optimization_barrier((col_pair2, inner2))
     boxes3 = (sums[:, 256:].astype(F32) + col_pair2[48:, 256:].astype(F32)).astype(BF16)
     payload = jnp.concatenate([sums[:, :256], boxes3], axis=1)
     col_pair4, col_across4 = paired(payload, "col", 4), paired_across(payload, "col", 4)
     col_pair8 = paired(boxes3, "col", 10)
-    direct, box_one, moved_basis = kernel_call(
+    direct, box_one = kernel_call(
         edge_kernel,
-        (shape((8, LOADS, PANELS), F32), shape((RANK, LOADS), F32), shape((8, RANK, PANELS))),
+        (shape((8, LOADS, PANELS), F32), shape((RANK, LOADS), F32)),
         near_scratch(True)
         + [pltpu.VMEM((6, 512, LOADS), BF16), pltpu.VMEM((WIDE, LOADS), BF16), pltpu.VMEM((8, RANK, LOADS), BF16)],
         "edge", near_cost, mask, feats, paired_cols, across_cols, inner0, inner1, inner2, by_rows, poles,
-        paired_rows, across_rows, flags, coupling, box_coupling, boxes1, col_pair2, col_across2, transfer, basis,
-        smem=(0,), after=(payload,),
+        paired_rows, across_rows, flags, coupling, box_coupling, boxes1, col_pair2, col_across2, basis,
+        after=(payload,),
     )
     out = kernel_call(
         last_kernel, shape((8, LOADS, PANELS)),

time: 81.7 us -> 80.3 us (0.983)
  the two profiles are of different devices: /device:TPU:1 before, /device:TPU:2 now
where the time goes in v4:
time: 80.3 us; the launch traced here: 79.8 us
  starting transfers between devices  47.1 us (59%)
  Pallas kernels  22.3 us (28%)
  waiting for transfers between devices  9.47 us (12%)
    ppermute x9, starting transfers between devices, paired(): lax.ppermute(value, axis, [(i, i ^ distance) for i in range(lax.axis_size...  40.9 us
    pallas_call x8, Pallas kernels, kernel_call(): pl.pallas_call(with_order, out_shape=outs, in_specs=spaces + [VMEM] * len...  22.3 us
    ppermute x9, waiting for transfers between devices, paired(): lax.ppermute(value, axis, [(i, i ^ distance) for i in range(lax.axis_size...  7.39 us
    ppermute x5, starting transfers between devices, paired_across(): lax.ppermute(value, axis, [(i, j) for i, j in moves if 0 <= j < count])  6.21 us
    ppermute x5, waiting for transfers between devices, paired_across(): lax.ppermute(value, axis, [(i, j) for i, j in moves if 0 <= j < count])  2.07 us
  transfers between devices with their start and end apart: 14, of which 4 were waited for; matrix products, arithmetic and copies ran while one was open for 0% of the time, Pallas kernels for 23%

profile of v4, /device:TPU:2, one launch (start us, length us, event | category | flops | bytes accessed | tf_op | source)
XLA Modules:
  0.0 79.8 jit_solution(9563752876457801583)
XLA Ops:
  0.0 2.6 %first.1 = (bf16[336,512]{1,0:T(8,128)(2,1)S(1)}, bf16[336,512]{1,0:T(8,128)(2,1)S(1)}, bf16[3,32,128]{2,1,0:T(8,128)(2,1)S(1)}, bf16[4,64,128]{2,1,0:T(8,128)(2,1)S(1)}, bf16[8,512,16]{2,1,0:T(8,128)(2,1)S(1)}) custom-call(bf16[8,64,512]{2,1,0:T(8,128)(2,1)} %bitcast.13, bf16[2,3,4,512]{3,2,1,0:T(4,128)(2,1)} %bitcast.18, bf16[8,64,512]{2,1,0:T(8,128)(2,1)} %bitcast.26, ...), custom_call_target="tpu_custom_call" | custom-call | flops 1000000000 | bytes 4194304 | tf_op jit(solution)/shard_map/first/pallas_call | solution.py:47
  2.6 4.3 %collective-permute-start.1 = (bf16[3,32,128]{2,1,0:T(8,128)(2,1)S(1)}, bf16[3,32,128]{2,1,0:T(8,128)(2,1)S(1)}, u32[]{:S(2)}, u32[]{:S(2)}) collective-permute-start(bf16[3,32,128]{2,1,0:T(8,128)(2,1)S(1)} %get-tuple-element.32.refs_5_), channel_id=1, source_target_pairs={{0,16},{16,0},{32,48},{48,32},{64,80},{80,64},{96,112},{112,96},{1... | collective-permute-start | bytes 73736 | tf_op jit(solution)/shard_map/ppermute | solution.py:31
  6.9 1.9 %collective-permute-start = (bf16[336,512]{1,0:T(8,128)(2,1)S(1)}, bf16[336,512]{1,0:T(8,128)(2,1)S(1)}, u32[]{:S(2)}, u32[]{:S(2)}) collective-permute-start(bf16[336,512]{1,0:T(8,128)(2,1)S(1)} %get-tuple-element.31), channel_id=1, source_target_pairs={{0,16},{16,0},{32,48},{48,32},{64,80},{80,64},{96,112},{112,96},{1... | collective-permute-start | bytes 1032200 | tf_op jit(solution)/shard_map/ppermute | solution.py:31
  8.9 0.0 collective-permute-done.1.refs_6_
  8.9 6.1 %collective-permute-start.2 = (bf16[4,32,128]{2,1,0:T(8,128)(2,1)S(1)}, bf16[4,32,128]{2,1,0:T(8,128)(2,1)S(1)}, u32[]{:S(2)}, u32[]{:S(2)}) collective-permute-start(bf16[4,32,128]{2,1,0:T(8,128)(2,1)S(1)} %pad_maximum_fusion.3.refs_4_), channel_id=1, source_target_pairs={{0,32},{16,48},{32,0},{48,16},{64,96},{80,112},{96,64},{112,80},{1... | collective-permute-start | bytes 98312 | tf_op jit(solution)/shard_map/ppermute | solution.py:31
  15.0 0.0 copy-done
  15.0 0.0 copy-done.1
  15.0 0.0 copy-done.6
  15.0 10.0 %inner0.1.refs_4_ = f32[8,64,512]{2,1,0:T(8,128)S(1)} custom-call(s32[8,8]{1,0:T(8,128)S(1)} %bitcast.31, bf16[8,64,512]{2,1,0:T(8,128)(2,1)S(1)} %bitcast.14, bf16[2,3,4,512]{3,2,1,0:T(4,128)(2,1)S(1)} %bitcast.19, bf16[8,512,16]{2,1,0:T(8,128)(2,1)S(1)} %get-tuple-element.29.refs_3_.refs_1_, bf16[4,32,128]{2,1,0:T(8,128)(2,1)S(1)} %pad_maximum_fusion.3.refs_4_), custom_call_target="tpu_custom_call" | custom-call | flops 6000000000 | bytes 4194304 | tf_op jit(solution)/shard_map/inner0/pallas_call | solution.py:47
  25.1 0.0 collective-permute-done.2.refs_7_
  25.1 3.1 %collective-permute-start.4 = (bf16[5,32,128]{2,1,0:T(8,128)(2,1)S(1)}, bf16[5,32,128]{2,1,0:T(8,128)(2,1)S(1)}, u32[]{:S(2)}, u32[]{:S(2)}) collective-permute-start(bf16[5,32,128]{2,1,0:T(8,128)(2,1)S(1)} %constant_dynamic-update-slice_fusion.refs_4_), channel_id=1, source_target_pairs={{0,96},{16,112},{32,64},{48,80},{64,32},{80,48},{96,0},{112,16},{1... | collective-permute-start | bytes 122888 | tf_op jit(solution)/shard_map/ppermute | solution.py:31
  28.2 1.9 %collective-permute-start.3 = (bf16[336,512]{1,0:T(8,128)(2,1)S(1)}, bf16[336,512]{1,0:T(8,128)(2,1)S(1)}, u32[]{:S(2)}, u32[]{:S(2)}) collective-permute-start(bf16[336,512]{1,0:T(8,128)(2,1)S(1)} %get-tuple-element.35), channel_id=1, source_target_pairs={{16,32},{32,16},{48,64},{64,48},{80,96},{96,80},{112,128},{128,112... | collective-permute-start | bytes 1032200 | tf_op jit(solution)/shard_map/ppermute | solution.py:37
  30.2 3.0 %collective-permute-done.4.refs_8_ = bf16[5,32,128]{2,1,0:T(8,128)(2,1)S(1)} collective-permute-done((bf16[5,32,128]{2,1,0:T(8,128)(2,1)S(1)}, bf16[5,32,128]{2,1,0:T(8,128)(2,1)S(1)}, u32[]{:S(2)}, u32[]{:S(2)}) %collective-permute-start.4) | collective-permute-done | bytes 40992 | tf_op jit(solution)/shard_map/ppermute | solution.py:31
  33.2 0.0 copy-start.8
  33.2 0.0 copy-start.7
  33.2 2.1 %collective-permute-start.6 = (bf16[6,32,128]{2,1,0:T(8,128)(2,1)S(1)}, bf16[6,32,128]{2,1,0:T(8,128)(2,1)S(1)}, u32[]{:S(2)}, u32[]{:S(2)}) collective-permute-start(bf16[6,32,128]{2,1,0:T(8,128)(2,1)S(1)} %pad_maximum_fusion.2.refs_4_), channel_id=1, source_target_pairs={{128,256},{144,272},{160,288},{176,304},{192,320},{208,336},{224,3... | collective-permute-start | bytes 147464 | tf_op jit(solution)/shard_map/ppermute | solution.py:37
  35.3 3.4 %collective-permute-start.5 = (bf16[6,32,128]{2,1,0:T(8,128)(2,1)S(1)}, bf16[6,32,128]{2,1,0:T(8,128)(2,1)S(1)}, u32[]{:S(2)}, u32[]{:S(2)}) collective-permute-start(bf16[6,32,128]{2,1,0:T(8,128)(2,1)S(1)} %pad_maximum_fusion.2.refs_4_), channel_id=1, source_target_pairs={{0,128},{16,144},{32,160},{48,176},{64,192},{80,208},{96,224},{112... | collective-permute-start | bytes 147464 | tf_op jit(solution)/shard_map/ppermute | solution.py:31
  38.7 0.0 collective-permute-done.refs_2_.refs_3_.refs_9_
  38.7 2.1 %collective-permute-done.3.refs_3_.refs_4_.refs_10_ = bf16[336,512]{1,0:T(8,128)(2,1)S(1)} collective-permute-done((bf16[336,512]{1,0:T(8,128)(2,1)S(1)}, bf16[336,512]{1,0:T(8,128)(2,1)S(1)}, u32[]{:S(2)}, u32[]{:S(2)}) %collective-permute-start.3) | collective-permute-done | bytes 344096 | tf_op jit(solution)/shard_map/ppermute | solution.py:37
  40.8 3.3 %byrows.1.refs_7_ = f32[8,64,512]{2,1,0:T(8,128)S(1)} custom-call(s32[8,8]{1,0:T(8,128)S(1)} %bitcast.33, bf16[8,512,16]{2,1,0:T(8,128)(2,1)S(1)} %get-tuple-element.29.refs_3_.refs_1_, bf16[336,512]{1,0:T(8,128)(2,1)S(1)} %collective-permute-done.refs_2_.refs_3_.refs_9_, bf16[336,512]{1,0:T(8,128)(2,1)S(1)} %collective-permute-done.3.refs_3_.refs_4_.refs_10_, ...), custom_call_target="tpu_custom_call" | custom-call | flops 6000000000 | bytes 4194304 | tf_op jit(solution)/shard_map/byrows/pallas_call | solution.py:47
  44.1 0.0 copy-start.4
  44.1 0.0 copy-start.5
  44.1 0.0 collective-permute-done.6.refs_10_
  44.1 0.0 collective-permute-done.5.refs_9_
  44.1 0.2 pack.1
  44.3 1.9 %collective-permute-start.7 = (bf16[496,512]{1,0:T(8,128)(2,1)S(1)}, bf16[496,512]{1,0:T(8,128)(2,1)S(1)}, u32[]{:S(2)}, u32[]{:S(2)}) collective-permute-start(bf16[496,512]{1,0:T(8,128)(2,1)S(1)} %get-tuple-element.40), channel_id=1, source_target_pairs={{0,1},{1,0},{2,3},{3,2},{4,5},{5,4},{6,7},{7,6},{8,9},{9,8},{10,11... | collective-permute-start | bytes 1523720 | tf_op jit(solution)/shard_map/ppermute | solution.py:31
  46.2 0.0 copy-done.8
  46.3 0.0 copy-done.7
  46.3 0.7 collective-permute-start.8
  47.0 1.1 %collective-permute-done.7.refs_2_ = bf16[496,512]{1,0:T(8,128)(2,1)S(1)} collective-permute-done((bf16[496,512]{1,0:T(8,128)(2,1)S(1)}, bf16[496,512]{1,0:T(8,128)(2,1)S(1)}, u32[]{:S(2)}, u32[]{:S(2)}) %collective-permute-start.7) | collective-permute-done | bytes 507936 | tf_op jit(solution)/shard_map/ppermute | solution.py:31
  48.1 0.0 copy-start.2
  48.1 0.0 copy-start.3
  48.2 0.8 %collective-permute-start.10 = (bf16[128,512]{1,0:T(8,128)(2,1)S(1)}, bf16[128,512]{1,0:T(8,128)(2,1)S(1)}, u32[]{:S(2)}, u32[]{:S(2)}) collective-permute-start(bf16[128,512]{1,0:T(8,128)(2,1)S(1)} %pad_maximum_fusion.refs_6_), channel_id=1, source_target_pairs={{2,4},{3,5},{4,2},{5,3},{6,8},{7,9},{8,6},{9,7},{10,12},{11,13},{1... | collective-permute-start | bytes 393224 | tf_op jit(solution)/shard_map/ppermute | solution.py:37
  49.0 8.5 %collective-permute-start.9 = (bf16[128,512]{1,0:T(8,128)(2,1)S(1)}, bf16[128,512]{1,0:T(8,128)(2,1)S(1)}, u32[]{:S(2)}, u32[]{:S(2)}) collective-permute-start(bf16[128,512]{1,0:T(8,128)(2,1)S(1)} %pad_maximum_fusion.refs_6_), channel_id=1, source_target_pairs={{0,2},{1,3},{2,0},{3,1},{4,6},{5,7},{6,4},{7,5},{8,10},{9,11},{10,... | collective-permute-start | bytes 393224 | tf_op jit(solution)/shard_map/ppermute | solution.py:31
  57.4 0.6 inner2.1
  58.0 3.3 %collective-permute-done.9.refs_15_.refs_6_ = bf16[128,512]{1,0:T(8,128)(2,1)S(1)} collective-permute-done((bf16[128,512]{1,0:T(8,128)(2,1)S(1)}, bf16[128,512]{1,0:T(8,128)(2,1)S(1)}, u32[]{:S(2)}, u32[]{:S(2)}) %collective-permute-start.9) | collective-permute-done | bytes 131104 | tf_op jit(solution)/shard_map/ppermute | solution.py:31
  61.4 6.6 %collective-permute-start.13 = (bf16[80,256]{1,0:T(8,128)(2,1)S(1)}, bf16[80,256]{1,0:T(8,128)(2,1)S(1)}, u32[]{:S(2)}, u32[]{:S(2)}) collective-permute-start(bf16[80,256]{1,0:T(8,128)(2,1)S(1)} %add_convert_fusion.1.refs_8_), channel_id=1, source_target_pairs={{0,10},{1,11},{2,8},{3,9},{4,14},{5,15},{6,12},{7,13},{8,2},{9,3},... | collective-permute-start | bytes 122888 | tf_op jit(solution)/shard_map/ppermute | solution.py:31
  68.0 0.7 collective-permute-start.12
  68.7 5.2 %collective-permute-start.11 = (bf16[80,512]{1,0:T(8,128)(2,1)S(1)}, bf16[80,512]{1,0:T(8,128)(2,1)S(1)}, u32[]{:S(2)}, u32[]{:S(2)}) collective-permute-start(bf16[80,512]{1,0:T(8,128)(2,1)S(1)} %pad_maximum_fusion.1.refs_18_), channel_id=1, source_target_pairs={{0,4},{1,5},{2,6},{3,7},{4,0},{5,1},{6,2},{7,3},{8,12},{9,13},{10,... | collective-permute-start | bytes 245768 | tf_op jit(solution)/shard_map/ppermute | solution.py:31
  73.9 0.0 collective-permute-done.8.refs_3_
  73.9 0.0 collective-permute-done.10.refs_16_.refs_7_
  73.9 0.0 copy-done.2
  73.9 0.0 copy-done.3
  73.9 4.0 %edge.1 = (f32[8,64,512]{2,1,0:T(8,128)S(1)}, f32[64,64]{1,0:T(8,128)S(1)}) custom-call(s32[8,8]{1,0:T(8,128)S(1)} %bitcast.35, bf16[8,512,16]{2,1,0:T(8,128)(2,1)S(1)} %get-tuple-element.29.refs_3_.refs_1_, bf16[496,512]{1,0:T(8,128)(2,1)S(1)} %collective-permute-done.7.refs_2_, bf16[416,512]{1,0:T(8,128)(2,1)S(1)} %collective-permute-done.8.refs_3_, ...), custom_call_target="tpu_custom_call" | custom-call | flops 6000000000 | bytes 4194304 | tf_op jit(solution)/shard_map/edge/pallas_call | solution.py:47
  78.0 0.0 collective-permute-done.13.refs_11_
  78.0 0.0 collective-permute-done.12.refs_10_
  78.0 0.0 collective-permute-done.11.refs_9_
  78.0 1.6 %last.1 = bf16[8,64,512]{2,1,0:T(8,128)(2,1)} custom-call(f32[8,64,512]{2,1,0:T(8,128)S(1)} %get-tuple-element.50.refs_0_, f32[64,64]{1,0:T(8,128)S(1)} %get-tuple-element.51.refs_1_, bf16[16,32]{1,0:T(8,128)(2,1)S(1)} %fusion.5.refs_11_.refs_2_, bf16[3,64,1600]{2,1,0:T(8,128)(2,1)S(1)} %bitcast.25, bf16[8,64,512]{2,1,0:T(8,128)(2,1)S(1)} %get-tuple-element.52.refs_4_, ...), custom_call_target="tpu_custom_call" | custom-call | flops 1000000000 | bytes 4194304 | tf_op jit(solution)/shard_map/last/pallas_call | solution.py:47
  (27 shorter events, 0.2 us)
Async XLA Ops:
  0.0 15.0 %copy-start = (bf16[2,4,64,512]{3,2,1,0:T(8,128)(2,1)S(1)}, bf16[2,4,64,512]{3,2,1,0:T(8,128)(2,1)}, u32[]{:S(2)}) copy-start(bf16[2,4,64,512]{3,2,1,0:T(8,128)(2,1)} %param.10) | copy-start | bytes 1572868
  0.0 15.0 %copy-start.1 = (bf16[2,4,3,512]{3,1,2,0:T(4,128)(2,1)S(1)}, bf16[2,4,3,512]{3,1,2,0:T(4,128)(2,1)}, u32[]{:S(2)}) copy-start(bf16[2,4,3,512]{3,1,2,0:T(4,128)(2,1)} %param.11) | copy-start | bytes 73732
  0.0 15.0 %copy-start.6 = (s32[2,4,8]{2,1,0:T(4,128)S(1)}, s32[2,4,8]{2,1,0:T(4,128)}, u32[]{:S(2)}) copy-start(s32[2,4,8]{2,1,0:T(4,128)} %param.13) | copy-start | bytes 772
  2.6 6.2 %collective-permute-start.1 = (bf16[3,32,128]{2,1,0:T(8,128)(2,1)S(1)}, bf16[3,32,128]{2,1,0:T(8,128)(2,1)S(1)}, u32[]{:S(2)}, u32[]{:S(2)}) collective-permute-start(bf16[3,32,128]{2,1,0:T(8,128)(2,1)S(1)} %get-tuple-element.32.refs_5_), channel_id=1, source_target_pairs={{0,16},{16,0},{32,48},{48,32},{64,80},{80,64},{96,112},{112,96},{1... | collective-permute-start | bytes 73736 | tf_op jit(solution)/shard_map/ppermute | solution.py:31
  6.9 31.8 %collective-permute-start = (bf16[336,512]{1,0:T(8,128)(2,1)S(1)}, bf16[336,512]{1,0:T(8,128)(2,1)S(1)}, u32[]{:S(2)}, u32[]{:S(2)}) collective-permute-start(bf16[336,512]{1,0:T(8,128)(2,1)S(1)} %get-tuple-element.31), channel_id=1, source_target_pairs={{0,16},{16,0},{32,48},{48,32},{64,80},{80,64},{96,112},{112,96},{1... | collective-permute-start | bytes 1032200 | tf_op jit(solution)/shard_map/ppermute | solution.py:31
  8.9 16.2 %collective-permute-start.2 = (bf16[4,32,128]{2,1,0:T(8,128)(2,1)S(1)}, bf16[4,32,128]{2,1,0:T(8,128)(2,1)S(1)}, u32[]{:S(2)}, u32[]{:S(2)}) collective-permute-start(bf16[4,32,128]{2,1,0:T(8,128)(2,1)S(1)} %pad_maximum_fusion.3.refs_4_), channel_id=1, source_target_pairs={{0,32},{16,48},{32,0},{48,16},{64,96},{80,112},{96,64},{112,80},{1... | collective-permute-start | bytes 98312 | tf_op jit(solution)/shard_map/ppermute | solution.py:31
  25.1 8.0 %collective-permute-start.4 = (bf16[5,32,128]{2,1,0:T(8,128)(2,1)S(1)}, bf16[5,32,128]{2,1,0:T(8,128)(2,1)S(1)}, u32[]{:S(2)}, u32[]{:S(2)}) collective-permute-start(bf16[5,32,128]{2,1,0:T(8,128)(2,1)S(1)} %constant_dynamic-update-slice_fusion.refs_4_), channel_id=1, source_target_pairs={{0,96},{16,112},{32,64},{48,80},{64,32},{80,48},{96,0},{112,16},{1... | collective-permute-start | bytes 122888 | tf_op jit(solution)/shard_map/ppermute | solution.py:31
  28.2 12.6 %collective-permute-start.3 = (bf16[336,512]{1,0:T(8,128)(2,1)S(1)}, bf16[336,512]{1,0:T(8,128)(2,1)S(1)}, u32[]{:S(2)}, u32[]{:S(2)}) collective-permute-start(bf16[336,512]{1,0:T(8,128)(2,1)S(1)} %get-tuple-element.35), channel_id=1, source_target_pairs={{16,32},{32,16},{48,64},{64,48},{80,96},{96,80},{112,128},{128,112... | collective-permute-start | bytes 1032200 | tf_op jit(solution)/shard_map/ppermute | solution.py:37
  33.2 13.0 %copy-start.8 = (s32[1,1,3,25]{3,1,2,0:T(1,128)S(1)}, s32[1,1,3,25]{3,1,2,0:T(1,128)}, u32[]{:S(2)}) copy-start(s32[1,1,3,25]{3,1,2,0:T(1,128)} %param.18) | copy-start | bytes 904
  33.2 13.1 %copy-start.7 = (s32[2,4,25]{2,1,0:T(4,128)S(1)}, s32[2,4,25]{2,1,0:T(4,128)}, u32[]{:S(2)}) copy-start(s32[2,4,25]{2,1,0:T(4,128)} %param.15) | copy-start | bytes 2404
  33.2 10.9 %collective-permute-start.6 = (bf16[6,32,128]{2,1,0:T(8,128)(2,1)S(1)}, bf16[6,32,128]{2,1,0:T(8,128)(2,1)S(1)}, u32[]{:S(2)}, u32[]{:S(2)}) collective-permute-start(bf16[6,32,128]{2,1,0:T(8,128)(2,1)S(1)} %pad_maximum_fusion.2.refs_4_), channel_id=1, source_target_pairs={{128,256},{144,272},{160,288},{176,304},{192,320},{208,336},{224,3... | collective-permute-start | bytes 147464 | tf_op jit(solution)/shard_map/ppermute | solution.py:37
  35.3 8.8 %collective-permute-start.5 = (bf16[6,32,128]{2,1,0:T(8,128)(2,1)S(1)}, bf16[6,32,128]{2,1,0:T(8,128)(2,1)S(1)}, u32[]{:S(2)}, u32[]{:S(2)}) collective-permute-start(bf16[6,32,128]{2,1,0:T(8,128)(2,1)S(1)} %pad_maximum_fusion.2.refs_4_), channel_id=1, source_target_pairs={{0,128},{16,144},{32,160},{48,176},{64,192},{80,208},{96,224},{112... | collective-permute-start | bytes 147464 | tf_op jit(solution)/shard_map/ppermute | solution.py:31
  44.1 13.3 %copy-start.4 = (bf16[2,4,64,512]{3,2,1,0:T(8,128)(2,1)S(1)}, bf16[2,4,64,512]{3,2,1,0:T(8,128)(2,1)}, u32[]{:S(2)}) copy-start(bf16[2,4,64,512]{3,2,1,0:T(8,128)(2,1)} %param.12) | copy-start | bytes 1572868
  44.1 13.3 %copy-start.5 = (bf16[2,4,64,64]{3,2,1,0:T(8,128)(2,1)S(1)}, bf16[2,4,64,64]{3,2,1,0:T(8,128)(2,1)}, u32[]{:S(2)}) copy-start(bf16[2,4,64,64]{3,2,1,0:T(8,128)(2,1)} %param.16) | copy-start | bytes 196612
  44.3 3.8 %collective-permute-start.7 = (bf16[496,512]{1,0:T(8,128)(2,1)S(1)}, bf16[496,512]{1,0:T(8,128)(2,1)S(1)}, u32[]{:S(2)}, u32[]{:S(2)}) collective-permute-start(bf16[496,512]{1,0:T(8,128)(2,1)S(1)} %get-tuple-element.40), channel_id=1, source_target_pairs={{0,1},{1,0},{2,3},{3,2},{4,5},{5,4},{6,7},{7,6},{8,9},{9,8},{10,11... | collective-permute-start | bytes 1523720 | tf_op jit(solution)/shard_map/ppermute | solution.py:31
  46.3 27.6 %collective-permute-start.8 = (bf16[416,512]{1,0:T(8,128)(2,1)S(1)}, bf16[416,512]{1,0:T(8,128)(2,1)S(1)}, u32[]{:S(2)}, u32[]{:S(2)}) collective-permute-start(bf16[416,512]{1,0:T(8,128)(2,1)S(1)} %get-tuple-element.41), channel_id=1, source_target_pairs={{1,2},{2,1},{3,4},{4,3},{5,6},{6,5},{7,8},{8,7},{9,10},{10,9},{11,... | collective-permute-start | bytes 1277960 | tf_op jit(solution)/shard_map/ppermute | solution.py:37
  48.1 25.8 %copy-start.2 = (bf16[2,4,64,1600]{3,2,1,0:T(8,128)(2,1)S(1)}, bf16[2,4,64,1600]{3,2,1,0:T(8,128)(2,1)}, u32[]{:S(2)}) copy-start(bf16[2,4,64,1600]{3,2,1,0:T(8,128)(2,1)} %param.14) | copy-start | bytes 4915204
  48.1 25.8 %copy-start.3 = (bf16[1,1,3,64,1600]{4,3,2,1,0:T(8,128)(2,1)S(1)}, bf16[1,1,3,64,1600]{4,3,2,1,0:T(8,128)(2,1)}, u32[]{:S(2)}) copy-start(bf16[1,1,3,64,1600]{4,3,2,1,0:T(8,128)(2,1)} %param.17) | copy-start | bytes 1843204
  48.2 25.7 %collective-permute-start.10 = (bf16[128,512]{1,0:T(8,128)(2,1)S(1)}, bf16[128,512]{1,0:T(8,128)(2,1)S(1)}, u32[]{:S(2)}, u32[]{:S(2)}) collective-permute-start(bf16[128,512]{1,0:T(8,128)(2,1)S(1)} %pad_maximum_fusion.refs_6_), channel_id=1, source_target_pairs={{2,4},{3,5},{4,2},{5,3},{6,8},{7,9},{8,6},{9,7},{10,12},{11,13},{1... | collective-permute-start | bytes 393224 | tf_op jit(solution)/shard_map/ppermute | solution.py:37
  49.0 12.4 %collective-permute-start.9 = (bf16[128,512]{1,0:T(8,128)(2,1)S(1)}, bf16[128,512]{1,0:T(8,128)(2,1)S(1)}, u32[]{:S(2)}, u32[]{:S(2)}) collective-permute-start(bf16[128,512]{1,0:T(8,128)(2,1)S(1)} %pad_maximum_fusion.refs_6_), channel_id=1, source_target_pairs={{0,2},{1,3},{2,0},{3,1},{4,6},{5,7},{6,4},{7,5},{8,10},{9,11},{10,... | collective-permute-start | bytes 393224 | tf_op jit(solution)/shard_map/ppermute | solution.py:31
  61.4 16.6 %collective-permute-start.13 = (bf16[80,256]{1,0:T(8,128)(2,1)S(1)}, bf16[80,256]{1,0:T(8,128)(2,1)S(1)}, u32[]{:S(2)}, u32[]{:S(2)}) collective-permute-start(bf16[80,256]{1,0:T(8,128)(2,1)S(1)} %add_convert_fusion.1.refs_8_), channel_id=1, source_target_pairs={{0,10},{1,11},{2,8},{3,9},{4,14},{5,15},{6,12},{7,13},{8,2},{9,3},... | collective-permute-start | bytes 122888 | tf_op jit(solution)/shard_map/ppermute | solution.py:31
  68.0 10.0 %collective-permute-start.12 = (bf16[80,512]{1,0:T(8,128)(2,1)S(1)}, bf16[80,512]{1,0:T(8,128)(2,1)S(1)}, u32[]{:S(2)}, u32[]{:S(2)}) collective-permute-start(bf16[80,512]{1,0:T(8,128)(2,1)S(1)} %pad_maximum_fusion.1.refs_18_), channel_id=1, source_target_pairs={{4,8},{5,9},{6,10},{7,11},{8,4},{9,5},{10,6},{11,7},{20,24},{21,25... | collective-permute-start | bytes 245768 | tf_op jit(solution)/shard_map/ppermute | solution.py:37
  68.7 9.3 %collective-permute-start.11 = (bf16[80,512]{1,0:T(8,128)(2,1)S(1)}, bf16[80,512]{1,0:T(8,128)(2,1)S(1)}, u32[]{:S(2)}, u32[]{:S(2)}) collective-permute-start(bf16[80,512]{1,0:T(8,128)(2,1)S(1)} %pad_maximum_fusion.1.refs_18_), channel_id=1, source_target_pairs={{0,4},{1,5},{2,6},{3,7},{4,0},{5,1},{6,2},{7,3},{8,12},{9,13},{10,... | collective-permute-start | bytes 245768 | tf_op jit(solution)/shard_map/ppermute | solution.py:31
